TPU v7x, 128 devices: a whole 4x4x4 slice. The times are simulated.
128 devices in a mesh: seq: 16 (over z, x), user: 8 (over y, core).
Axes of the slice: x: 4, y: 4, z: 4, core: 2. Of those that a mesh axis runs over, the one named last changes fastest.
Arguments:
- query: bfloat16 [8, 8192, 512], P('user', 'seq'), may hold values from -6 to 6
- key: bfloat16 [8, 8192, 512], P('user', 'seq'), may hold values from -6 to 6
- value: bfloat16 [8, 8192, 512], P('user', 'seq'), may hold values from -6 to 6
- gate: bfloat16 [8, 8192, 512], P('user', 'seq'), may hold values from -6 to 6
- history: bfloat16 [8, 8192, 128], P('user', 'seq'), may hold values from -6 to 6
- w_out: bfloat16 [512, 128], replicated, may hold values from -0.25 to 0.25
- table: bfloat16 [524288, 128], P(('seq', 'user')), may hold values from -0.5 to 0.5
- item_owner: int32 [8, 8192, 5], P('user', 'seq'), may hold values from 0 to 127, all different within a row; in each aligned block of 512 rows (0 to 511, 512 to 1023, ..., all dimensions but the last counted through in order) at most 30 rows name the same one
- item_row: int32 [8, 8192, 5], P('user', 'seq'), may hold values from 0 to 4095
- global_blocks: int32 [8, 2], P('user'), may hold values from 0 to 63, as said below
- lengths: int32 [8], replicated, may hold values from 2048 to 8192, as said below
Outputs:
- d_query: bfloat16 [8, 8192, 512], P('user', 'seq')
- d_key: bfloat16 [8, 8192, 512], P('user', 'seq')
- d_value: bfloat16 [8, 8192, 512], P('user', 'seq')
- d_gate: bfloat16 [8, 8192, 512], P('user', 'seq')
- table_grad: float32 [524288, 128], P(('seq', 'user'))
Inputs may be any that keep to these rules, and one draw needn't show every extreme that they name: `item_owner`: in the events of one device (512 aligned events of one user), no owner is named by more than 30 entries, a bound that some block reaches; the 5 owners of one event differ. `global_blocks`: the 2 block numbers of one user differ; the first lies among the blocks of the first 512 events. `lengths`: some user's length is 8192.
All inputs are finite; a program needn't handle non-finite values.
Results may differ from a plain program's by a relative error of at most 0.023.
Values may be sent and summed in bfloat16 or wider, within the bound.
No kernel may reach another device: no remote copies, remote signals or barrier semaphores. Data moves between devices by JAX's collectives and lax.ppermute only.
A program may use at most 128 MiB of HBM per device.

v0:
```python
import functools

import jax
import jax.numpy as jnp
from jax import lax
from jax.experimental import pallas as pl
from jax.experimental.pallas import tpu as pltpu
from jax.sharding import PartitionSpec as P

HEADS = 8
HEAD_DIM = 64
D = 512
E = 128
BLK = 128
GLOB = 2
ITEMS = 5
EVENTS = 512
NBD = EVENTS // BLK
PAIRS = HEADS // 2
NDEV = 128
NSEQ = 16
ROWS = 4096
SLOTS = 32
HI = 4
LO = ROWS // HI
BF = jnp.bfloat16
F32 = jnp.float32
VMEM_LIMIT = 56 * 1024 * 1024
SMEM_SPEC = pl.BlockSpec(memory_space=pltpu.SMEM)


def dot(a, b):
    return jnp.dot(a, b, preferred_element_type=F32)


def dot_nt(a, b):
    return lax.dot_general(a, b, (((1,), (1,)), ((), ())), preferred_element_type=F32)


def dot_tn(a, b):
    return lax.dot_general(a, b, (((0,), (0,)), ((), ())), preferred_element_type=F32)


def params(**more):
    return pltpu.CompilerParams(vmem_limit_bytes=VMEM_LIMIT, **more)


def whole(shape):
    return pl.BlockSpec(shape, lambda *_: (0,) * len(shape))


def iota(shape, dim):
    return lax.broadcasted_iota(jnp.int32, shape, dim)


def route_kernel(meta, owner, row, key, value, req, rank_out, pos_out, halo, cand):
    halo[0] = key[EVENTS - BLK :, :]
    halo[1] = value[EVENTS - BLK :, :]
    for g in range(GLOB):
        start = pl.multiple_of((meta[2 + g] % NBD) * BLK, BLK)
        cand[0, g * BLK : (g + 1) * BLK, :] = key[pl.ds(start, BLK), :]
        cand[1, g * BLK : (g + 1) * BLK, :] = value[pl.ds(start, BLK), :]
    dev = iota((NDEV, EVENTS), 0)
    rows = jnp.full((NDEV, EVENTS), -1, jnp.int32)
    for j in range(ITEMS):
        rows = jnp.where(owner[j] == dev, row[j], rows)
    hit = rows >= 0
    before = jnp.where(iota((EVENTS, EVENTS), 0) < iota((EVENTS, EVENTS), 1), 1.0, 0.0).astype(BF)
    rank = dot(jnp.where(hit, 1.0, 0.0).astype(BF), before)
    rank = jnp.where(hit, rank, -1.0)
    rank_out[...] = rank
    pos_out[...] = jnp.where(owner[0] == dev, 1.0, 0.0)
    plus = (rows + 1).astype(F32)
    lane = iota((NDEV, SLOTS), 1)
    asked = jnp.zeros((NDEV, SLOTS), F32)
    for k in range(SLOTS):
        column = jnp.sum(jnp.where(rank == k, plus, 0.0), axis=1, keepdims=True)
        asked = jnp.where(lane == k, column, asked)
    req[...] = asked.astype(jnp.int32) - 1


def route(meta, owner, row, key, value):
    return pl.pallas_call(
        route_kernel,
        out_shape=(
            jax.ShapeDtypeStruct((NDEV, SLOTS), jnp.int32),
            jax.ShapeDtypeStruct((NDEV, EVENTS), F32),
            jax.ShapeDtypeStruct((NDEV, EVENTS), F32),
            jax.ShapeDtypeStruct((2, BLK, D), BF),
            jax.ShapeDtypeStruct((2, GLOB * BLK, D), BF),
        ),
        in_specs=[SMEM_SPEC] + [pl.BlockSpec(memory_space=pltpu.VMEM)] * 4,
        out_specs=[pl.BlockSpec(memory_space=pltpu.VMEM)] * 5,
        compiler_params=params(),
        cost_estimate=pl.CostEstimate(flops=10**8, bytes_accessed=3 * 10**6, transcendentals=0),
        name="route",
    )(meta, owner, row, key, value)


def gather_kernel(asked, table, found):
    lo = asked[...] & (LO - 1)
    hi = asked[...] >> (LO.bit_length() - 1)
    wide = jnp.concatenate([table[h * LO : (h + 1) * LO, :] for h in range(HI)], axis=1)
    group = 16
    size = group * SLOTS
    lane = iota((size, E), 1)

    def spread(x, first):
        return jnp.concatenate(
            [jnp.broadcast_to(x[:, s : s + 1], (SLOTS, E)) for s in range(first, first + group)],
            axis=0,
        )

    for first in range(0, NDEV, group):
        low = spread(lo, first)
        high = spread(hi, first)
        onehot = jnp.concatenate(
            [jnp.where(low == lane + b * E, 1.0, 0.0).astype(BF) for b in range(LO // E)], axis=1
        )
        picked = dot(onehot, wide)
        out = jnp.zeros((size, E), F32)
        for h in range(HI):
            out = jnp.where(high == h, picked[:, h * E : (h + 1) * E], out)
        found[first * SLOTS : first * SLOTS + size, :] = out.astype(BF)


def gather(asked, table):
    return pl.pallas_call(
        gather_kernel,
        out_shape=jax.ShapeDtypeStruct((NDEV * SLOTS, E), BF),
        in_specs=[pl.BlockSpec(memory_space=pltpu.VMEM)] * 2,
        out_specs=pl.BlockSpec(memory_space=pltpu.VMEM),
        compiler_params=params(),
        cost_estimate=pl.CostEstimate(
            flops=2 * NDEV * SLOTS * ROWS * E, bytes_accessed=2 * 10**6, transcendentals=0
        ),
        name="gather_rows",
    )(asked, table)


def scatter_kernel(asked, slots, incoming, grad, spread):
    step = pl.program_id(0)
    shift = LO.bit_length() - 1

    @pl.when(step == 0)
    def _():
        hi = asked[...] >> shift
        group = 8
        size = group * SLOTS
        for first in range(0, NDEV, group):
            high = jnp.concatenate(
                [jnp.broadcast_to(hi[:, s : s + 1], (SLOTS, E)) for s in range(first, first + group)],
                axis=0,
            )
            part = incoming[first * SLOTS : first * SLOTS + size, :].astype(F32)
            for h in range(HI):
                spread[first * SLOTS : first * SLOTS + size, h * E : (h + 1) * E] = jnp.where(
                    high == h, part, 0.0
                ).astype(BF)

    size = LO // 4
    sub = iota((size, E), 0) + step * size
    lo = slots[...] & (LO - 1)
    onehot = jnp.concatenate(
        [
            jnp.where(sub == lo[i : i + 1, :], 1.0, 0.0).astype(BF)
            for i in range(NDEV * SLOTS // E)
        ],
        axis=1,
    )
    total = dot(onehot, spread[...])
    for h in range(HI):
        grad[h] = total[:, h * E : (h + 1) * E]


def scatter(asked, slots, incoming):
    count = NDEV * SLOTS
    return pl.pallas_call(
        scatter_kernel,
        grid=(4,),
        out_shape=jax.ShapeDtypeStruct((HI, LO, E), F32),
        in_specs=[whole((SLOTS, NDEV)), whole((count // E, E)), whole((count, E))],
        out_specs=pl.BlockSpec((HI, LO // 4, E), lambda i: (0, i, 0)),
        scratch_shapes=[pltpu.VMEM((count, HI * E), BF)],
        compiler_params=params(),
        cost_estimate=pl.CostEstimate(
            flops=2 * count * ROWS * E, bytes_accessed=3 * 10**6, transcendentals=0
        ),
        name="scatter_rows",
    )(asked, slots, incoming)


def head_masks():
    lane = iota((1, 2 * HEAD_DIM), 1)
    return [
        jnp.where(lane < HEAD_DIM, 1.0, 0.0).astype(BF),
        jnp.where(lane >= HEAD_DIM, 1.0, 0.0).astype(BF),
    ]


def forward_kernel(
    meta, q, k, v, halo, glob, gate, history, w_out, probs, slope, normed_out, inv_out, user, attn
):
    pair = pl.program_id(0)
    base, length = meta[0], meta[1]
    masks = head_masks()
    q16 = q[...] * jnp.asarray(1.0 / 16.0, BF)
    kx = jnp.concatenate([halo[0], k[...]], axis=0)
    vx = jnp.concatenate([halo[1], v[...]], axis=0)
    kg, vg = glob[0], glob[1]
    lane = iota((BLK, 2 * BLK), 1)
    sub = iota((BLK, 2 * BLK), 0)
    gid = jnp.where(lane < BLK, meta[2], meta[3])
    glob_pos = gid * BLK + lane % BLK
    near, far = [], []
    for i in range(NBD):
        pos = (base + i - 1) * BLK + lane
        near.append((pos >= 0) & (pos < length) & (lane <= sub + BLK))
        far.append((gid < base + i - 1) & (glob_pos < length))
    vx_m = [vx * m for m in masks]
    vg_both = jnp.concatenate([vg * m for m in masks], axis=0)

    def act(u, mask):
        w = jnp.where(mask, 1.0 + jnp.tanh(u), 0.0)
        p = u * w
        return p.astype(BF), (w + p * (2.0 - w)).astype(BF)

    for i in range(NBD):
        rows = slice(i * BLK, (i + 1) * BLK)
        keys = slice(i * BLK, (i + 2) * BLK)
        near_p, far_p = [], []
        for h in range(2):
            qm = q16[rows] * masks[h]
            p, f = act(dot_nt(qm, kx[keys]), near[i])
            probs[h, rows, : 2 * BLK] = p
            slope[h, rows, : 2 * BLK] = f
            near_p.append(p)
            p, f = act(dot_nt(qm, kg), far[i])
            probs[h, rows, 2 * BLK :] = p
            slope[h, rows, 2 * BLK :] = f
            far_p.append(p)
        near_v = jnp.concatenate([m[keys] for m in vx_m], axis=0)
        attn[pair, rows, :] = dot(jnp.concatenate(near_p, axis=1), near_v) + dot(
            jnp.concatenate(far_p, axis=1), vg_both
        )

    @pl.when(pair == PAIRS - 1)
    def _():
        step = 128
        for r in range(0, EVENTS, step):
            rows = slice(r, r + step)
            x = jnp.concatenate([attn[p, rows, :] for p in range(PAIRS)], axis=1)
            centered = x - jnp.mean(x, axis=1, keepdims=True)
            var = jnp.mean(centered * centered, axis=1, keepdims=True)
            inv = lax.rsqrt(var + 1e-05)
            normed = centered * inv
            normed_out[rows, :] = normed
            inv_out[rows, :] = inv
            gated = (normed * gate[rows, :].astype(F32)).astype(BF)
            user[rows, :] = dot(gated, w_out[...]) + history[rows, :].astype(F32)


def pair_block(rows):
    return pl.BlockSpec((rows, 2 * HEAD_DIM), lambda p: (0, p))


def pair_stack(rows):
    return pl.BlockSpec((2, rows, 2 * HEAD_DIM), lambda p: (0, 0, p))


def head_block():
    return pl.BlockSpec((2, EVENTS, (2 + GLOB) * BLK), lambda p: (p, 0, 0))


def forward(meta, q, k, v, halo, glob, gate, history, w_out):
    square = (HEADS, EVENTS, (2 + GLOB) * BLK)
    return pl.pallas_call(
        forward_kernel,
        grid=(PAIRS,),
        out_shape=(
            jax.ShapeDtypeStruct(square, BF),
            jax.ShapeDtypeStruct(square, BF),
            jax.ShapeDtypeStruct((EVENTS, D), F32),
            jax.ShapeDtypeStruct((EVENTS, 1), F32),
            jax.ShapeDtypeStruct((EVENTS, E), F32),
        ),
        in_specs=[SMEM_SPEC]
        + [pair_block(EVENTS)] * 3
        + [pair_stack(BLK), pair_stack(GLOB * BLK)]
        + [whole((EVENTS, D)), whole((EVENTS, E)), whole((D, E))],
        out_specs=[
            head_block(),
            head_block(),
            whole((EVENTS, D)),
            whole((EVENTS, 1)),
            whole((EVENTS, E)),
        ],
        scratch_shapes=[pltpu.VMEM((PAIRS, EVENTS, 2 * HEAD_DIM), F32)],
        compiler_params=params(),
        cost_estimate=pl.CostEstimate(
            flops=10**9, bytes_accessed=13 * 10**6, transcendentals=2 * 10**6
        ),
        name="attend_forward",
    )(meta, q, k, v, halo, glob, gate, history, w_out)


def backward_kernel(q, k, v, halo, glob, grad, probs, slope, d_q, d_k, d_v, edge, d_glob):
    masks = head_masks()
    sixteenth = jnp.asarray(1.0 / 16.0, BF)
    q16 = q[...] * sixteenth
    kx = jnp.concatenate([halo[0], k[...]], axis=0)
    vx = jnp.concatenate([halo[1], v[...]], axis=0)
    kg, vg = glob[0], glob[1]
    do = grad[...]
    q_t = [(q16 * m).T for m in masks]
    do_t = [(do * m).T for m in masks]
    kx_m = [kx * (m * sixteenth) for m in masks]
    kg_both = jnp.concatenate([kg * (m * sixteenth) for m in masks], axis=0)
    far_ds = [[], []]
    carry = None
    for i in range(NBD):
        rows = slice(i * BLK, (i + 1) * BLK)
        keys = slice(i * BLK, (i + 2) * BLK)
        near_ds, far_i = [], []
        for h in range(2):
            dom = do[rows] * masks[h]
            ds = dot_nt(dom, vx[keys]) * slope[h, rows, : 2 * BLK].astype(F32)
            near_ds.append(ds.astype(BF))
            ds = dot_nt(dom, vg) * slope[h, rows, 2 * BLK :].astype(F32)
            far_i.append(ds.astype(BF))
            far_ds[h].append(far_i[-1])
        near_k = jnp.concatenate([m[keys] for m in kx_m], axis=0)
        d_q[rows, :] = (
            dot(jnp.concatenate(near_ds, axis=1), near_k)
            + dot(jnp.concatenate(far_i, axis=1), kg_both)
        ).astype(BF)
        near_p = jnp.concatenate([probs[h, rows, : 2 * BLK] for h in range(2)], axis=0)
        dk = dot(
            jnp.concatenate([t[:, rows] for t in q_t], axis=1), jnp.concatenate(near_ds, axis=0)
        ).T
        dv = dot(jnp.concatenate([t[:, rows] for t in do_t], axis=1), near_p).T
        if i == 0:
            edge[0] = dk[:BLK].astype(BF)
            edge[1] = dv[:BLK].astype(BF)
        else:
            last = slice((i - 1) * BLK, i * BLK)
            d_k[last, :] = (carry[0] + dk[:BLK]).astype(BF)
            d_v[last, :] = (carry[1] + dv[:BLK]).astype(BF)
        carry = (dk[BLK:], dv[BLK:])
    last = slice((NBD - 1) * BLK, NBD * BLK)
    d_k[last, :] = carry[0].astype(BF)
    d_v[last, :] = carry[1].astype(BF)
    far_ds = jnp.concatenate(far_ds[0] + far_ds[1], axis=0)
    far_p = jnp.concatenate([probs[h, :, 2 * BLK :] for h in range(2)], axis=0)
    d_glob[0] = dot(jnp.concatenate(q_t, axis=1), far_ds).T.astype(BF)
    d_glob[1] = dot(jnp.concatenate(do_t, axis=1), far_p).T.astype(BF)


def backward(q, k, v, halo, glob, grad, probs, slope):
    rows = jax.ShapeDtypeStruct((EVENTS, D), BF)
    return pl.pallas_call(
        backward_kernel,
        grid=(PAIRS,),
        out_shape=(
            rows,
            rows,
            rows,
            jax.ShapeDtypeStruct((2, BLK, D), BF),
            jax.ShapeDtypeStruct((2, GLOB * BLK, D), BF),
        ),
        in_specs=[pair_block(EVENTS)] * 3
        + [pair_stack(BLK), pair_stack(GLOB * BLK), pair_block(EVENTS)]
        + [head_block()] * 2,
        out_specs=[pair_block(EVENTS)] * 3 + [pair_stack(BLK), pair_stack(GLOB * BLK)],
        compiler_params=params(),
        cost_estimate=pl.CostEstimate(
            flops=2 * 10**9, bytes_accessed=13 * 10**6, transcendentals=0
        ),
        name="attend_backward",
    )(q, k, v, halo, glob, grad, probs, slope)


def middle_kernel(
    meta, items, rank, pos, user, normed, inv, gate, w_out, outgoing, d_attn, d_gate, score
):
    user_b = user[...].astype(BF)
    user_t = user[...].T.astype(BF)
    group = 8
    size = group * SLOTS
    slot = iota((SLOTS, EVENTS), 0).astype(F32)
    for d in range(0, NDEV, group):
        s = dot(items[d * SLOTS : d * SLOTS + size, :], user_t)
        for r in range(group):
            own = rank[d + r : d + r + 1, :] == slot
            part = jnp.where(own, s[r * SLOTS : (r + 1) * SLOTS, :], 0.0)
            score[d + r : d + r + 1, :] = jnp.sum(part, axis=0, keepdims=True)
    first = pos[...]
    score0 = jnp.sum(first * score[...], axis=0, keepdims=True)
    event = meta[0] * BLK + iota((1, EVENTS), 1)
    valid = jnp.where(event < meta[1], 1.0, 0.0)
    other = (rank[...] >= 0.0) & (first == 0.0)
    side = jnp.where(other, jax.nn.sigmoid(score[...] - score0), 0.0) * valid
    coef = side - first * jnp.sum(side, axis=0, keepdims=True)
    score[...] = coef
    d_user_t = jnp.zeros((E, EVENTS), F32)
    for d in range(0, NDEV, group):
        c = jnp.concatenate(
            [
                jnp.where(rank[r : r + 1, :] == slot, score[r : r + 1, :], 0.0).astype(BF)
                for r in range(d, d + group)
            ],
            axis=0,
        )
        rows = slice(d * SLOTS, d * SLOTS + size)
        outgoing[rows, :] = dot(c, user_b).astype(BF)
        d_user_t = d_user_t + dot_tn(items[rows, :], c)
    d_user = d_user_t.T.astype(BF)
    step = 128
    for r in range(0, EVENTS, step):
        rows = slice(r, r + step)
        d_gated = dot_nt(d_user[rows], w_out[...])
        n = normed[rows, :]
        d_gate[rows, :] = (d_gated * n).astype(BF)
        dn = d_gated * gate[rows, :].astype(F32)
        d_attn[rows, :] = (
            (
                dn
                - jnp.mean(dn, axis=1, keepdims=True)
                - n * jnp.mean(dn * n, axis=1, keepdims=True)
            )
            * inv[rows, :]
        ).astype(BF)


def middle(meta, items, rank, pos, user, normed, inv, gate, w_out):
    return pl.pallas_call(
        middle_kernel,
        out_shape=(
            jax.ShapeDtypeStruct((NDEV * SLOTS, E), BF),
            jax.ShapeDtypeStruct((EVENTS, D), BF),
            jax.ShapeDtypeStruct((EVENTS, D), BF),
        ),
        in_specs=[SMEM_SPEC] + [pl.BlockSpec(memory_space=pltpu.VMEM)] * 8,
        out_specs=[pl.BlockSpec(memory_space=pltpu.VMEM)] * 3,
        scratch_shapes=[pltpu.VMEM((NDEV, EVENTS), F32)],
        compiler_params=params(),
        cost_estimate=pl.CostEstimate(
            flops=2 * 10**9, bytes_accessed=6 * 10**6, transcendentals=10**5
        ),
        name="ranking",
    )(meta, items, rank, pos, user, normed, inv, gate, w_out)


def finish_kernel(meta, d_k, d_v, edge, total, key_out, value_out):
    for which, (mine, out) in enumerate(((d_k, key_out), (d_v, value_out))):
        out[...] = mine[...]
        tail = slice(EVENTS - BLK, EVENTS)
        out[tail, :] = (mine[tail, :].astype(F32) + edge[which].astype(F32)).astype(BF)
        for g in range(GLOB):

            @pl.when(meta[2 + g] // NBD == meta[4])
            def _():
                place = pl.ds(pl.multiple_of((meta[2 + g] % NBD) * BLK, BLK), BLK)
                more = total[which, g * BLK : (g + 1) * BLK, :].astype(F32)
                out[place, :] = (out[place, :].astype(F32) + more).astype(BF)


def finish(meta, d_k, d_v, edge, total):
    rows = jax.ShapeDtypeStruct((EVENTS, D), BF)
    return pl.pallas_call(
        finish_kernel,
        out_shape=(rows, rows),
        in_specs=[SMEM_SPEC] + [pl.BlockSpec(memory_space=pltpu.VMEM)] * 4,
        out_specs=[pl.BlockSpec(memory_space=pltpu.VMEM)] * 2,
        compiler_params=params(),
        cost_estimate=pl.CostEstimate(flops=10**6, bytes_accessed=3 * 10**6, transcendentals=0),
        name="add_received",
    )(meta, d_k, d_v, edge, total)


def from_behind(block, axis, distance):
    devices = range(lax.axis_size(axis))
    route_pairs = [(i - distance, i) for i in devices if i - distance in devices]
    return lax.ppermute(block, axis, route_pairs)


def exchange(x, axis):
    return lax.all_to_all(x, axis, split_axis=0, concat_axis=0, tiled=True)


def on_device(
    query, key, value, gate, history, w_out, table, item_owner, item_row, global_blocks, lengths
):
    seq = lax.axis_index("seq")
    user_idx = lax.axis_index("user")
    length = lax.dynamic_slice_in_dim(lengths, user_idx, 1)
    gids = global_blocks[0]
    meta = jnp.concatenate([(seq * NBD).reshape(1), length, gids, seq.reshape(1)]).astype(jnp.int32)
    q, k, v = query[0], key[0], value[0]
    owner = item_owner[0].T.reshape(ITEMS, 1, EVENTS)
    row = item_row[0].T.reshape(ITEMS, 1, EVENTS)
    req, rank, pos, tail, cand = route(meta, owner, row, k, v)
    asked = exchange(req.reshape(NDEV, 1, SLOTS), ("seq", "user")).reshape(NDEV, SLOTS)
    halo = from_behind(tail, "seq", 1)
    pieces = exchange(cand.reshape(NSEQ, 2 * GLOB * BLK // NSEQ, D), "seq")
    holder = gids[(seq % (NSEQ // 2)) // (NSEQ // 4)] // NBD
    piece = lax.dynamic_index_in_dim(pieces, holder, 0, keepdims=True)
    glob = exchange(jnp.broadcast_to(piece, pieces.shape), "seq").reshape(2, GLOB * BLK, D)
    asked_t = asked.T
    found = gather(asked_t, table)
    items = exchange(found.reshape(NDEV, SLOTS, E), ("seq", "user")).reshape(NDEV * SLOTS, E)
    probs, slope, normed, inv, user = forward(meta, q, k, v, halo, glob, gate[0], history[0], w_out)
    outgoing, d_attn, d_gate = middle(meta, items, rank, pos, user, normed, inv, gate[0], w_out)
    incoming = exchange(outgoing.reshape(NDEV, SLOTS, E), ("seq", "user"))
    d_q, d_k, d_v, edge, d_glob = backward(q, k, v, halo, glob, d_attn, probs, slope)
    parts = exchange(d_glob.reshape(NSEQ, 2 * GLOB * BLK // NSEQ, D), "seq")
    part = jnp.sum(parts.astype(F32), axis=0, keepdims=True).astype(BF)
    total = exchange(jnp.broadcast_to(part, parts.shape), "seq").reshape(2, GLOB * BLK, D)
    back = from_behind(edge, "seq", -1)
    grad = scatter(asked_t, asked.reshape(NDEV * SLOTS // E, E), incoming.reshape(NDEV * SLOTS, E))
    d_key, d_value = finish(meta, d_k, d_v, back, total)
    return (d_q[None], d_key[None], d_value[None], d_gate[None], grad.reshape(ROWS, E))


def solution(mesh):
    return jax.shard_map(
        on_device,
        mesh=mesh,
        in_specs=(
            P("user", "seq", None),
            P("user", "seq", None),
            P("user", "seq", None),
            P("user", "seq", None),
            P("user", "seq", None),
            P(),
            P(("seq", "user"), None),
            P("user", "seq", None),
            P("user", "seq", None),
            P("user", None),
            P(),
        ),
        out_specs=(
            P("user", "seq", None),
            P("user", "seq", None),
            P("user", "seq", None),
            P("user", "seq", None),
            P(("seq", "user"), None),
        ),
        check_vma=False,
    )
```

profile of v0, /device:TPU:32, one launch (start us, length us, event | category | flops | bytes accessed | tf_op | source)
XLA Modules:
  0.0 179.8 jit_solution(233914273086696311)
XLA Ops:
  0.6 0.7 copy.27
  1.3 0.6 reshape.63.owner
  1.9 0.7 copy.26
  2.7 0.6 reshape.64.row
  3.3 1.2 dynamic_slice.10
  4.5 1.9 %pad_add_fusion.meta = s32[5]{0:T(128)} fusion(s32[1]{0:T(128)} %bitcast.5, s32[2]{0:T(128)} %bitcast.61, s32[1]{0:T(128)} %dynamic_slice.10, s32[1]{0:T(128)} %bitcast.3), kind=kLoop, calls=%fused_computation.3 | loop fusion | flops 15 | bytes 40 | tf_op jit(solution)/shard_map/concatenate | solution.py:498
  6.4 3.3 %route.1 = (s32[128,32]{1,0:T(8,128)}, f32[128,512]{1,0:T(8,128)}, f32[128,512]{1,0:T(8,128)}, bf16[2,128,512]{2,1,0:T(8,128)(2,1)}, bf16[2,256,512]{2,1,0:T(8,128)(2,1)}) custom-call(s32[5]{0:T(128)} %pad_add_fusion.meta, s32[5,1,512]{2,1,0:T(1,128)} %reshape.63.owner, s32[5,1,512]{2,1,0:T(1,128)} %reshape.64.row, bf16[512,512]{1,0:T(8,128)(2,1)} %bitcast.42, ...), custom_call_target="tpu_custom_call" | custom-call | flops 100000000 | bytes 3000000 | tf_op jit(solution)/shard_map/route/pallas_call | solution.py:83
  9.7 7.9 %all-to-all-start = ((bf16[16,32,512]{2,1,0:T(8,128)(2,1)}), bf16[16,32,512]{2,1,0:T(8,128)(2,1)S(1)}, u32[]{:S(2)}, u32[]{:S(2)}) async-start(bf16[16,32,512]{2,1,0:T(8,128)(2,1)} %bitcast.54), calls=%async_computation | async-start | bytes 1048576 | tf_op jit(solution)/shard_map/all_to_all | solution.py:488
  17.6 1.2 constant_dynamic-slice_fusion
  21.4 5.1 %all-to-all-done = bf16[16,32,512]{2,1,0:T(8,128)(2,1)S(1)} async-done(((bf16[16,32,512]{2,1,0:T(8,128)(2,1)}), bf16[16,32,512]{2,1,0:T(8,128)(2,1)S(1)}, u32[]{:S(2)}, u32[]{:S(2)}) %all-to-all-start) | async-done | bytes 524320 | tf_op jit(solution)/shard_map/all_to_all | solution.py:488
  26.6 8.1 %all-to-all-start.2 = ((s32[128,1,32]{2,1,0:T(1,128)}), s32[128,1,32]{2,1,0:T(1,128)S(1)}, u32[]{:S(2)}, u32[]{:S(2)}) async-start(s32[128,1,32]{2,1,0:T(1,128)} %bitcast.56), calls=%async_computation.2 | async-start | bytes 131072 | tf_op jit(solution)/shard_map/all_to_all | solution.py:488
  34.6 9.0 %all-to-all-done.2 = s32[128,1,32]{2,1,0:T(1,128)S(1)} async-done(((s32[128,1,32]{2,1,0:T(1,128)}), s32[128,1,32]{2,1,0:T(1,128)S(1)}, u32[]{:S(2)}, u32[]{:S(2)}) %all-to-all-start.2) | async-done | bytes 16416 | tf_op jit(solution)/shard_map/all_to_all | solution.py:488
  43.6 0.8 broadcast_in_dim.26
  44.5 4.6 %all-to-all-start.1 = ((bf16[16,32,512]{2,1,0:T(8,128)(2,1)}), bf16[16,32,512]{2,1,0:T(8,128)(2,1)S(1)}, u32[]{:S(2)}, u32[]{:S(2)}) async-start(bf16[16,32,512]{2,1,0:T(8,128)(2,1)} %broadcast_in_dim.26), calls=%async_computation.1 | async-start | bytes 1048576 | tf_op jit(solution)/shard_map/all_to_all | solution.py:488
  49.0 0.7 copy.21
  49.7 0.0 copy-start.5
  49.7 6.8 %gather_rows.1 = bf16[4096,128]{1,0:T(8,128)(2,1)} custom-call(s32[32,128]{1,0:T(8,128)} %bitcast.59, bf16[4096,128]{1,0:T(8,128)(2,1)} %table.1), custom_call_target="tpu_custom_call" | custom-call | flops 4294967296 | bytes 2000000 | tf_op jit(solution)/shard_map/gather_rows/pallas_call | solution.py:128
  56.5 1.7 all-to-all-done.1
  58.2 0.0 copy-start
  58.2 6.4 %all-to-all-start.3 = ((bf16[128,32,128]{2,1,0:T(8,128)(2,1)}), bf16[128,32,128]{2,1,0:T(8,128)(2,1)S(1)}, u32[]{:S(2)}, u32[]{:S(2)}) async-start(bf16[128,32,128]{2,1,0:T(8,128)(2,1)} %bitcast.51), calls=%async_computation.3 | async-start | bytes 2097152 | tf_op jit(solution)/shard_map/all_to_all | solution.py:488
  64.6 0.0 copy-done.5
  64.6 3.6 %collective-permute-start = (bf16[2,128,512]{2,1,0:T(8,128)(2,1)S(1)}, bf16[2,128,512]{2,1,0:T(8,128)(2,1)S(1)}, u32[]{:S(2)}, u32[]{:S(2)}) collective-permute-start(bf16[2,128,512]{2,1,0:T(8,128)(2,1)S(1)} %copy-done.5), channel_id=1, source_target_pairs={{0,8},{8,16},{16,24},{24,32},{32,40},{40,48},{48,56},{56,64},{64,7... | collective-permute-start | bytes 786440 | tf_op jit(solution)/shard_map/ppermute | solution.py:484
  68.2 16.8 %collective-permute-done.halo = bf16[2,128,512]{2,1,0:T(8,128)(2,1)S(1)} collective-permute-done((bf16[2,128,512]{2,1,0:T(8,128)(2,1)S(1)}, bf16[2,128,512]{2,1,0:T(8,128)(2,1)S(1)}, u32[]{:S(2)}, u32[]{:S(2)}) %collective-permute-start) | collective-permute-done | bytes 262176 | tf_op jit(solution)/shard_map/ppermute | solution.py:484
  85.0 0.0 copy-start.3
  85.0 0.0 copy-done
  85.0 0.7 copy-done.3
  85.7 9.9 %attend_forward.1 = (bf16[8,512,512]{2,1,0:T(8,128)(2,1)}, bf16[8,512,512]{2,1,0:T(8,128)(2,1)}, f32[512,512]{1,0:T(8,128)}, f32[512,1]{1,0:T(8,128)}, f32[512,128]{1,0:T(8,128)}) custom-call(s32[5]{0:T(128)} %pad_add_fusion.meta, bf16[512,512]{1,0:T(8,128)(2,1)} %bitcast.52, bf16[512,512]{1,0:T(8,128)(2,1)} %bitcast.43, bf16[512,512]{1,0:T(8,128)(2,1)} %bitcast.46, ...), custom_call_target="tpu_custom_call" | custom-call | flops 1000000000 | bytes 13000000 | tf_op jit(solution)/shard_map/attend_forward/pallas_call | solution.py:277
  95.7 0.0 all-to-all-done.3
  95.7 0.0 copy-start.2
  95.7 1.0 copy-done.2
  96.7 7.0 %ranking.1 = (bf16[4096,128]{1,0:T(8,128)(2,1)}, bf16[512,512]{1,0:T(8,128)(2,1)}, bf16[512,512]{1,0:T(8,128)(2,1)}) custom-call(s32[5]{0:T(128)} %pad_add_fusion.meta, bf16[4096,128]{1,0:T(8,128)(2,1)} %bitcast.50, f32[128,512]{1,0:T(8,128)} %get-tuple-element.28.rank, f32[128,512]{1,0:T(8,128)} %get-tuple-element.29.pos, ...), custom_call_target="tpu_custom_call" | custom-call | flops 2000000000 | bytes 6000000 | tf_op jit(solution)/shard_map/ranking/pallas_call | solution.py:436
  103.7 9.1 %attend_backward.1 = (bf16[512,512]{1,0:T(8,128)(2,1)}, bf16[512,512]{1,0:T(8,128)(2,1)}, bf16[512,512]{1,0:T(8,128)(2,1)}, bf16[2,128,512]{2,1,0:T(8,128)(2,1)}, bf16[2,256,512]{2,1,0:T(8,128)(2,1)}) custom-call(bf16[512,512]{1,0:T(8,128)(2,1)} %bitcast.53, bf16[512,512]{1,0:T(8,128)(2,1)} %bitcast.44, bf16[512,512]{1,0:T(8,128)(2,1)} %bitcast.47, ...), custom_call_target="tpu_custom_call" | custom-call | flops 2000000000 | bytes 13000000 | tf_op jit(solution)/shard_map/attend_backward/pallas_call | solution.py:361
  112.8 0.0 copy-start.6
  112.8 14.4 %all_to_all.35 = bf16[16,32,512]{2,1,0:T(8,128)(2,1)S(1)} all-to-all(bf16[16,32,512]{2,1,0:T(8,128)(2,1)} %bitcast.55), channel_id=1, replica_groups=mesh['seq'=16,'user'=8] {'seq'}, dimensions={0} | all-to-all | bytes 1048576 | tf_op jit(solution)/shard_map/all_to_all | solution.py:488
  127.1 0.1 reduce_sum.12
  127.3 14.3 %all_to_all.36 = bf16[16,32,512]{2,1,0:T(8,128)(2,1)} all-to-all(bf16[16,32,512]{2,1,0:T(8,128)(2,1)S(1)} %broadcast_in_dim.28), channel_id=1, replica_groups=mesh['seq'=16,'user'=8] {'seq'}, dimensions={0} | all-to-all | bytes 1048576 | tf_op jit(solution)/shard_map/all_to_all | solution.py:488
  141.6 7.1 %all-to-all-start.6 = ((bf16[128,32,128]{2,1,0:T(8,128)(2,1)}), bf16[128,32,128]{2,1,0:T(8,128)(2,1)S(1)}, u32[]{:S(2)}, u32[]{:S(2)}) async-start(bf16[128,32,128]{2,1,0:T(8,128)(2,1)} %bitcast.27), calls=%async_computation.6 | async-start | bytes 2097152 | tf_op jit(solution)/shard_map/all_to_all | solution.py:488
  148.6 0.0 copy-done.6
  148.6 4.5 %collective-permute-start.1 = (bf16[2,128,512]{2,1,0:T(8,128)(2,1)S(1)}, bf16[2,128,512]{2,1,0:T(8,128)(2,1)S(1)}, u32[]{:S(2)}, u32[]{:S(2)}) collective-permute-start(bf16[2,128,512]{2,1,0:T(8,128)(2,1)S(1)} %copy-done.6), channel_id=1, source_target_pairs={{8,0},{16,8},{24,16},{32,24},{40,32},{48,40},{56,48},{64,56},{72,6... | collective-permute-start | bytes 786440 | tf_op jit(solution)/shard_map/ppermute | solution.py:484
  153.1 0.5 broadcast.6
  153.6 0.8 reduce.4
  154.4 0.7 reshape_reshape.3.slots
  155.1 12.2 %collective-permute-done.1.edge = bf16[2,128,512]{2,1,0:T(8,128)(2,1)S(1)} collective-permute-done((bf16[2,128,512]{2,1,0:T(8,128)(2,1)S(1)}, bf16[2,128,512]{2,1,0:T(8,128)(2,1)S(1)}, u32[]{:S(2)}, u32[]{:S(2)}) %collective-permute-start.1) | collective-permute-done | bytes 262176 | tf_op jit(solution)/shard_map/ppermute | solution.py:484
  167.3 0.0 copy-start.4
  167.3 0.7 copy-done.4
  168.0 2.6 %add_received.1 = (bf16[512,512]{1,0:T(8,128)(2,1)}, bf16[512,512]{1,0:T(8,128)(2,1)}) custom-call(s32[5]{0:T(128)} %pad_add_fusion.meta, bf16[512,512]{1,0:T(8,128)(2,1)} %get-tuple-element.37.d_k, bf16[512,512]{1,0:T(8,128)(2,1)} %get-tuple-element.38.d_v, bf16[2,128,512]{2,1,0:T(8,128)(2,1)} %copy-done.4, bf16[2,256,512]{2,1,0:T(8,128)(2,1)} %bitcast.48), custom_call_target="tpu_custom_call" | custom-call | flops 1000000 | bytes 3000000 | tf_op jit(solution)/shard_map/add_received/pallas_call | solution.py:470
  170.6 0.0 all-to-all-done.6
  170.6 0.0 copy-start.1
  170.6 1.0 copy-done.1
  171.6 8.2 %scatter_rows.1 = f32[4,1024,128]{2,1,0:T(8,128)} custom-call(s32[32,128]{1,0:T(8,128)} %bitcast.60, s32[32,128]{1,0:T(8,128)} %reshape_reshape.3.slots, bf16[4096,128]{1,0:T(8,128)(2,1)} %bitcast.49), custom_call_target="tpu_custom_call" | custom-call | flops 4294967296 | bytes 3000000 | tf_op jit(solution)/shard_map/scatter_rows/pallas_call | solution.py:178
  (2 shorter events, 0.1 us)
Async XLA Ops:
  9.7 16.9 %all-to-all-start = ((bf16[16,32,512]{2,1,0:T(8,128)(2,1)}), bf16[16,32,512]{2,1,0:T(8,128)(2,1)S(1)}, u32[]{:S(2)}, u32[]{:S(2)}) async-start(bf16[16,32,512]{2,1,0:T(8,128)(2,1)} %bitcast.54), calls=%async_computation | async-start | bytes 1048576 | tf_op jit(solution)/shard_map/all_to_all | solution.py:488
  26.6 17.1 %all-to-all-start.2 = ((s32[128,1,32]{2,1,0:T(1,128)}), s32[128,1,32]{2,1,0:T(1,128)S(1)}, u32[]{:S(2)}, u32[]{:S(2)}) async-start(s32[128,1,32]{2,1,0:T(1,128)} %bitcast.56), calls=%async_computation.2 | async-start | bytes 131072 | tf_op jit(solution)/shard_map/all_to_all | solution.py:488
  44.5 13.7 %all-to-all-start.1 = ((bf16[16,32,512]{2,1,0:T(8,128)(2,1)}), bf16[16,32,512]{2,1,0:T(8,128)(2,1)S(1)}, u32[]{:S(2)}, u32[]{:S(2)}) async-start(bf16[16,32,512]{2,1,0:T(8,128)(2,1)} %broadcast_in_dim.26), calls=%async_computation.1 | async-start | bytes 1048576 | tf_op jit(solution)/shard_map/all_to_all | solution.py:488
  49.7 14.9 %copy-start.5 = (bf16[2,128,512]{2,1,0:T(8,128)(2,1)S(1)}, bf16[2,128,512]{2,1,0:T(8,128)(2,1)}, u32[]{:S(2)}) copy-start(bf16[2,128,512]{2,1,0:T(8,128)(2,1)} %get-tuple-element.25) | copy-start | bytes 786436
  58.2 26.9 %copy-start = (bf16[16,32,512]{2,1,0:T(8,128)(2,1)}, bf16[16,32,512]{2,1,0:T(8,128)(2,1)S(1)}, u32[]{:S(2)}) copy-start(bf16[16,32,512]{2,1,0:T(8,128)(2,1)S(1)} %all-to-all-done.1) | copy-start | bytes 1572868
  58.2 37.5 %all-to-all-start.3 = ((bf16[128,32,128]{2,1,0:T(8,128)(2,1)}), bf16[128,32,128]{2,1,0:T(8,128)(2,1)S(1)}, u32[]{:S(2)}, u32[]{:S(2)}) async-start(bf16[128,32,128]{2,1,0:T(8,128)(2,1)} %bitcast.51), calls=%async_computation.3 | async-start | bytes 2097152 | tf_op jit(solution)/shard_map/all_to_all | solution.py:488
  64.6 20.4 %collective-permute-start = (bf16[2,128,512]{2,1,0:T(8,128)(2,1)S(1)}, bf16[2,128,512]{2,1,0:T(8,128)(2,1)S(1)}, u32[]{:S(2)}, u32[]{:S(2)}) collective-permute-start(bf16[2,128,512]{2,1,0:T(8,128)(2,1)S(1)} %copy-done.5), channel_id=1, source_target_pairs={{0,8},{8,16},{16,24},{24,32},{32,40},{40,48},{48,56},{56,64},{64,7... | collective-permute-start | bytes 786440 | tf_op jit(solution)/shard_map/ppermute | solution.py:484
  85.0 0.7 copy-start.3
  95.7 1.0 copy-start.2
  112.8 35.9 %copy-start.6 = (bf16[2,128,512]{2,1,0:T(8,128)(2,1)S(1)}, bf16[2,128,512]{2,1,0:T(8,128)(2,1)}, u32[]{:S(2)}) copy-start(bf16[2,128,512]{2,1,0:T(8,128)(2,1)} %get-tuple-element.39) | copy-start | bytes 786436
  141.6 29.1 %all-to-all-start.6 = ((bf16[128,32,128]{2,1,0:T(8,128)(2,1)}), bf16[128,32,128]{2,1,0:T(8,128)(2,1)S(1)}, u32[]{:S(2)}, u32[]{:S(2)}) async-start(bf16[128,32,128]{2,1,0:T(8,128)(2,1)} %bitcast.27), calls=%async_computation.6 | async-start | bytes 2097152 | tf_op jit(solution)/shard_map/all_to_all | solution.py:488
  148.6 18.7 %collective-permute-start.1 = (bf16[2,128,512]{2,1,0:T(8,128)(2,1)S(1)}, bf16[2,128,512]{2,1,0:T(8,128)(2,1)S(1)}, u32[]{:S(2)}, u32[]{:S(2)}) collective-permute-start(bf16[2,128,512]{2,1,0:T(8,128)(2,1)S(1)} %copy-done.6), channel_id=1, source_target_pairs={{8,0},{16,8},{24,16},{32,24},{40,32},{48,40},{56,48},{64,56},{72,6... | collective-permute-start | bytes 786440 | tf_op jit(solution)/shard_map/ppermute | solution.py:484
  167.3 0.7 copy-start.4
  170.6 1.0 copy-start.1
where the time goes:
time: 183 us; the launch traced here: 180 us
  Pallas kernels  47 us (26%)
  waiting for transfers between devices  44.8 us (24%)
  starting transfers between devices  42 us (23%)
  blocking collectives  28.6 us (16%)
  local copies, waits for them, and re-layouts  11.2 us (6%)
  between operations  3.37 us (2%)
  other arithmetic  2.79 us (2%)
    all_to_all x5, starting transfers between devices, exchange(): return lax.all_to_all(x, axis, split_axis=0, concat_axis=0, tiled=True)  34 us
    ppermute x2, waiting for transfers between devices, from_behind(): return lax.ppermute(block, axis, route_pairs)  29 us
    all_to_all x2, blocking collectives, exchange(): return lax.all_to_all(x, axis, split_axis=0, concat_axis=0, tiled=True)  28.6 us
    all_to_all x5, waiting for transfers between devices, exchange(): return lax.all_to_all(x, axis, split_axis=0, concat_axis=0, tiled=True)  15.8 us
    pallas_call x1, Pallas kernels, forward(): pl.pallas_call(forward_kernel, grid=(PAIRS,), out_shape=(jax.ShapeDtypeSt...  9.95 us
    pallas_call x1, Pallas kernels, backward(): pl.pallas_call(backward_kernel, grid=(PAIRS,), out_shape=(rows, rows, row...  9.08 us
    pallas_call x1, Pallas kernels, scatter(): pl.pallas_call(scatter_kernel, grid=(4,), out_shape=jax.ShapeDtypeStruct(...  8.17 us
    ppermute x2, starting transfers between devices, from_behind(): return lax.ppermute(block, axis, route_pairs)  8.03 us
  transfers between devices with their start and end apart: 7, of which 5 were waited for; matrix products, arithmetic and copies ran while one was open for 2% of the time, Pallas kernels for 11%

commit v1 on v0

v1 whole, which is shorter than its diff:
```python
import functools

import jax
import jax.numpy as jnp
from jax import lax
from jax.experimental import pallas as pl
from jax.experimental.pallas import tpu as pltpu
from jax.sharding import PartitionSpec as P

HEADS = 8
HEAD_DIM = 64
D = 512
E = 128
BLK = 128
GLOB = 2
ITEMS = 5
EVENTS = 512
NBD = EVENTS // BLK
PAIRS = HEADS // 2
NDEV = 128
NSEQ = 16
CHUNKS = 2 * GLOB
ROWS = 4096
SLOTS = 32
FIRST = 64.0
HI = 4
LO = ROWS // HI
BF = jnp.bfloat16
F32 = jnp.float32
VMEM_LIMIT = 24 * 1024 * 1024
SMEM_SPEC = pl.BlockSpec(memory_space=pltpu.SMEM)
VMEM_SPEC = pl.BlockSpec(memory_space=pltpu.VMEM)
ANY_SPEC = pl.BlockSpec(memory_space=pl.ANY)
XSIZE = 4


def dot(a, b):
    return jnp.dot(a, b, preferred_element_type=F32)


def dot_nt(a, b):
    return lax.dot_general(a, b, (((1,), (1,)), ((), ())), preferred_element_type=F32)


def dot_tn(a, b):
    return lax.dot_general(a, b, (((0,), (0,)), ((), ())), preferred_element_type=F32)


def params(**more):
    return pltpu.CompilerParams(vmem_limit_bytes=VMEM_LIMIT, **more)


def fast(shape, dtype):
    return pltpu.VMEM(shape, dtype)


def slow(shape, dtype):
    return pltpu.HBM(shape, dtype)


def in_vmem(*arrays):
    return [pltpu.with_memory_space_constraint(x, pltpu.VMEM) for x in arrays]


def in_hbm(*arrays):
    return [pltpu.with_memory_space_constraint(x, pltpu.HBM) for x in arrays]


def whole(shape):
    return pl.BlockSpec(shape, lambda *_: (0,) * len(shape))


def iota(shape, dim):
    return lax.broadcasted_iota(jnp.int32, shape, dim)


def chunk_of(shift):
    return (lax.axis_index("seq") + shift) % XSIZE


def pieces_kernel(gids, key, value, halo, cand0, cand1, cand2, cand3, sems):
    seq = lax.axis_index("seq")
    tail = pl.ds(EVENTS - BLK, BLK)
    tails = [
        pltpu.make_async_copy(src.at[tail, :], halo.at[i], sems.at[CHUNKS + i])
        for i, src in enumerate((key, value))
    ]
    for copy in tails:
        copy.start()
    cases = []
    for d, out in enumerate((cand0, cand1, cand2, cand3)):
        c = chunk_of(d)
        gid = gids[0, c % GLOB]
        place = pl.ds(pl.multiple_of((gid % NBD) * BLK, BLK), BLK)
        held = gid // NBD == seq
        for i, src in enumerate((key, value)):
            copy = pltpu.make_async_copy(src.at[place, :], out, sems.at[d])
            cases.append((held & (c // GLOB == i), copy))

        @pl.when(jnp.logical_not(held))
        def _():
            out[...] = jnp.zeros((BLK, D), BF)

    for case, copy in cases:

        @pl.when(case)
        def _():
            copy.start()

    for case, copy in cases:

        @pl.when(case)
        def _():
            copy.wait()

    for copy in tails:
        copy.wait()


def pieces(gids, key, value):
    return pl.pallas_call(
        pieces_kernel,
        out_shape=(jax.ShapeDtypeStruct((2, BLK, D), BF),)
        + (jax.ShapeDtypeStruct((BLK, D), BF),) * CHUNKS,
        in_specs=[SMEM_SPEC] + [ANY_SPEC] * 2,
        out_specs=[VMEM_SPEC] * (1 + CHUNKS),
        scratch_shapes=[pltpu.SemaphoreType.DMA((CHUNKS + 2,))],
        compiler_params=params(),
        cost_estimate=pl.CostEstimate(flops=10**6, bytes_accessed=2 * 10**6, transcendentals=0),
        name="pieces",
    )(gids, *in_hbm(key, value))


def route_kernel(owner, row, req, code):
    dev = iota((NDEV, EVENTS), 0)
    rows = jnp.full((NDEV, EVENTS), -1, jnp.int32)
    for j in range(ITEMS):
        rows = jnp.where(owner[j] == dev, row[j], rows)
    hit = rows >= 0
    before = jnp.where(iota((EVENTS, EVENTS), 0) < iota((EVENTS, EVENTS), 1), 1.0, 0.0).astype(BF)
    rank = dot(jnp.where(hit, 1.0, 0.0).astype(BF), before)
    rank = jnp.where(hit, rank, -1.0)
    code[...] = jnp.where(owner[0] == dev, rank + FIRST, rank)
    plus = (rows + 1).astype(F32)
    lane = iota((NDEV, E), 1) - (lax.axis_index("user") % (E // SLOTS)) * SLOTS
    asked = jnp.zeros((NDEV, E), F32)
    for k in range(SLOTS):
        column = jnp.sum(jnp.where(rank == k, plus, 0.0), axis=1, keepdims=True)
        asked = jnp.where(lane == k, column, asked)
    req[...] = asked.astype(jnp.int32)


def route(owner, row):
    return pl.pallas_call(
        route_kernel,
        out_shape=(
            slow((NDEV, E), jnp.int32),
            slow((NDEV, EVENTS), F32),
        ),
        in_specs=[VMEM_SPEC] * 2,
        out_specs=[VMEM_SPEC] * 2,
        compiler_params=params(),
        cost_estimate=pl.CostEstimate(flops=10**8, bytes_accessed=10**6, transcendentals=0),
        name="route",
    )(*in_hbm(owner, row))


def slot_rows(asked, count):
    rows = asked[pl.ds(0, count, stride=4), :]
    for j in range(1, 4):
        rows = rows + asked[pl.ds(j, count, stride=4), :]
    return rows - 1


def slot_columns(rows):
    count = rows.shape[0]
    full = jnp.concatenate([rows.astype(F32), jnp.zeros((E - count, E), F32)], axis=0)
    return full.T[:, :count].astype(jnp.int32)


def spread_columns(x, first, count):
    return jnp.concatenate(
        [jnp.broadcast_to(x[:, i : i + 1], (E, E)) for i in range(first, first + count)], axis=0
    )


def gather_kernel(asked, table_far, found_far, table, found, sems):
    slabs = [slice(h * LO, (h + 1) * LO) for h in range(HI)]
    loads = [
        pltpu.make_async_copy(table_far.at[slab, :], table.at[slab, :], sems.at[h])
        for h, slab in enumerate(slabs)
    ]
    for load in loads:
        load.start()
    columns = slot_columns(slot_rows(asked, NDEV // 4))
    lo = columns & (LO - 1)
    hi = columns >> (LO.bit_length() - 1)
    group = 8
    size = group * E
    lane = iota((size, E), 1)
    sends = []
    for step in range(NDEV // 4 // group):
        low = spread_columns(lo, step * group, group)
        high = spread_columns(hi, step * group, group)
        onehot = jnp.concatenate(
            [jnp.where(low == lane + b * E, 1.0, 0.0).astype(BF) for b in range(LO // E)], axis=1
        )
        if step == 0:
            for load in loads:
                load.wait()
        picked = dot(onehot, jnp.concatenate([table[slab, :] for slab in slabs], axis=1))
        out = jnp.zeros((size, E), F32)
        for h in range(HI):
            out = jnp.where(high == h, picked[:, h * E : (h + 1) * E], out)
        rows = slice(step * size, (step + 1) * size)
        found[rows, :] = out.astype(BF)
        sends.append(
            pltpu.make_async_copy(found.at[rows, :], found_far.at[rows, :], sems.at[HI + step])
        )
        sends[-1].start()
    for send in sends:
        send.wait()


def gather(asked, table):
    return pl.pallas_call(
        gather_kernel,
        out_shape=slow((NDEV * SLOTS, E), BF),
        in_specs=[VMEM_SPEC, ANY_SPEC],
        out_specs=ANY_SPEC,
        scratch_shapes=[
            pltpu.VMEM((ROWS, E), BF),
            pltpu.VMEM((NDEV * SLOTS, E), BF),
            pltpu.SemaphoreType.DMA((HI + 4,)),
        ],
        compiler_params=params(),
        cost_estimate=pl.CostEstimate(
            flops=2 * NDEV * SLOTS * ROWS * E, bytes_accessed=2 * 10**6, transcendentals=0
        ),
        name="gather_rows",
    )(asked, *in_hbm(table))


HALVES = 2


def scatter_kernel(half, asked, incoming, *refs):
    grad, spread = refs[-2:]
    rows = slot_rows(asked, NDEV // 4)
    hi = slot_columns(rows) >> (LO.bit_length() - 1)
    group = 2
    size = group * E
    for first in range(0, NDEV // 4, group):
        high = spread_columns(hi, first, group)
        part = incoming[first * E : first * E + size, :].astype(F32)
        for h in range(HI):
            spread[first * E : first * E + size, h * E : (h + 1) * E] = jnp.where(
                high == h, part, 0.0
            ).astype(BF)
    size = LO // HALVES
    sub = iota((size, E), 0) + half * size
    lo = rows & (LO - 1)
    onehot = jnp.concatenate(
        [jnp.where(sub == lo[i : i + 1, :], 1.0, 0.0).astype(BF) for i in range(NDEV // 4)], axis=1
    )
    total = dot(onehot, spread[...])
    for h in range(HI):
        grad[h] = total[:, h * E : (h + 1) * E]


def scatter(half, asked, incoming, before=()):
    count = NDEV * SLOTS
    return pl.pallas_call(
        functools.partial(scatter_kernel, half),
        grid=(1,),
        out_shape=slow((HI, LO, E), F32),
        in_specs=[whole((NDEV, E)), whole((count, E))] + [ANY_SPEC] * len(before),
        out_specs=pl.BlockSpec((HI, LO // HALVES, E), lambda i: (0, half, 0)),
        scratch_shapes=[pltpu.VMEM((count, HI * E), BF)],
        input_output_aliases={2 + i: i for i in range(len(before))},
        compiler_params=params(),
        cost_estimate=pl.CostEstimate(
            flops=count * ROWS * E, bytes_accessed=2 * 10**6, transcendentals=0
        ),
        name="scatter_rows",
    )(asked, incoming, *in_hbm(*before))


def head_masks():
    lane = iota((1, 2 * HEAD_DIM), 1)
    return [
        jnp.where(lane < HEAD_DIM, 1.0, 0.0).astype(BF),
        jnp.where(lane >= HEAD_DIM, 1.0, 0.0).astype(BF),
    ]


def act(u, mask):
    w = jnp.where(mask, 1.0 + jnp.tanh(u), 0.0)
    p = u * w
    return p.astype(BF), (w + p * (2.0 - w)).astype(BF)


def near_forward_kernel(lengths, q, k, v, halo, probs, slope, attn):
    base = lax.axis_index("seq") * NBD
    length = lengths[lax.axis_index("user")]
    masks = head_masks()
    q16 = q[...] * jnp.asarray(1.0 / 16.0, BF)
    kx = jnp.concatenate([halo[0], k[...]], axis=0)
    vx = jnp.concatenate([halo[1], v[...]], axis=0)
    lane = iota((BLK, 2 * BLK), 1)
    sub = iota((BLK, 2 * BLK), 0)
    vx_m = [vx * m for m in masks]
    both = [jnp.concatenate([q16[i * BLK : (i + 1) * BLK] * m for m in masks]) for i in range(NBD)]
    logits = [dot_nt(both[i], kx[i * BLK : (i + 2) * BLK]) for i in range(NBD)]
    held = []
    for i in range(NBD):
        rows = slice(i * BLK, (i + 1) * BLK)
        at = (base + i - 1) * BLK + lane
        mask = (at >= 0) & (at < length) & (lane <= sub + BLK)
        parts = []
        for h in range(2):
            p, f = act(logits[i][h * BLK : (h + 1) * BLK], mask)
            probs[h, rows, :] = p
            slope[h, rows, :] = f
            parts.append(p)
        held.append(jnp.concatenate(parts, axis=1))
    for i in range(NBD):
        keys = slice(i * BLK, (i + 2) * BLK)
        attn[i * BLK : (i + 1) * BLK, :] = dot(
            held[i], jnp.concatenate([m[keys] for m in vx_m], axis=0)
        )


def unrotate(parts, scratch):
    for d in range(CHUNKS):
        scratch[chunk_of(CHUNKS - d)] = parts[d][...]
    keys = jnp.concatenate([scratch[g] for g in range(GLOB)], axis=0)
    values = jnp.concatenate([scratch[GLOB + g] for g in range(GLOB)], axis=0)
    return keys, values


def far_forward_kernel(
    lengths,
    gids,
    q,
    glob0,
    glob1,
    glob2,
    glob3,
    near,
    gate,
    history,
    w_out,
    probs,
    slope,
    normed_out,
    inv_out,
    user,
    attn,
    scratch,
):
    pair = pl.program_id(0)
    base = lax.axis_index("seq") * NBD
    length = lengths[lax.axis_index("user")]
    masks = head_masks()
    q16 = q[...] * jnp.asarray(1.0 / 16.0, BF)
    kg, vg = unrotate((glob0, glob1, glob2, glob3), scratch)
    lane = iota((BLK, 2 * BLK), 1)
    gid = jnp.where(lane < BLK, gids[0, 0], gids[0, 1])
    at = gid * BLK + lane % BLK
    vg_both = jnp.concatenate([vg * m for m in masks], axis=0)
    logits = dot_nt(jnp.concatenate([q16 * m for m in masks], axis=0), kg)
    held = []
    for i in range(NBD):
        rows = slice(i * BLK, (i + 1) * BLK)
        mask = (gid < base + i - 1) & (at < length)
        parts = []
        for h in range(2):
            p, f = act(logits[h * EVENTS + i * BLK : h * EVENTS + (i + 1) * BLK], mask)
            probs[h, rows, :] = p
            slope[h, rows, :] = f
            parts.append(p)
        held.append(jnp.concatenate(parts, axis=1))
    attn[pair] = near[...] + dot(jnp.concatenate(held, axis=0), vg_both)

    @pl.when(pair == PAIRS - 1)
    def _():
        step = 128
        for r in range(0, EVENTS, step):
            rows = slice(r, r + step)
            x = jnp.concatenate([attn[p, rows, :] for p in range(PAIRS)], axis=1)
            centered = x - jnp.mean(x, axis=1, keepdims=True)
            var = jnp.mean(centered * centered, axis=1, keepdims=True)
            inv = lax.rsqrt(var + 1e-05)
            normed = centered * inv
            normed_out[rows, :] = normed
            inv_out[rows, :] = inv
            gated = (normed * gate[rows, :].astype(F32)).astype(BF)
            user[rows, :] = dot(gated, w_out[...]) + history[rows, :].astype(F32)


def pair_block(rows):
    return pl.BlockSpec((rows, 2 * HEAD_DIM), lambda p: (0, p))


def pair_stack(rows):
    return pl.BlockSpec((2, rows, 2 * HEAD_DIM), lambda p: (0, 0, p))


def head_block():
    return pl.BlockSpec((2, EVENTS, 2 * BLK), lambda p: (p, 0, 0))


SQUARE = slow((HEADS, EVENTS, 2 * BLK), BF)


def near_forward(lengths, q, k, v, halo):
    return pl.pallas_call(
        near_forward_kernel,
        grid=(PAIRS,),
        out_shape=(SQUARE, SQUARE, fast((EVENTS, D), F32)),
        in_specs=[SMEM_SPEC] + [pair_block(EVENTS)] * 3 + [pair_stack(BLK)],
        out_specs=[head_block(), head_block(), pair_block(EVENTS)],
        compiler_params=params(),
        cost_estimate=pl.CostEstimate(
            flops=5 * 10**8, bytes_accessed=7 * 10**6, transcendentals=10**6
        ),
        name="near_forward",
    )(lengths, q, k, v, halo)


def far_forward(lengths, gids, q, glob, near, gate, history, w_out):
    return pl.pallas_call(
        far_forward_kernel,
        grid=(PAIRS,),
        out_shape=(
            SQUARE,
            SQUARE,
            slow((EVENTS, D), F32),
            slow((EVENTS, 1), F32),
            slow((EVENTS, E), F32),
        ),
        in_specs=[SMEM_SPEC] * 2
        + [pair_block(EVENTS)]
        + [pair_block(BLK)] * CHUNKS
        + [pair_block(EVENTS)]
        + [whole((EVENTS, D)), whole((EVENTS, E)), whole((D, E))],
        out_specs=[
            head_block(),
            head_block(),
            whole((EVENTS, D)),
            whole((EVENTS, 1)),
            whole((EVENTS, E)),
        ],
        scratch_shapes=[
            pltpu.VMEM((PAIRS, EVENTS, 2 * HEAD_DIM), F32),
            pltpu.VMEM((CHUNKS, BLK, 2 * HEAD_DIM), BF),
        ],
        compiler_params=params(),
        cost_estimate=pl.CostEstimate(
            flops=6 * 10**8, bytes_accessed=9 * 10**6, transcendentals=10**6
        ),
        name="far_forward",
    )(lengths, gids, q, *glob, *in_vmem(near), gate, history, w_out)


def far_backward_kernel(
    q, glob0, glob1, glob2, glob3, grad, probs, slope, d_q, out0, out1, out2, out3, scratch
):
    masks = head_masks()
    sixteenth = jnp.asarray(1.0 / 16.0, BF)
    q16 = q[...] * sixteenth
    kg, vg = unrotate((glob0, glob1, glob2, glob3), scratch)
    do = grad[...]
    q_t = jnp.concatenate([(q16 * m).T for m in masks], axis=1)
    do_t = jnp.concatenate([(do * m).T for m in masks], axis=1)
    kg_both = jnp.concatenate([kg * (m * sixteenth) for m in masks], axis=0)
    d_probs = dot_nt(jnp.concatenate([do * m for m in masks], axis=0), vg)
    ds = [
        (d_probs[h * EVENTS : (h + 1) * EVENTS] * slope[h].astype(F32)).astype(BF) for h in range(2)
    ]
    d_q[...] = dot(jnp.concatenate(ds, axis=1), kg_both)
    d_k = dot(q_t, jnp.concatenate(ds, axis=0)).T.astype(BF)
    d_v = dot(do_t, jnp.concatenate([probs[0], probs[1]], axis=0)).T.astype(BF)
    for g in range(GLOB):
        scratch[g] = d_k[g * BLK : (g + 1) * BLK]
        scratch[GLOB + g] = d_v[g * BLK : (g + 1) * BLK]
    for d, out in enumerate((out0, out1, out2, out3)):
        out[...] = scratch[chunk_of(d)]


def far_backward(q, glob, grad, probs, slope):
    return pl.pallas_call(
        far_backward_kernel,
        grid=(PAIRS,),
        out_shape=(fast((EVENTS, D), F32),)
        + (jax.ShapeDtypeStruct((BLK, D), BF),) * CHUNKS,
        in_specs=[pair_block(EVENTS)]
        + [pair_block(BLK)] * CHUNKS
        + [pair_block(EVENTS)]
        + [head_block()] * 2,
        out_specs=[pair_block(EVENTS)] + [pair_block(BLK)] * CHUNKS,
        scratch_shapes=[pltpu.VMEM((CHUNKS, BLK, 2 * HEAD_DIM), BF)],
        compiler_params=params(),
        cost_estimate=pl.CostEstimate(
            flops=10**9, bytes_accessed=7 * 10**6, transcendentals=0
        ),
        name="far_backward",
    )(*in_hbm(q), *glob, *in_hbm(grad, probs, slope))


def near_backward_kernel(q, k, v, halo, grad, probs, slope, far, d_q, d_k, d_v, edge):
    masks = head_masks()
    sixteenth = jnp.asarray(1.0 / 16.0, BF)
    q16 = q[...] * sixteenth
    kx = jnp.concatenate([halo[0], k[...]], axis=0)
    vx = jnp.concatenate([halo[1], v[...]], axis=0)
    do = grad[...]
    q_t = [(q16 * m).T for m in masks]
    do_t = [(do * m).T for m in masks]
    kx_m = [kx * (m * sixteenth) for m in masks]
    blocks = [slice(i * BLK, (i + 1) * BLK) for i in range(NBD)]
    windows = [slice(i * BLK, (i + 2) * BLK) for i in range(NBD)]
    d_probs = [
        dot_nt(jnp.concatenate([do[blocks[i]] * m for m in masks], axis=0), vx[windows[i]])
        for i in range(NBD)
    ]
    all_ds = [
        [
            (d_probs[i][h * BLK : (h + 1) * BLK] * slope[h, blocks[i], :].astype(F32)).astype(BF)
            for h in range(2)
        ]
        for i in range(NBD)
    ]
    carry = None
    for i in range(NBD):
        rows, keys, ds = blocks[i], windows[i], all_ds[i]
        near_k = jnp.concatenate([m[keys] for m in kx_m], axis=0)
        d_q[rows, :] = (far[rows, :] + dot(jnp.concatenate(ds, axis=1), near_k)).astype(BF)
        near_p = jnp.concatenate([probs[h, rows, :] for h in range(2)], axis=0)
        dk = dot(jnp.concatenate([t[:, rows] for t in q_t], axis=1), jnp.concatenate(ds, axis=0)).T
        dv = dot(jnp.concatenate([t[:, rows] for t in do_t], axis=1), near_p).T
        if i == 0:
            edge[0] = dk[:BLK].astype(BF)
            edge[1] = dv[:BLK].astype(BF)
        else:
            last = slice((i - 1) * BLK, i * BLK)
            d_k[last, :] = (carry[0] + dk[:BLK]).astype(BF)
            d_v[last, :] = (carry[1] + dv[:BLK]).astype(BF)
        carry = (dk[BLK:], dv[BLK:])
    last = slice((NBD - 1) * BLK, NBD * BLK)
    d_k[last, :] = carry[0].astype(BF)
    d_v[last, :] = carry[1].astype(BF)


def near_backward(q, k, v, halo, grad, probs, slope, far):
    rows = jax.ShapeDtypeStruct((EVENTS, D), BF)
    return pl.pallas_call(
        near_backward_kernel,
        grid=(PAIRS,),
        out_shape=(
            rows,
            slow((EVENTS, D), BF),
            slow((EVENTS, D), BF),
            jax.ShapeDtypeStruct((2, BLK, D), BF),
        ),
        in_specs=[pair_block(EVENTS)] * 3
        + [pair_stack(BLK), pair_block(EVENTS)]
        + [head_block()] * 2
        + [pair_block(EVENTS)],
        out_specs=[pair_block(EVENTS)] * 3 + [pair_stack(BLK)],
        compiler_params=params(),
        cost_estimate=pl.CostEstimate(
            flops=10**9, bytes_accessed=9 * 10**6, transcendentals=0
        ),
        name="near_backward",
    )(q, k, v, halo, grad, probs, slope, *in_vmem(far))


def middle_kernel(
    lengths,
    code,
    user,
    inv,
    w_out,
    items_far,
    normed_far,
    gate_far,
    out_far,
    attn_far,
    gated_far,
    score,
    items,
    normed,
    gate,
    outgoing,
    d_attn,
    d_gate,
    sems,
):
    parts = 4
    portion = NDEV * SLOTS // parts
    slices = [slice(i * portion, (i + 1) * portion) for i in range(parts)]
    item_loads = [
        pltpu.make_async_copy(items_far.at[rows, :], items.at[rows, :], sems.at[3 + i])
        for i, rows in enumerate(slices)
    ]
    loads = [
        pltpu.make_async_copy(normed_far, normed, sems.at[0]),
        pltpu.make_async_copy(gate_far, gate, sems.at[1]),
    ]
    for load in item_loads + loads:
        load.start()
    send = pltpu.make_async_copy(outgoing, out_far, sems.at[2])
    user_b = user[...].astype(BF)
    user_t = user[...].T.astype(BF)
    first = code[...] >= FIRST
    rank = jnp.where(first, code[...] - FIRST, code[...])
    group = 8
    size = group * SLOTS
    slot = iota((SLOTS, EVENTS), 0).astype(F32)
    for d in range(0, NDEV, group):
        if d * SLOTS % portion == 0:
            item_loads[d * SLOTS // portion].wait()
        s = dot(items[d * SLOTS : d * SLOTS + size, :], user_t)
        for r in range(group):
            own = rank[d + r : d + r + 1, :] == slot
            part = jnp.where(own, s[r * SLOTS : (r + 1) * SLOTS, :], 0.0)
            score[d + r : d + r + 1, :] = jnp.sum(part, axis=0, keepdims=True)
    score0 = jnp.sum(jnp.where(first, score[...], 0.0), axis=0, keepdims=True)
    event = lax.axis_index("seq") * EVENTS + iota((1, EVENTS), 1)
    valid = jnp.where(event < lengths[lax.axis_index("user")], 1.0, 0.0)
    other = (rank >= 0.0) & jnp.logical_not(first)
    side = jnp.where(other, jax.nn.sigmoid(score[...] - score0), 0.0) * valid
    coef = jnp.where(first, -jnp.sum(side, axis=0, keepdims=True), side)
    d_user_t = jnp.zeros((E, EVENTS), F32)
    for d in range(0, NDEV, group):
        c = jnp.concatenate(
            [
                jnp.where(rank[r : r + 1, :] == slot, coef[r : r + 1, :], 0.0).astype(BF)
                for r in range(d, d + group)
            ],
            axis=0,
        )
        rows = slice(d * SLOTS, d * SLOTS + size)
        outgoing[rows, :] = dot(c, user_b).astype(BF)
        d_user_t = d_user_t + dot_tn(items[rows, :], c)
    send.start()
    sends = [send]
    d_user = d_user_t.T.astype(BF)
    for load in loads:
        load.wait()
    step = 128
    for r in range(0, EVENTS, step):
        rows = slice(r, r + step)
        d_gated = dot_nt(d_user[rows], w_out[...])
        n = normed[rows, :]
        d_gate[rows, :] = (d_gated * n).astype(BF)
        dn = d_gated * gate[rows, :].astype(F32)
        d_attn[rows, :] = (
            (
                dn
                - jnp.mean(dn, axis=1, keepdims=True)
                - n * jnp.mean(dn * n, axis=1, keepdims=True)
            )
            * inv[rows, :]
        ).astype(BF)
        for i, (near, far) in enumerate(((d_attn, attn_far), (d_gate, gated_far))):
            copy = pltpu.make_async_copy(
                near.at[rows, :], far.at[rows, :], sems.at[3 + parts + 2 * (r // step) + i]
            )
            copy.start()
            sends.append(copy)
    for send in sends:
        send.wait()


def middle(lengths, items, code, user, normed, inv, gate, w_out):
    return pl.pallas_call(
        middle_kernel,
        out_shape=(
            slow((NDEV * SLOTS, E), BF),
            slow((EVENTS, D), BF),
            slow((EVENTS, D), BF),
        ),
        in_specs=[SMEM_SPEC] + [VMEM_SPEC] * 4 + [ANY_SPEC] * 3,
        out_specs=[ANY_SPEC] * 3,
        scratch_shapes=[
            pltpu.VMEM((NDEV, EVENTS), F32),
            pltpu.VMEM((NDEV * SLOTS, E), BF),
            pltpu.VMEM((EVENTS, D), F32),
            pltpu.VMEM((EVENTS, D), BF),
            pltpu.VMEM((NDEV * SLOTS, E), BF),
            pltpu.VMEM((EVENTS, D), BF),
            pltpu.VMEM((EVENTS, D), BF),
            pltpu.SemaphoreType.DMA((3 + 4 + 2 * EVENTS // 128,)),
        ],
        compiler_params=params(),
        cost_estimate=pl.CostEstimate(
            flops=2 * 10**9, bytes_accessed=6 * 10**6, transcendentals=10**5
        ),
        name="ranking",
    )(lengths, *in_hbm(code, user, inv, w_out, items, normed, gate))


def finish_kernel(gids, d_k, d_v, edge, glob0, glob1, glob2, glob3, key_out, value_out):
    seq = lax.axis_index("seq")
    outs = (key_out, value_out)
    for which, mine in enumerate((d_k, d_v)):
        outs[which][...] = mine[...]
        tail = slice(EVENTS - BLK, EVENTS)
        outs[which][tail, :] = (mine[tail, :].astype(F32) + edge[which].astype(F32)).astype(BF)
    for d, more in enumerate((glob0, glob1, glob2, glob3)):
        c = chunk_of(CHUNKS - d)
        gid = gids[0, c % GLOB]
        place = pl.ds(pl.multiple_of((gid % NBD) * BLK, BLK), BLK)
        for which in range(2):

            @pl.when((gid // NBD == seq) & (c // GLOB == which))
            def _():
                out = outs[which]
                out[place, :] = (out[place, :].astype(F32) + more[...].astype(F32)).astype(BF)


def finish(gids, d_k, d_v, edge, total):
    rows = jax.ShapeDtypeStruct((EVENTS, D), BF)
    return pl.pallas_call(
        finish_kernel,
        out_shape=(rows, rows),
        in_specs=[SMEM_SPEC] + [VMEM_SPEC] * (3 + CHUNKS),
        out_specs=[VMEM_SPEC] * 2,
        compiler_params=params(),
        cost_estimate=pl.CostEstimate(flops=10**6, bytes_accessed=3 * 10**6, transcendentals=0),
        name="add_received",
    )(gids, d_k, d_v, edge, *total)


def from_behind(block, axis, distance):
    devices = range(lax.axis_size(axis))
    route_pairs = [(i - distance, i) for i in devices if i - distance in devices]
    return lax.ppermute(block, axis, route_pairs)


def exchange(x, axis):
    return lax.all_to_all(x, axis, split_axis=0, concat_axis=0, tiled=True)


def around_x(x, distance):
    pairs = [(i, i // XSIZE * XSIZE + (i + distance) % XSIZE) for i in range(NSEQ)]
    return lax.ppermute(x, "seq", pairs)


def around_z(x, distance):
    return lax.ppermute(x, "seq", [(i, (i + distance * XSIZE) % NSEQ) for i in range(NSEQ)])


def add_all(parts):
    return sum(p.astype(F32) for p in parts).astype(BF)


def from_x(chunks):
    return [chunks[0]] + [around_x(chunks[d], d) for d in range(1, CHUNKS)]


def from_z(mine):
    return [mine] + [around_z(mine, d) for d in range(1, NSEQ // XSIZE)]


def share_x(mine):
    return [mine] + [around_x(mine, d) for d in range(1, CHUNKS)]


def together(*values):
    return lax.optimization_barrier(values)


def on_device(
    query, key, value, gate, history, w_out, table, item_owner, item_row, gids, lengths
):
    q, k, v = query[0], key[0], value[0]
    owner = jnp.transpose(item_owner, (2, 0, 1))
    row = jnp.transpose(item_row, (2, 0, 1))
    tail, *cand = pieces(gids, k, v)
    parts = from_x(cand)
    owner, _ = together(owner, cand[0])
    req, code = route(owner, row)
    req, *parts = together(req, *parts)
    mine = add_all(parts)
    req, mine = together(req, mine)
    parts = from_z(mine)
    asked = exchange(req.reshape(NDEV, 1, E), ("seq", "user")).reshape(NDEV, E)
    mine = add_all(parts)
    glob = share_x(mine)
    halo = from_behind(tail, "seq", 1)
    asked, _ = together(asked, mine)
    found = gather(asked, table)
    found, halo, *glob = together(found, halo, *glob)
    items = exchange(found.reshape(NDEV, SLOTS, E), ("seq", "user")).reshape(NDEV * SLOTS, E)
    near_p, near_f, near = near_forward(lengths, q, k, v, halo)
    far_p, far_f, normed, inv, user = far_forward(
        lengths, gids, q, glob, near, gate[0], history[0], w_out
    )
    outgoing, d_attn, d_gate = middle(lengths, items, code, user, normed, inv, gate[0], w_out)
    incoming = exchange(outgoing.reshape(NDEV, SLOTS, E), ("seq", "user"))
    far_q, *d_glob = far_backward(q, glob, d_attn, far_p, far_f)
    parts = from_x(d_glob)
    d_q, d_k, d_v, edge = near_backward(q, k, v, halo, d_attn, near_p, near_f, far_q)
    d_k, *parts = together(d_k, *parts)
    mine = add_all(parts)
    back = from_behind(edge, "seq", -1)
    incoming, mine = together(incoming.reshape(NDEV * SLOTS, E), mine)
    grad = scatter(0, asked, incoming)
    grad, *parts = together(grad, *from_z(mine))
    mine = add_all(parts)
    grad, mine = together(grad, mine)
    grad = scatter(1, asked, incoming, (grad,))
    grad, *total = together(grad, *share_x(mine))
    d_key, d_value = finish(gids, d_k, d_v, back, total)
    return (d_q[None], d_key[None], d_value[None], d_gate[None], grad.reshape(ROWS, E))


def solution(mesh):
    return jax.shard_map(
        on_device,
        mesh=mesh,
        in_specs=(
            P("user", "seq", None),
            P("user", "seq", None),
            P("user", "seq", None),
            P("user", "seq", None),
            P("user", "seq", None),
            P(),
            P(("seq", "user"), None),
            P("user", "seq", None),
            P("user", "seq", None),
            P("user", None),
            P(),
        ),
        out_specs=(
            P("user", "seq", None),
            P("user", "seq", None),
            P("user", "seq", None),
            P("user", "seq", None),
            P(("seq", "user"), None),
        ),
        check_vma=False,
    )
```

time: 183 us -> 129 us (0.70); the launches traced: 180 us -> 128 us
  blocking collectives: 28.6 us -> 0 us
  waiting for transfers between devices: 44.8 us -> 21.9 us
  starting transfers between devices: 42 us -> 56 us
  local copies, waits for them, and re-layouts: 11.2 us -> 0.73 us
  other arithmetic: 2.79 us -> 0.27 us
  between operations: 3.37 us -> 0.98 us
    ppermute x0 -> x18, starting transfers between devices: none -> 32.1 us  [the longest x12 21.2 us: around_x(): return lax.ppermute(x, 'seq', pairs)]
    ppermute x2, waiting for transfers between devices: 29 us -> 0.01 us  [from_behind(): return lax.ppermute(block, axis, route_pairs)]
    all_to_all x2 -> x0, blocking collectives: 28.6 us -> none  [exchange(): return lax.all_to_all(x, axis, split_axis=0, concat_axis=0, tiled=True)]
    all_to_all x5 -> x3, starting transfers between devices: 34 us -> 18.7 us  [exchange(): return lax.all_to_all(x, axis, split_axis=0, concat_axis=0, tiled=True)]
    ppermute x0 -> x18, waiting for transfers between devices: none -> 9.53 us  [the longest x12 9.06 us: around_x(): return lax.ppermute(x, 'seq', pairs)]
    unnamed x16 -> x30, local copies, waits for them, and re-layouts: 4.78 us -> 0.73 us
    all_to_all x5 -> x3, waiting for transfers between devices: 15.8 us -> 12.4 us  [exchange(): return lax.all_to_all(x, axis, split_axis=0, concat_axis=0, tiled=True)]
    ppermute x2, starting transfers between devices: 8.03 us -> 5.14 us  [from_behind(): return lax.ppermute(block, axis, route_pairs)]
  transfers between devices with their start and end apart: 7 -> 23, of which waited for: 5 -> 8; matrix products, arithmetic and copies ran while one was open for 2% -> 0% of each run, Pallas kernels for 11% -> 29%
where the time goes in v1:
time: 129 us; the launch traced here: 128 us
  starting transfers between devices  56 us (43%)
  Pallas kernels  48.6 us (38%)
  waiting for transfers between devices  21.9 us (17%)
    ppermute x12, starting transfers between devices, around_x(): return lax.ppermute(x, 'seq', pairs)  21.2 us
    all_to_all x3, starting transfers between devices, exchange(): return lax.all_to_all(x, axis, split_axis=0, concat_axis=0, tiled=True)  18.7 us
    all_to_all x3, waiting for transfers between devices, exchange(): return lax.all_to_all(x, axis, split_axis=0, concat_axis=0, tiled=True)  12.4 us
    ppermute x6, starting transfers between devices, around_z(): lax.ppermute(x, 'seq', [(i, (i + distance * XSIZE) % NSEQ) for i in range...  11 us
    ppermute x12, waiting for transfers between devices, around_x(): return lax.ppermute(x, 'seq', pairs)  9.06 us
    pallas_call x2, Pallas kernels, scatter(): pl.pallas_call(functools.partial(scatter_kernel, half), grid=(1,), out_sh...  8 us
    pallas_call x1, Pallas kernels, middle(): pl.pallas_call(middle_kernel, out_shape=(slow((NDEV * SLOTS, E), BF), slo...  7.47 us
    pallas_call x1, Pallas kernels, gather(): pl.pallas_call(gather_kernel, out_shape=slow((NDEV * SLOTS, E), BF), in_s...  6.47 us
  transfers between devices with their start and end apart: 23, of which 8 were waited for; matrix products, arithmetic and copies ran while one was open for 0% of the time, Pallas kernels for 29%

profile of v1, /device:TPU:32, one launch (start us, length us, event | category | flops | bytes accessed | tf_op | source)
XLA Modules:
  0.0 128.5 jit_solution(11840535407761742520)
XLA Ops:
  0.6 0.0 copy-start.12
  0.6 0.6 copy-done.12
  1.3 2.3 %pieces.1 = (bf16[2,128,512]{2,1,0:T(8,128)(2,1)}, bf16[128,512]{1,0:T(8,128)(2,1)S(1)}, bf16[128,512]{1,0:T(8,128)(2,1)S(1)}, bf16[128,512]{1,0:T(8,128)(2,1)S(1)}, bf16[128,512]{1,0:T(8,128)(2,1)S(1)}) custom-call(s32[1,2]{1,0:T(1,128)S(1)} %copy-done.12, bf16[512,512]{1,0:T(8,128)(2,1)} %bitcast.24, bf16[512,512]{1,0:T(8,128)(2,1)} %bitcast.27), custom_call_target="tpu_custom_call" | custom-call | flops 1000000 | bytes 2000000 | tf_op jit(solution)/shard_map/pieces/pallas_call | solution.py:121
  3.6 1.6 %collective-permute-start = (bf16[128,512]{1,0:T(8,128)(2,1)S(1)}, bf16[128,512]{1,0:T(8,128)(2,1)S(1)}, u32[]{:S(2)}, u32[]{:S(2)}) collective-permute-start(bf16[128,512]{1,0:T(8,128)(2,1)S(1)} %get-tuple-element.71), channel_id=1, source_target_pairs={{0,8},{8,16},{16,24},{24,0},{32,40},{40,48},{48,56},{56,32},{64,72... | collective-permute-start | bytes 393224 | tf_op jit(solution)/shard_map/ppermute | solution.py:750
  5.1 2.9 %collective-permute-start.1 = (bf16[128,512]{1,0:T(8,128)(2,1)S(1)}, bf16[128,512]{1,0:T(8,128)(2,1)S(1)}, u32[]{:S(2)}, u32[]{:S(2)}) collective-permute-start(bf16[128,512]{1,0:T(8,128)(2,1)S(1)} %get-tuple-element.72), channel_id=1, source_target_pairs={{0,16},{8,24},{16,0},{24,8},{32,48},{40,56},{48,32},{56,40},{64,80... | collective-permute-start | bytes 393224 | tf_op jit(solution)/shard_map/ppermute | solution.py:750
  8.0 1.3 collective-permute-start.2
  9.3 2.5 %route.1 = (s32[128,128]{1,0:T(8,128)}, f32[128,512]{1,0:T(8,128)}) custom-call(s32[5,1,512]{2,1,0:T(1,128)} %bitcast.44, s32[5,1,512]{2,1,0:T(1,128)} %bitcast.45), custom_call_target="tpu_custom_call" | custom-call | flops 100000000 | bytes 1000000 | tf_op jit(solution)/shard_map/route/pallas_call | solution.py:154
  11.8 0.0 collective-permute-done
  11.8 2.1 %collective-permute-done.1 = bf16[128,512]{1,0:T(8,128)(2,1)S(1)} collective-permute-done((bf16[128,512]{1,0:T(8,128)(2,1)S(1)}, bf16[128,512]{1,0:T(8,128)(2,1)S(1)}, u32[]{:S(2)}, u32[]{:S(2)}) %collective-permute-start.1) | collective-permute-done | bytes 131104 | tf_op jit(solution)/shard_map/ppermute | solution.py:750
  13.9 0.0 collective-permute-done.2
  13.9 0.1 add_convert_fusion.3
  13.9 0.2 collective-permute-start.5
  14.1 3.3 %collective-permute-start.4 = (bf16[128,512]{1,0:T(8,128)(2,1)S(1)}, bf16[128,512]{1,0:T(8,128)(2,1)S(1)}, u32[]{:S(2)}, u32[]{:S(2)}) collective-permute-start(bf16[128,512]{1,0:T(8,128)(2,1)S(1)} %add_convert_fusion.3), channel_id=1, source_target_pairs={{0,64},{8,72},{16,80},{24,88},{32,96},{40,104},{48,112},{56,120},{... | collective-permute-start | bytes 393224 | tf_op jit(solution)/shard_map/ppermute | solution.py:754
  17.4 2.2 %collective-permute-start.3 = (bf16[128,512]{1,0:T(8,128)(2,1)S(1)}, bf16[128,512]{1,0:T(8,128)(2,1)S(1)}, u32[]{:S(2)}, u32[]{:S(2)}) collective-permute-start(bf16[128,512]{1,0:T(8,128)(2,1)S(1)} %add_convert_fusion.3), channel_id=1, source_target_pairs={{0,32},{8,40},{16,48},{24,56},{32,64},{40,72},{48,80},{56,88},{64,... | collective-permute-start | bytes 393224 | tf_op jit(solution)/shard_map/ppermute | solution.py:754
  19.6 3.2 %collective-permute-start.6 = (bf16[2,128,512]{2,1,0:T(8,128)(2,1)}, bf16[2,128,512]{2,1,0:T(8,128)(2,1)S(1)}, u32[]{:S(2)}, u32[]{:S(2)}) collective-permute-start(bf16[2,128,512]{2,1,0:T(8,128)(2,1)} %get-tuple-element.82), channel_id=1, source_target_pairs={{0,8},{8,16},{16,24},{24,32},{32,40},{40,48},{48,56},{56,64},{64,7... | collective-permute-start | bytes 786440 | tf_op jit(solution)/shard_map/ppermute | solution.py:741
  22.9 7.7 %all-to-all-start = ((s32[128,1,128]{2,1,0:T(1,128)}), s32[128,1,128]{2,1,0:T(1,128)S(1)}, u32[]{:S(2)}, u32[]{:S(2)}) async-start(s32[128,1,128]{2,1,0:T(1,128)} %bitcast.40), calls=%async_computation | async-start | bytes 131072 | tf_op jit(solution)/shard_map/all_to_all | solution.py:745
  30.6 0.0 collective-permute-done.4
  30.6 0.0 collective-permute-done.3
  30.6 0.1 add_convert_fusion.2.glob0
  30.7 2.8 %collective-permute-start.9 = (bf16[128,512]{1,0:T(8,128)(2,1)S(1)}, bf16[128,512]{1,0:T(8,128)(2,1)S(1)}, u32[]{:S(2)}, u32[]{:S(2)}) collective-permute-start(bf16[128,512]{1,0:T(8,128)(2,1)S(1)} %add_convert_fusion.2.glob0), channel_id=1, source_target_pairs={{0,24},{8,0},{16,8},{24,16},{32,56},{40,32},{48,40},{56,48},{64,88... | collective-permute-start | bytes 393224 | tf_op jit(solution)/shard_map/ppermute | solution.py:750
  33.5 0.8 collective-permute-start.8
  34.3 0.9 collective-permute-start.7
  35.2 4.4 %all-to-all-done = s32[128,1,128]{2,1,0:T(1,128)S(1)} async-done(((s32[128,1,128]{2,1,0:T(1,128)}), s32[128,1,128]{2,1,0:T(1,128)S(1)}, u32[]{:S(2)}, u32[]{:S(2)}) %all-to-all-start) | async-done | bytes 65568 | tf_op jit(solution)/shard_map/all_to_all | solution.py:745
  39.6 6.5 %gather_rows.1 = bf16[4096,128]{1,0:T(8,128)(2,1)} custom-call(s32[128,128]{1,0:T(8,128)S(1)} %bitcast.35, bf16[4096,128]{1,0:T(8,128)(2,1)} %table_far.1), custom_call_target="tpu_custom_call" | custom-call | flops 4294967296 | bytes 2000000 | tf_op jit(solution)/shard_map/gather_rows/pallas_call | solution.py:226
  46.1 0.0 copy-start
  46.1 0.0 copy-start.4
  46.1 0.0 copy-start.5
  46.1 0.0 copy-start.7
  46.1 0.0 copy-start.10
  46.1 0.0 copy-start.11
  46.1 0.0 copy-start.13
  46.1 0.0 collective-permute-done.6.halo
  46.2 6.1 %all-to-all-start.1 = ((bf16[128,32,128]{2,1,0:T(8,128)(2,1)}), bf16[128,32,128]{2,1,0:T(8,128)(2,1)}, u32[]{:S(2)}, u32[]{:S(2)}) async-start(bf16[128,32,128]{2,1,0:T(8,128)(2,1)} %bitcast.39), calls=%async_computation.1 | async-start | bytes 2097152 | tf_op jit(solution)/shard_map/all_to_all | solution.py:745
  52.3 4.5 %near_forward.1 = (bf16[8,512,256]{2,1,0:T(8,128)(2,1)}, bf16[8,512,256]{2,1,0:T(8,128)(2,1)}, f32[512,512]{1,0:T(8,128)S(1)}) custom-call(s32[8]{0:T(128)S(1)} %copy-done.14, bf16[512,512]{1,0:T(8,128)(2,1)S(1)} %bitcast.21, bf16[512,512]{1,0:T(8,128)(2,1)S(1)} %bitcast.25, bf16[512,512]{1,0:T(8,128)(2,1)S(1)} %bitcast.28, ...), custom_call_target="tpu_custom_call" | custom-call | flops 500000000 | bytes 7000000 | tf_op jit(solution)/shard_map/near_forward/pallas_call | solution.py:418
  56.9 5.9 %far_forward.1 = (bf16[8,512,256]{2,1,0:T(8,128)(2,1)}, bf16[8,512,256]{2,1,0:T(8,128)(2,1)}, f32[512,512]{1,0:T(8,128)}, f32[512,1]{1,0:T(8,128)}, f32[512,128]{1,0:T(8,128)}) custom-call(s32[8]{0:T(128)S(1)} %copy-done.14, s32[1,2]{1,0:T(1,128)S(1)} %copy-done.13, bf16[512,512]{1,0:T(8,128)(2,1)S(1)} %bitcast.22, ...), custom_call_target="tpu_custom_call" | custom-call | flops 600000000 | bytes 9000000 | tf_op jit(solution)/shard_map/far_forward/pallas_call | solution.py:433
  62.8 8.0 %all-to-all-done.1 = bf16[128,32,128]{2,1,0:T(8,128)(2,1)} async-done(((bf16[128,32,128]{2,1,0:T(8,128)(2,1)}), bf16[128,32,128]{2,1,0:T(8,128)(2,1)}, u32[]{:S(2)}, u32[]{:S(2)}) %all-to-all-start.1) | async-done | bytes 1048608 | tf_op jit(solution)/shard_map/all_to_all | solution.py:745
  70.8 7.5 %ranking.1 = (bf16[4096,128]{1,0:T(8,128)(2,1)}, bf16[512,512]{1,0:T(8,128)(2,1)}, bf16[512,512]{1,0:T(8,128)(2,1)}) custom-call(s32[8]{0:T(128)S(1)} %copy-done.14, f32[128,512]{1,0:T(8,128)} %get-tuple-element.84.code, f32[512,128]{1,0:T(8,128)} %get-tuple-element.90.user, f32[512,1]{1,0:T(8,128)} %get-tuple-element.91.inv, bf16[512,128]{1,0:T(8,128)(2,1)} %w_out.3, ...), custom_call_target="tpu_custom_call" | custom-call | flops 2000000000 | bytes 6000000 | tf_op jit(solution)/shard_map/ranking/pallas_call | solution.py:679
  78.2 4.9 %all-to-all-start.2 = ((bf16[128,32,128]{2,1,0:T(8,128)(2,1)}), bf16[128,32,128]{2,1,0:T(8,128)(2,1)S(1)}, u32[]{:S(2)}, u32[]{:S(2)}) async-start(bf16[128,32,128]{2,1,0:T(8,128)(2,1)} %bitcast.38), calls=%async_computation.2 | async-start | bytes 2097152 | tf_op jit(solution)/shard_map/all_to_all | solution.py:745
  83.1 0.0 copy-start.1
  83.2 0.0 copy-start.2
  83.2 0.0 copy-start.6
  83.2 5.5 %far_backward.1 = (f32[512,512]{1,0:T(8,128)S(1)}, bf16[128,512]{1,0:T(8,128)(2,1)S(1)}, bf16[128,512]{1,0:T(8,128)(2,1)S(1)}, bf16[128,512]{1,0:T(8,128)(2,1)S(1)}, bf16[128,512]{1,0:T(8,128)(2,1)S(1)}) custom-call(bf16[512,512]{1,0:T(8,128)(2,1)} %bitcast.20, bf16[128,512]{1,0:T(8,128)(2,1)S(1)} %add_convert_fusion.2.glob0, ...), custom_call_target="tpu_custom_call" | custom-call | flops 1000000000 | bytes 7000000 | tf_op jit(solution)/shard_map/far_backward/pallas_call | solution.py:493
  88.7 1.5 %collective-permute-start.10 = (bf16[128,512]{1,0:T(8,128)(2,1)S(1)}, bf16[128,512]{1,0:T(8,128)(2,1)S(1)}, u32[]{:S(2)}, u32[]{:S(2)}) collective-permute-start(bf16[128,512]{1,0:T(8,128)(2,1)S(1)} %get-tuple-element.103), channel_id=1, source_target_pairs={{0,8},{8,16},{16,24},{24,0},{32,40},{40,48},{48,56},{56,32},{64,72... | collective-permute-start | bytes 393224 | tf_op jit(solution)/shard_map/ppermute | solution.py:750
  90.3 2.7 %collective-permute-start.11 = (bf16[128,512]{1,0:T(8,128)(2,1)S(1)}, bf16[128,512]{1,0:T(8,128)(2,1)S(1)}, u32[]{:S(2)}, u32[]{:S(2)}) collective-permute-start(bf16[128,512]{1,0:T(8,128)(2,1)S(1)} %get-tuple-element.104), channel_id=1, source_target_pairs={{0,16},{8,24},{16,0},{24,8},{32,48},{40,56},{48,32},{56,40},{64,80... | collective-permute-start | bytes 393224 | tf_op jit(solution)/shard_map/ppermute | solution.py:750
  93.0 1.4 %collective-permute-start.12 = (bf16[128,512]{1,0:T(8,128)(2,1)S(1)}, bf16[128,512]{1,0:T(8,128)(2,1)S(1)}, u32[]{:S(2)}, u32[]{:S(2)}) collective-permute-start(bf16[128,512]{1,0:T(8,128)(2,1)S(1)} %get-tuple-element.105), channel_id=1, source_target_pairs={{0,24},{8,0},{16,8},{24,16},{32,56},{40,32},{48,40},{56,48},{64,88... | collective-permute-start | bytes 393224 | tf_op jit(solution)/shard_map/ppermute | solution.py:750
  94.4 4.2 %near_backward.1 = (bf16[512,512]{1,0:T(8,128)(2,1)}, bf16[512,512]{1,0:T(8,128)(2,1)}, bf16[512,512]{1,0:T(8,128)(2,1)}, bf16[2,128,512]{2,1,0:T(8,128)(2,1)S(1)}) custom-call(bf16[512,512]{1,0:T(8,128)(2,1)S(1)} %bitcast.23, bf16[512,512]{1,0:T(8,128)(2,1)S(1)} %bitcast.26, bf16[512,512]{1,0:T(8,128)(2,1)S(1)} %bitcast.29, ...), custom_call_target="tpu_custom_call" | custom-call | flops 1000000000 | bytes 9000000 | tf_op jit(solution)/shard_map/near_backward/pallas_call | solution.py:558
  98.7 1.9 %collective-permute-start.13 = (bf16[2,128,512]{2,1,0:T(8,128)(2,1)S(1)}, bf16[2,128,512]{2,1,0:T(8,128)(2,1)S(1)}, u32[]{:S(2)}, u32[]{:S(2)}) collective-permute-start(bf16[2,128,512]{2,1,0:T(8,128)(2,1)S(1)} %get-tuple-element.108), channel_id=1, source_target_pairs={{8,0},{16,8},{24,16},{32,24},{40,32},{48,40},{56,48},{64,56},{72,6... | collective-permute-start | bytes 786440 | tf_op jit(solution)/shard_map/ppermute | solution.py:741
  100.6 2.7 %collective-permute-done.11 = bf16[128,512]{1,0:T(8,128)(2,1)S(1)} collective-permute-done((bf16[128,512]{1,0:T(8,128)(2,1)S(1)}, bf16[128,512]{1,0:T(8,128)(2,1)S(1)}, u32[]{:S(2)}, u32[]{:S(2)}) %collective-permute-start.11) | collective-permute-done | bytes 131104 | tf_op jit(solution)/shard_map/ppermute | solution.py:750
  103.3 0.1 add_convert_fusion.1
  103.4 0.4 collective-permute-start.16
  103.8 2.9 %collective-permute-start.15 = (bf16[128,512]{1,0:T(8,128)(2,1)S(1)}, bf16[128,512]{1,0:T(8,128)(2,1)S(1)}, u32[]{:S(2)}, u32[]{:S(2)}) collective-permute-start(bf16[128,512]{1,0:T(8,128)(2,1)S(1)} %add_convert_fusion.1), channel_id=1, source_target_pairs={{0,64},{8,72},{16,80},{24,88},{32,96},{40,104},{48,112},{56,120},{... | collective-permute-start | bytes 393224 | tf_op jit(solution)/shard_map/ppermute | solution.py:754
  106.7 2.0 %collective-permute-start.14 = (bf16[128,512]{1,0:T(8,128)(2,1)S(1)}, bf16[128,512]{1,0:T(8,128)(2,1)S(1)}, u32[]{:S(2)}, u32[]{:S(2)}) collective-permute-start(bf16[128,512]{1,0:T(8,128)(2,1)S(1)} %add_convert_fusion.1), channel_id=1, source_target_pairs={{0,32},{8,40},{16,48},{24,56},{32,64},{40,72},{48,80},{56,88},{64,... | collective-permute-start | bytes 393224 | tf_op jit(solution)/shard_map/ppermute | solution.py:754
  108.7 4.0 %scatter_rows.2.refs_0_ = f32[4,1024,128]{2,1,0:T(8,128)} custom-call(s32[128,128]{1,0:T(8,128)S(1)} %bitcast.36, bf16[4096,128]{1,0:T(8,128)(2,1)S(1)} %bitcast.30), custom_call_target="tpu_custom_call" | custom-call | flops 2147483648 | bytes 2000000 | tf_op jit(solution)/shard_map/scatter_rows/pallas_call | solution.py:273
  112.7 0.5 collective-permute-done.14
  113.2 0.1 add_convert_fusion.glob0
  113.3 0.0 copy-start.8
  113.3 0.0 copy-start.9
  113.3 4.3 %collective-permute-start.19 = (bf16[128,512]{1,0:T(8,128)(2,1)S(1)}, bf16[128,512]{1,0:T(8,128)(2,1)S(1)}, u32[]{:S(2)}, u32[]{:S(2)}) collective-permute-start(bf16[128,512]{1,0:T(8,128)(2,1)S(1)} %add_convert_fusion.glob0), channel_id=1, source_target_pairs={{0,24},{8,0},{16,8},{24,16},{32,56},{40,32},{48,40},{56,48},{64,88... | collective-permute-start | bytes 393224 | tf_op jit(solution)/shard_map/ppermute | solution.py:750
  117.6 0.9 collective-permute-start.17
  118.5 4.0 %scatter_rows.3 = f32[4,1024,128]{2,1,0:T(8,128)} custom-call(s32[128,128]{1,0:T(8,128)S(1)} %bitcast.37, bf16[4096,128]{1,0:T(8,128)(2,1)S(1)} %bitcast.31, f32[4,1024,128]{2,1,0:T(8,128)} %scatter_rows.2.refs_0_), custom_call_target="tpu_custom_call", output_to_operand_aliasing={{}: (2, {})} | custom-call | flops 2147483648 | bytes 2000000 | tf_op jit(solution)/shard_map/scatter_rows/pallas_call | solution.py:273
  122.5 0.8 collective-permute-done.19.glob3
  123.3 2.2 %collective-permute-done.18.glob2 = bf16[128,512]{1,0:T(8,128)(2,1)S(1)} collective-permute-done((bf16[128,512]{1,0:T(8,128)(2,1)S(1)}, bf16[128,512]{1,0:T(8,128)(2,1)S(1)}, u32[]{:S(2)}, u32[]{:S(2)}) %collective-permute-start.18) | collective-permute-done | bytes 131104 | tf_op jit(solution)/shard_map/ppermute | solution.py:750
  125.5 1.3 collective-permute-done.17.glob1
  126.8 1.7 %add_received.1 = (bf16[512,512]{1,0:T(8,128)(2,1)}, bf16[512,512]{1,0:T(8,128)(2,1)}) custom-call(s32[1,2]{1,0:T(1,128)S(1)} %copy-done.13, bf16[512,512]{1,0:T(8,128)(2,1)S(1)} %copy-done.8, bf16[512,512]{1,0:T(8,128)(2,1)S(1)} %copy-done.9, bf16[2,128,512]{2,1,0:T(8,128)(2,1)S(1)} %collective-permute-done.13.edge, ...), custom_call_target="tpu_custom_call" | custom-call | flops 1000000 | bytes 3000000 | tf_op jit(solution)/shard_map/add_received/pallas_call | solution.py:727
  (27 shorter events, 0.1 us)
Async XLA Ops:
  0.6 0.7 copy-start.12
  3.6 8.2 %collective-permute-start = (bf16[128,512]{1,0:T(8,128)(2,1)S(1)}, bf16[128,512]{1,0:T(8,128)(2,1)S(1)}, u32[]{:S(2)}, u32[]{:S(2)}) collective-permute-start(bf16[128,512]{1,0:T(8,128)(2,1)S(1)} %get-tuple-element.71), channel_id=1, source_target_pairs={{0,8},{8,16},{16,24},{24,0},{32,40},{40,48},{48,56},{56,32},{64,72... | collective-permute-start | bytes 393224 | tf_op jit(solution)/shard_map/ppermute | solution.py:750
  5.1 8.7 %collective-permute-start.1 = (bf16[128,512]{1,0:T(8,128)(2,1)S(1)}, bf16[128,512]{1,0:T(8,128)(2,1)S(1)}, u32[]{:S(2)}, u32[]{:S(2)}) collective-permute-start(bf16[128,512]{1,0:T(8,128)(2,1)S(1)} %get-tuple-element.72), channel_id=1, source_target_pairs={{0,16},{8,24},{16,0},{24,8},{32,48},{40,56},{48,32},{56,40},{64,80... | collective-permute-start | bytes 393224 | tf_op jit(solution)/shard_map/ppermute | solution.py:750
  8.0 5.9 %collective-permute-start.2 = (bf16[128,512]{1,0:T(8,128)(2,1)S(1)}, bf16[128,512]{1,0:T(8,128)(2,1)S(1)}, u32[]{:S(2)}, u32[]{:S(2)}) collective-permute-start(bf16[128,512]{1,0:T(8,128)(2,1)S(1)} %get-tuple-element.73), channel_id=1, source_target_pairs={{0,24},{8,0},{16,8},{24,16},{32,56},{40,32},{48,40},{56,48},{64,88... | collective-permute-start | bytes 393224 | tf_op jit(solution)/shard_map/ppermute | solution.py:750
  13.9 16.6 %collective-permute-start.5 = (bf16[128,512]{1,0:T(8,128)(2,1)S(1)}, bf16[128,512]{1,0:T(8,128)(2,1)S(1)}, u32[]{:S(2)}, u32[]{:S(2)}) collective-permute-start(bf16[128,512]{1,0:T(8,128)(2,1)S(1)} %add_convert_fusion.3), channel_id=1, source_target_pairs={{0,96},{8,104},{16,112},{24,120},{32,0},{40,8},{48,16},{56,24},{64... | collective-permute-start | bytes 393224 | tf_op jit(solution)/shard_map/ppermute | solution.py:754
  14.1 16.5 %collective-permute-start.4 = (bf16[128,512]{1,0:T(8,128)(2,1)S(1)}, bf16[128,512]{1,0:T(8,128)(2,1)S(1)}, u32[]{:S(2)}, u32[]{:S(2)}) collective-permute-start(bf16[128,512]{1,0:T(8,128)(2,1)S(1)} %add_convert_fusion.3), channel_id=1, source_target_pairs={{0,64},{8,72},{16,80},{24,88},{32,96},{40,104},{48,112},{56,120},{... | collective-permute-start | bytes 393224 | tf_op jit(solution)/shard_map/ppermute | solution.py:754
  17.4 13.2 %collective-permute-start.3 = (bf16[128,512]{1,0:T(8,128)(2,1)S(1)}, bf16[128,512]{1,0:T(8,128)(2,1)S(1)}, u32[]{:S(2)}, u32[]{:S(2)}) collective-permute-start(bf16[128,512]{1,0:T(8,128)(2,1)S(1)} %add_convert_fusion.3), channel_id=1, source_target_pairs={{0,32},{8,40},{16,48},{24,56},{32,64},{40,72},{48,80},{56,88},{64,... | collective-permute-start | bytes 393224 | tf_op jit(solution)/shard_map/ppermute | solution.py:754
  19.6 26.5 %collective-permute-start.6 = (bf16[2,128,512]{2,1,0:T(8,128)(2,1)}, bf16[2,128,512]{2,1,0:T(8,128)(2,1)S(1)}, u32[]{:S(2)}, u32[]{:S(2)}) collective-permute-start(bf16[2,128,512]{2,1,0:T(8,128)(2,1)} %get-tuple-element.82), channel_id=1, source_target_pairs={{0,8},{8,16},{16,24},{24,32},{32,40},{40,48},{48,56},{56,64},{64,7... | collective-permute-start | bytes 786440 | tf_op jit(solution)/shard_map/ppermute | solution.py:741
  22.9 16.7 %all-to-all-start = ((s32[128,1,128]{2,1,0:T(1,128)}), s32[128,1,128]{2,1,0:T(1,128)S(1)}, u32[]{:S(2)}, u32[]{:S(2)}) async-start(s32[128,1,128]{2,1,0:T(1,128)} %bitcast.40), calls=%async_computation | async-start | bytes 131072 | tf_op jit(solution)/shard_map/all_to_all | solution.py:745
  30.7 15.5 %collective-permute-start.9 = (bf16[128,512]{1,0:T(8,128)(2,1)S(1)}, bf16[128,512]{1,0:T(8,128)(2,1)S(1)}, u32[]{:S(2)}, u32[]{:S(2)}) collective-permute-start(bf16[128,512]{1,0:T(8,128)(2,1)S(1)} %add_convert_fusion.2.glob0), channel_id=1, source_target_pairs={{0,24},{8,0},{16,8},{24,16},{32,56},{40,32},{48,40},{56,48},{64,88... | collective-permute-start | bytes 393224 | tf_op jit(solution)/shard_map/ppermute | solution.py:750
  33.5 12.7 %collective-permute-start.8 = (bf16[128,512]{1,0:T(8,128)(2,1)S(1)}, bf16[128,512]{1,0:T(8,128)(2,1)S(1)}, u32[]{:S(2)}, u32[]{:S(2)}) collective-permute-start(bf16[128,512]{1,0:T(8,128)(2,1)S(1)} %add_convert_fusion.2.glob0), channel_id=1, source_target_pairs={{0,16},{8,24},{16,0},{24,8},{32,48},{40,56},{48,32},{56,40},{64,80... | collective-permute-start | bytes 393224 | tf_op jit(solution)/shard_map/ppermute | solution.py:750
  34.3 11.9 %collective-permute-start.7 = (bf16[128,512]{1,0:T(8,128)(2,1)S(1)}, bf16[128,512]{1,0:T(8,128)(2,1)S(1)}, u32[]{:S(2)}, u32[]{:S(2)}) collective-permute-start(bf16[128,512]{1,0:T(8,128)(2,1)S(1)} %add_convert_fusion.2.glob0), channel_id=1, source_target_pairs={{0,8},{8,16},{16,24},{24,0},{32,40},{40,48},{48,56},{56,32},{64,72... | collective-permute-start | bytes 393224 | tf_op jit(solution)/shard_map/ppermute | solution.py:750
  39.6 12.7 %copy-start.14 = (s32[8]{0:T(128)S(1)}, s32[8]{0:T(128)}, u32[]{:S(2)}) copy-start(s32[8]{0:T(128)} %lengths.5) | copy-start | bytes 100
  46.1 6.2 %copy-start = (bf16[1,512,512]{2,1,0:T(8,128)(2,1)S(1)}, bf16[1,512,512]{2,1,0:T(8,128)(2,1)}, u32[]{:S(2)}) copy-start(bf16[1,512,512]{2,1,0:T(8,128)(2,1)} %param.11) | copy-start | bytes 1572868
  46.1 6.2 %copy-start.4 = (bf16[1,512,512]{2,1,0:T(8,128)(2,1)S(1)}, bf16[1,512,512]{2,1,0:T(8,128)(2,1)}, u32[]{:S(2)}) copy-start(bf16[1,512,512]{2,1,0:T(8,128)(2,1)} %param.12) | copy-start | bytes 1572868
  46.1 6.2 %copy-start.5 = (bf16[1,512,512]{2,1,0:T(8,128)(2,1)S(1)}, bf16[1,512,512]{2,1,0:T(8,128)(2,1)}, u32[]{:S(2)}) copy-start(bf16[1,512,512]{2,1,0:T(8,128)(2,1)} %param.13) | copy-start | bytes 1572868
  46.1 10.7 %copy-start.7 = (bf16[1,512,512]{2,1,0:T(8,128)(2,1)S(1)}, bf16[1,512,512]{2,1,0:T(8,128)(2,1)}, u32[]{:S(2)}) copy-start(bf16[1,512,512]{2,1,0:T(8,128)(2,1)} %param.14) | copy-start | bytes 1572868
  46.1 10.7 %copy-start.10 = (bf16[1,512,128]{2,1,0:T(8,128)(2,1)S(1)}, bf16[1,512,128]{2,1,0:T(8,128)(2,1)}, u32[]{:S(2)}) copy-start(bf16[1,512,128]{2,1,0:T(8,128)(2,1)} %param.15) | copy-start | bytes 393220
  46.1 10.7 %copy-start.11 = (bf16[512,128]{1,0:T(8,128)(2,1)S(1)}, bf16[512,128]{1,0:T(8,128)(2,1)}, u32[]{:S(2)}) copy-start(bf16[512,128]{1,0:T(8,128)(2,1)} %w_out.3) | copy-start | bytes 393220
  46.1 10.7 %copy-start.13 = (s32[1,2]{1,0:T(1,128)S(1)}, s32[1,2]{1,0:T(1,128)}, u32[]{:S(2)}) copy-start(s32[1,2]{1,0:T(1,128)} %gids.5) | copy-start | bytes 28
  46.2 24.6 %all-to-all-start.1 = ((bf16[128,32,128]{2,1,0:T(8,128)(2,1)}), bf16[128,32,128]{2,1,0:T(8,128)(2,1)}, u32[]{:S(2)}, u32[]{:S(2)}) async-start(bf16[128,32,128]{2,1,0:T(8,128)(2,1)} %bitcast.39), calls=%async_computation.1 | async-start | bytes 2097152 | tf_op jit(solution)/shard_map/all_to_all | solution.py:745
  78.2 25.2 %all-to-all-start.2 = ((bf16[128,32,128]{2,1,0:T(8,128)(2,1)}), bf16[128,32,128]{2,1,0:T(8,128)(2,1)S(1)}, u32[]{:S(2)}, u32[]{:S(2)}) async-start(bf16[128,32,128]{2,1,0:T(8,128)(2,1)} %bitcast.38), calls=%async_computation.2 | async-start | bytes 2097152 | tf_op jit(solution)/shard_map/all_to_all | solution.py:745
  83.1 11.3 %copy-start.1 = (bf16[1,512,512]{2,1,0:T(8,128)(2,1)S(1)}, bf16[1,512,512]{2,1,0:T(8,128)(2,1)}, u32[]{:S(2)}) copy-start(bf16[1,512,512]{2,1,0:T(8,128)(2,1)} %param.11) | copy-start | bytes 1572868
  83.2 11.3 %copy-start.2 = (bf16[8,512,256]{2,1,0:T(8,128)(2,1)S(1)}, bf16[8,512,256]{2,1,0:T(8,128)(2,1)}, u32[]{:S(2)}) copy-start(bf16[8,512,256]{2,1,0:T(8,128)(2,1)} %get-tuple-element.95.probs) | copy-start | bytes 6291460
  83.2 11.3 %copy-start.3 = (bf16[8,512,256]{2,1,0:T(8,128)(2,1)S(1)}, bf16[8,512,256]{2,1,0:T(8,128)(2,1)}, u32[]{:S(2)}) copy-start(bf16[8,512,256]{2,1,0:T(8,128)(2,1)} %get-tuple-element.96.slope) | copy-start | bytes 6291460
  83.2 11.3 %copy-start.6 = (bf16[512,512]{1,0:T(8,128)(2,1)S(1)}, bf16[512,512]{1,0:T(8,128)(2,1)}, u32[]{:S(2)}) copy-start(bf16[512,512]{1,0:T(8,128)(2,1)} %get-tuple-element.94.grad) | copy-start | bytes 1572868
  88.7 11.9 %collective-permute-start.10 = (bf16[128,512]{1,0:T(8,128)(2,1)S(1)}, bf16[128,512]{1,0:T(8,128)(2,1)S(1)}, u32[]{:S(2)}, u32[]{:S(2)}) collective-permute-start(bf16[128,512]{1,0:T(8,128)(2,1)S(1)} %get-tuple-element.103), channel_id=1, source_target_pairs={{0,8},{8,16},{16,24},{24,0},{32,40},{40,48},{48,56},{56,32},{64,72... | collective-permute-start | bytes 393224 | tf_op jit(solution)/shard_map/ppermute | solution.py:750
  90.3 13.1 %collective-permute-start.11 = (bf16[128,512]{1,0:T(8,128)(2,1)S(1)}, bf16[128,512]{1,0:T(8,128)(2,1)S(1)}, u32[]{:S(2)}, u32[]{:S(2)}) collective-permute-start(bf16[128,512]{1,0:T(8,128)(2,1)S(1)} %get-tuple-element.104), channel_id=1, source_target_pairs={{0,16},{8,24},{16,0},{24,8},{32,48},{40,56},{48,32},{56,40},{64,80... | collective-permute-start | bytes 393224 | tf_op jit(solution)/shard_map/ppermute | solution.py:750
  93.0 10.4 %collective-permute-start.12 = (bf16[128,512]{1,0:T(8,128)(2,1)S(1)}, bf16[128,512]{1,0:T(8,128)(2,1)S(1)}, u32[]{:S(2)}, u32[]{:S(2)}) collective-permute-start(bf16[128,512]{1,0:T(8,128)(2,1)S(1)} %get-tuple-element.105), channel_id=1, source_target_pairs={{0,24},{8,0},{16,8},{24,16},{32,56},{40,32},{48,40},{56,48},{64,88... | collective-permute-start | bytes 393224 | tf_op jit(solution)/shard_map/ppermute | solution.py:750
  98.7 28.1 %collective-permute-start.13 = (bf16[2,128,512]{2,1,0:T(8,128)(2,1)S(1)}, bf16[2,128,512]{2,1,0:T(8,128)(2,1)S(1)}, u32[]{:S(2)}, u32[]{:S(2)}) collective-permute-start(bf16[2,128,512]{2,1,0:T(8,128)(2,1)S(1)} %get-tuple-element.108), channel_id=1, source_target_pairs={{8,0},{16,8},{24,16},{32,24},{40,32},{48,40},{56,48},{64,56},{72,6... | collective-permute-start | bytes 786440 | tf_op jit(solution)/shard_map/ppermute | solution.py:741
  103.4 9.3 %collective-permute-start.16 = (bf16[128,512]{1,0:T(8,128)(2,1)S(1)}, bf16[128,512]{1,0:T(8,128)(2,1)S(1)}, u32[]{:S(2)}, u32[]{:S(2)}) collective-permute-start(bf16[128,512]{1,0:T(8,128)(2,1)S(1)} %add_convert_fusion.1), channel_id=1, source_target_pairs={{0,96},{8,104},{16,112},{24,120},{32,0},{40,8},{48,16},{56,24},{64... | collective-permute-start | bytes 393224 | tf_op jit(solution)/shard_map/ppermute | solution.py:754
  103.8 9.0 %collective-permute-start.15 = (bf16[128,512]{1,0:T(8,128)(2,1)S(1)}, bf16[128,512]{1,0:T(8,128)(2,1)S(1)}, u32[]{:S(2)}, u32[]{:S(2)}) collective-permute-start(bf16[128,512]{1,0:T(8,128)(2,1)S(1)} %add_convert_fusion.1), channel_id=1, source_target_pairs={{0,64},{8,72},{16,80},{24,88},{32,96},{40,104},{48,112},{56,120},{... | collective-permute-start | bytes 393224 | tf_op jit(solution)/shard_map/ppermute | solution.py:754
  106.7 6.5 %collective-permute-start.14 = (bf16[128,512]{1,0:T(8,128)(2,1)S(1)}, bf16[128,512]{1,0:T(8,128)(2,1)S(1)}, u32[]{:S(2)}, u32[]{:S(2)}) collective-permute-start(bf16[128,512]{1,0:T(8,128)(2,1)S(1)} %add_convert_fusion.1), channel_id=1, source_target_pairs={{0,32},{8,40},{16,48},{24,56},{32,64},{40,72},{48,80},{56,88},{64,... | collective-permute-start | bytes 393224 | tf_op jit(solution)/shard_map/ppermute | solution.py:754
  113.3 13.5 %copy-start.8 = (bf16[512,512]{1,0:T(8,128)(2,1)S(1)}, bf16[512,512]{1,0:T(8,128)(2,1)}, u32[]{:S(2)}) copy-start(bf16[512,512]{1,0:T(8,128)(2,1)} %get-tuple-element.106.d_k) | copy-start | bytes 1572868
  113.3 13.5 %copy-start.9 = (bf16[512,512]{1,0:T(8,128)(2,1)S(1)}, bf16[512,512]{1,0:T(8,128)(2,1)}, u32[]{:S(2)}) copy-start(bf16[512,512]{1,0:T(8,128)(2,1)} %get-tuple-element.107.d_v) | copy-start | bytes 1572868
  113.3 10.0 %collective-permute-start.19 = (bf16[128,512]{1,0:T(8,128)(2,1)S(1)}, bf16[128,512]{1,0:T(8,128)(2,1)S(1)}, u32[]{:S(2)}, u32[]{:S(2)}) collective-permute-start(bf16[128,512]{1,0:T(8,128)(2,1)S(1)} %add_convert_fusion.glob0), channel_id=1, source_target_pairs={{0,24},{8,0},{16,8},{24,16},{32,56},{40,32},{48,40},{56,48},{64,88... | collective-permute-start | bytes 393224 | tf_op jit(solution)/shard_map/ppermute | solution.py:750
  117.6 7.9 %collective-permute-start.18 = (bf16[128,512]{1,0:T(8,128)(2,1)S(1)}, bf16[128,512]{1,0:T(8,128)(2,1)S(1)}, u32[]{:S(2)}, u32[]{:S(2)}) collective-permute-start(bf16[128,512]{1,0:T(8,128)(2,1)S(1)} %add_convert_fusion.glob0), channel_id=1, source_target_pairs={{0,16},{8,24},{16,0},{24,8},{32,48},{40,56},{48,32},{56,40},{64,80... | collective-permute-start | bytes 393224 | tf_op jit(solution)/shard_map/ppermute | solution.py:750
  117.6 9.2 %collective-permute-start.17 = (bf16[128,512]{1,0:T(8,128)(2,1)S(1)}, bf16[128,512]{1,0:T(8,128)(2,1)S(1)}, u32[]{:S(2)}, u32[]{:S(2)}) collective-permute-start(bf16[128,512]{1,0:T(8,128)(2,1)S(1)} %add_convert_fusion.glob0), channel_id=1, source_target_pairs={{0,8},{8,16},{16,24},{24,0},{32,40},{40,48},{48,56},{56,32},{64,72... | collective-permute-start | bytes 393224 | tf_op jit(solution)/shard_map/ppermute | solution.py:750

commit v2 on v1

--- a/solution.py
+++ b/solution.py
@@ -128,7 +128,7 @@
         compiler_params=params(),
         cost_estimate=pl.CostEstimate(flops=10**6, bytes_accessed=2 * 10**6, transcendentals=0),
         name="pieces",
-    )(gids, *in_hbm(key, value))
+    )(*in_hbm(gids, key, value))
 
 
 def route_kernel(owner, row, req, code):
@@ -140,7 +140,7 @@
     before = jnp.where(iota((EVENTS, EVENTS), 0) < iota((EVENTS, EVENTS), 1), 1.0, 0.0).astype(BF)
     rank = dot(jnp.where(hit, 1.0, 0.0).astype(BF), before)
     rank = jnp.where(hit, rank, -1.0)
-    code[...] = jnp.where(owner[0] == dev, rank + FIRST, rank)
+    code[...] = jnp.where(owner[0] == dev, rank + FIRST, rank).astype(BF)
     plus = (rows + 1).astype(F32)
     lane = iota((NDEV, E), 1) - (lax.axis_index("user") % (E // SLOTS)) * SLOTS
     asked = jnp.zeros((NDEV, E), F32)
@@ -155,7 +155,7 @@
         route_kernel,
         out_shape=(
             slow((NDEV, E), jnp.int32),
-            slow((NDEV, EVENTS), F32),
+            slow((NDEV, EVENTS), BF),
         ),
         in_specs=[VMEM_SPEC] * 2,
         out_specs=[VMEM_SPEC] * 2,
@@ -184,7 +184,7 @@
     )
 
 
-def gather_kernel(asked, table_far, found_far, table, found, sems):
+def gather_kernel(asked, table_far, found_far, kept, table, found, sems):
     slabs = [slice(h * LO, (h + 1) * LO) for h in range(HI)]
     loads = [
         pltpu.make_async_copy(table_far.at[slab, :], table.at[slab, :], sems.at[h])
@@ -192,6 +192,8 @@
     ]
     for load in loads:
         load.start()
+    keep = pltpu.make_async_copy(asked, kept, sems.at[HI + 4])
+    keep.start()
     columns = slot_columns(slot_rows(asked, NDEV // 4))
     lo = columns & (LO - 1)
     hi = columns >> (LO.bit_length() - 1)
@@ -220,25 +222,26 @@
         sends[-1].start()
     for send in sends:
         send.wait()
+    keep.wait()
 
 
 def gather(asked, table):
     return pl.pallas_call(
         gather_kernel,
-        out_shape=slow((NDEV * SLOTS, E), BF),
+        out_shape=(slow((NDEV * SLOTS, E), BF), slow((NDEV, E), jnp.int32)),
         in_specs=[VMEM_SPEC, ANY_SPEC],
-        out_specs=ANY_SPEC,
+        out_specs=[ANY_SPEC] * 2,
         scratch_shapes=[
             pltpu.VMEM((ROWS, E), BF),
             pltpu.VMEM((NDEV * SLOTS, E), BF),
-            pltpu.SemaphoreType.DMA((HI + 4,)),
+            pltpu.SemaphoreType.DMA((HI + 5,)),
         ],
         compiler_params=params(),
         cost_estimate=pl.CostEstimate(
             flops=2 * NDEV * SLOTS * ROWS * E, bytes_accessed=2 * 10**6, transcendentals=0
         ),
         name="gather_rows",
-    )(asked, *in_hbm(table))
+    )(*in_vmem(asked), *in_hbm(table))
 
 
 HALVES = 2
@@ -396,7 +399,7 @@
             normed_out[rows, :] = normed
             inv_out[rows, :] = inv
             gated = (normed * gate[rows, :].astype(F32)).astype(BF)
-            user[rows, :] = dot(gated, w_out[...]) + history[rows, :].astype(F32)
+            user[rows, :] = (dot(gated, w_out[...]) + history[rows, :].astype(F32)).astype(BF)
 
 
 def pair_block(rows):
@@ -426,7 +429,7 @@
             flops=5 * 10**8, bytes_accessed=7 * 10**6, transcendentals=10**6
         ),
         name="near_forward",
-    )(lengths, q, k, v, halo)
+    )(*in_hbm(lengths), q, k, v, halo)
 
 
 def far_forward(lengths, gids, q, glob, near, gate, history, w_out):
@@ -438,7 +441,7 @@
             SQUARE,
             slow((EVENTS, D), F32),
             slow((EVENTS, 1), F32),
-            slow((EVENTS, E), F32),
+            slow((EVENTS, E), BF),
         ),
         in_specs=[SMEM_SPEC] * 2
         + [pair_block(EVENTS)]
@@ -461,7 +464,7 @@
             flops=6 * 10**8, bytes_accessed=9 * 10**6, transcendentals=10**6
         ),
         name="far_forward",
-    )(lengths, gids, q, *glob, *in_vmem(near), gate, history, w_out)
+    )(*in_hbm(lengths, gids), q, *glob, *in_vmem(near), *in_hbm(gate, history, w_out))
 
 
 def far_backward_kernel(
@@ -579,49 +582,51 @@
 
 def middle_kernel(
     lengths,
+    items,
     code,
     user,
-    inv,
-    w_out,
-    items_far,
     normed_far,
     gate_far,
+    inv_far,
+    w_far,
     out_far,
     attn_far,
     gated_far,
     score,
-    items,
     normed,
     gate,
+    inv,
+    w_out,
     outgoing,
     d_attn,
     d_gate,
     sems,
 ):
-    parts = 4
-    portion = NDEV * SLOTS // parts
-    slices = [slice(i * portion, (i + 1) * portion) for i in range(parts)]
-    item_loads = [
-        pltpu.make_async_copy(items_far.at[rows, :], items.at[rows, :], sems.at[3 + i])
-        for i, rows in enumerate(slices)
-    ]
     loads = [
         pltpu.make_async_copy(normed_far, normed, sems.at[0]),
         pltpu.make_async_copy(gate_far, gate, sems.at[1]),
+        pltpu.make_async_copy(inv_far, inv, sems.at[2]),
+        pltpu.make_async_copy(w_far, w_out, sems.at[3]),
     ]
-    for load in item_loads + loads:
+    for load in loads:
         load.start()
-    send = pltpu.make_async_copy(outgoing, out_far, sems.at[2])
-    user_b = user[...].astype(BF)
-    user_t = user[...].T.astype(BF)
-    first = code[...] >= FIRST
-    rank = jnp.where(first, code[...] - FIRST, code[...])
+    sends = []
+
+    def send(near, far, rows):
+        copy = pltpu.make_async_copy(near.at[rows, :], far.at[rows, :], sems.at[4 + len(sends)])
+        copy.start()
+        sends.append(copy)
+
+    portion = NDEV * SLOTS // 4
+    user_b = user[...]
+    user_t = user_b.T
+    mark = code[...].astype(F32)
+    first = mark >= FIRST
+    rank = jnp.where(first, mark - FIRST, mark)
     group = 8
     size = group * SLOTS
     slot = iota((SLOTS, EVENTS), 0).astype(F32)
     for d in range(0, NDEV, group):
-        if d * SLOTS % portion == 0:
-            item_loads[d * SLOTS // portion].wait()
         s = dot(items[d * SLOTS : d * SLOTS + size, :], user_t)
         for r in range(group):
             own = rank[d + r : d + r + 1, :] == slot
@@ -645,8 +650,8 @@
         rows = slice(d * SLOTS, d * SLOTS + size)
         outgoing[rows, :] = dot(c, user_b).astype(BF)
         d_user_t = d_user_t + dot_tn(items[rows, :], c)
-    send.start()
-    sends = [send]
+        if rows.stop % portion == 0:
+            send(outgoing, out_far, slice(rows.stop - portion, rows.stop))
     d_user = d_user_t.T.astype(BF)
     for load in loads:
         load.wait()
@@ -665,14 +670,10 @@
             )
             * inv[rows, :]
         ).astype(BF)
-        for i, (near, far) in enumerate(((d_attn, attn_far), (d_gate, gated_far))):
-            copy = pltpu.make_async_copy(
-                near.at[rows, :], far.at[rows, :], sems.at[3 + parts + 2 * (r // step) + i]
-            )
-            copy.start()
-            sends.append(copy)
-    for send in sends:
-        send.wait()
+        send(d_attn, attn_far, rows)
+        send(d_gate, gated_far, rows)
+    for copy in sends:
+        copy.wait()
 
 
 def middle(lengths, items, code, user, normed, inv, gate, w_out):
@@ -683,24 +684,25 @@
             slow((EVENTS, D), BF),
             slow((EVENTS, D), BF),
         ),
-        in_specs=[SMEM_SPEC] + [VMEM_SPEC] * 4 + [ANY_SPEC] * 3,
+        in_specs=[SMEM_SPEC] + [VMEM_SPEC] * 3 + [ANY_SPEC] * 4,
         out_specs=[ANY_SPEC] * 3,
         scratch_shapes=[
             pltpu.VMEM((NDEV, EVENTS), F32),
-            pltpu.VMEM((NDEV * SLOTS, E), BF),
             pltpu.VMEM((EVENTS, D), F32),
             pltpu.VMEM((EVENTS, D), BF),
+            pltpu.VMEM((EVENTS, 1), F32),
+            pltpu.VMEM((D, E), BF),
             pltpu.VMEM((NDEV * SLOTS, E), BF),
             pltpu.VMEM((EVENTS, D), BF),
             pltpu.VMEM((EVENTS, D), BF),
-            pltpu.SemaphoreType.DMA((3 + 4 + 2 * EVENTS // 128,)),
+            pltpu.SemaphoreType.DMA((4 + 4 + 2 * EVENTS // 128,)),
         ],
         compiler_params=params(),
         cost_estimate=pl.CostEstimate(
             flops=2 * 10**9, bytes_accessed=6 * 10**6, transcendentals=10**5
         ),
         name="ranking",
-    )(lengths, *in_hbm(code, user, inv, w_out, items, normed, gate))
+    )(*in_hbm(lengths), *in_vmem(items), *in_hbm(code, user, normed, gate, inv, w_out))
 
 
 def finish_kernel(gids, d_k, d_v, edge, glob0, glob1, glob2, glob3, key_out, value_out):
@@ -732,7 +734,7 @@
         compiler_params=params(),
         cost_estimate=pl.CostEstimate(flops=10**6, bytes_accessed=3 * 10**6, transcendentals=0),
         name="add_received",
-    )(gids, d_k, d_v, edge, *total)
+    )(*in_hbm(gids), d_k, d_v, edge, *total)
 
 
 def from_behind(block, axis, distance):
@@ -784,17 +786,18 @@
     parts = from_x(cand)
     owner, _ = together(owner, cand[0])
     req, code = route(owner, row)
+    tail, _ = together(tail, req)
+    halo = from_behind(tail, "seq", 1)
     req, *parts = together(req, *parts)
     mine = add_all(parts)
-    req, mine = together(req, mine)
     parts = from_z(mine)
+    req, halo, _ = together(req, halo, mine)
     asked = exchange(req.reshape(NDEV, 1, E), ("seq", "user")).reshape(NDEV, E)
     mine = add_all(parts)
     glob = share_x(mine)
-    halo = from_behind(tail, "seq", 1)
     asked, _ = together(asked, mine)
-    found = gather(asked, table)
-    found, halo, *glob = together(found, halo, *glob)
+    found, asked = gather(asked, table)
+    found, *glob = together(found, *glob)
     items = exchange(found.reshape(NDEV, SLOTS, E), ("seq", "user")).reshape(NDEV * SLOTS, E)
     near_p, near_f, near = near_forward(lengths, q, k, v, halo)
     far_p, far_f, normed, inv, user = far_forward(

time: 129 us -> 126 us (0.977)
  starting transfers between devices: 56 us -> 54.6 us
    ppermute x2, waiting for transfers between devices: 0.01 us -> 3.01 us  [from_behind(): return lax.ppermute(block, axis, route_pairs)]
    ppermute x12, waiting for transfers between devices: 9.06 us -> 7.01 us  [around_x(): return lax.ppermute(x, 'seq', pairs)]
    pallas_call x1, Pallas kernels: 7.47 us -> 6.13 us  [middle(): pl.pallas_call(middle_kernel, out_shape=(slow((NDEV * SLOTS, E), BF), slo...]
  transfers between devices with their start and end apart: 23 -> 23, of which waited for: 8 -> 8; matrix products, arithmetic and copies ran while one was open for 0% -> 0% of each run, Pallas kernels for 29% -> 30%
where the time goes in v2:
time: 126 us
  starting transfers between devices  54.6 us (43%)
  Pallas kernels  47.4 us (38%)
  waiting for transfers between devices  22.6 us (18%)
    ppermute x12, starting transfers between devices, around_x(): return lax.ppermute(x, 'seq', pairs)  21.1 us
    all_to_all x3, starting transfers between devices, exchange(): return lax.all_to_all(x, axis, split_axis=0, concat_axis=0, tiled=True)  18.1 us
    all_to_all x3, waiting for transfers between devices, exchange(): return lax.all_to_all(x, axis, split_axis=0, concat_axis=0, tiled=True)  12.1 us
    ppermute x6, starting transfers between devices, around_z(): lax.ppermute(x, 'seq', [(i, (i + distance * XSIZE) % NSEQ) for i in range...  11 us
    pallas_call x2, Pallas kernels, scatter(): pl.pallas_call(functools.partial(scatter_kernel, half), grid=(1,), out_sh...  7.96 us
    ppermute x12, waiting for transfers between devices, around_x(): return lax.ppermute(x, 'seq', pairs)  7.01 us
    pallas_call x1, Pallas kernels, gather(): pl.pallas_call(gather_kernel, out_shape=(slow((NDEV * SLOTS, E), BF), slo...  6.49 us
    pallas_call x1, Pallas kernels, far_forward(): pl.pallas_call(far_forward_kernel, grid=(PAIRS,), out_shape=(SQUARE, SQUA...  6.47 us
  transfers between devices with their start and end apart: 23, of which 8 were waited for; matrix products, arithmetic and copies ran while one was open for 0% of the time, Pallas kernels for 30%

profile of v2, /device:TPU:32, one launch (start us, length us, event | category | flops | bytes accessed | tf_op | source)
XLA Modules:
  0.0 126.0 jit_solution(14533140235621249421)
XLA Ops:
  0.6 1.7 %pieces.1 = (bf16[2,128,512]{2,1,0:T(8,128)(2,1)S(1)}, bf16[128,512]{1,0:T(8,128)(2,1)S(1)}, bf16[128,512]{1,0:T(8,128)(2,1)S(1)}, bf16[128,512]{1,0:T(8,128)(2,1)S(1)}, bf16[128,512]{1,0:T(8,128)(2,1)S(1)}) custom-call(s32[1,2]{1,0:T(1,128)} %gids.5, bf16[512,512]{1,0:T(8,128)(2,1)} %bitcast.24, bf16[512,512]{1,0:T(8,128)(2,1)} %bitcast.27), custom_call_target="tpu_custom_call" | custom-call | flops 1000000 | bytes 2000000 | tf_op jit(solution)/shard_map/pieces/pallas_call | solution.py:121
  2.3 1.6 %collective-permute-start = (bf16[128,512]{1,0:T(8,128)(2,1)S(1)}, bf16[128,512]{1,0:T(8,128)(2,1)S(1)}, u32[]{:S(2)}, u32[]{:S(2)}) collective-permute-start(bf16[128,512]{1,0:T(8,128)(2,1)S(1)} %get-tuple-element.73), channel_id=1, source_target_pairs={{0,8},{8,16},{16,24},{24,0},{32,40},{40,48},{48,56},{56,32},{64,72... | collective-permute-start | bytes 393224 | tf_op jit(solution)/shard_map/ppermute | solution.py:752
  3.9 2.7 %collective-permute-start.1 = (bf16[128,512]{1,0:T(8,128)(2,1)S(1)}, bf16[128,512]{1,0:T(8,128)(2,1)S(1)}, u32[]{:S(2)}, u32[]{:S(2)}) collective-permute-start(bf16[128,512]{1,0:T(8,128)(2,1)S(1)} %get-tuple-element.74), channel_id=1, source_target_pairs={{0,16},{8,24},{16,0},{24,8},{32,48},{40,56},{48,32},{56,40},{64,80... | collective-permute-start | bytes 393224 | tf_op jit(solution)/shard_map/ppermute | solution.py:752
  6.6 1.4 %collective-permute-start.2 = (bf16[128,512]{1,0:T(8,128)(2,1)S(1)}, bf16[128,512]{1,0:T(8,128)(2,1)S(1)}, u32[]{:S(2)}, u32[]{:S(2)}) collective-permute-start(bf16[128,512]{1,0:T(8,128)(2,1)S(1)} %get-tuple-element.75), channel_id=1, source_target_pairs={{0,24},{8,0},{16,8},{24,16},{32,56},{40,32},{48,40},{56,48},{64,88... | collective-permute-start | bytes 393224 | tf_op jit(solution)/shard_map/ppermute | solution.py:752
  8.1 2.5 %route.1 = (s32[128,128]{1,0:T(8,128)}, bf16[128,512]{1,0:T(8,128)(2,1)}) custom-call(s32[5,1,512]{2,1,0:T(1,128)} %bitcast.43, s32[5,1,512]{2,1,0:T(1,128)} %bitcast.44), custom_call_target="tpu_custom_call" | custom-call | flops 100000000 | bytes 1000000 | tf_op jit(solution)/shard_map/route/pallas_call | solution.py:154
  10.6 2.5 %collective-permute-start.3 = (bf16[2,128,512]{2,1,0:T(8,128)(2,1)S(1)}, bf16[2,128,512]{2,1,0:T(8,128)(2,1)S(1)}, u32[]{:S(2)}, u32[]{:S(2)}) collective-permute-start(bf16[2,128,512]{2,1,0:T(8,128)(2,1)S(1)} %get-tuple-element.78), channel_id=1, source_target_pairs={{0,8},{8,16},{16,24},{24,32},{32,40},{40,48},{48,56},{56,64},{64,7... | collective-permute-start | bytes 786440 | tf_op jit(solution)/shard_map/ppermute | solution.py:743
  13.1 0.0 collective-permute-done
  13.1 0.0 collective-permute-done.1
  13.1 0.0 collective-permute-done.2
  13.1 0.1 add_convert_fusion.3
  13.2 0.2 collective-permute-start.6
  13.4 3.3 %collective-permute-start.5 = (bf16[128,512]{1,0:T(8,128)(2,1)S(1)}, bf16[128,512]{1,0:T(8,128)(2,1)S(1)}, u32[]{:S(2)}, u32[]{:S(2)}) collective-permute-start(bf16[128,512]{1,0:T(8,128)(2,1)S(1)} %add_convert_fusion.3), channel_id=1, source_target_pairs={{0,64},{8,72},{16,80},{24,88},{32,96},{40,104},{48,112},{56,120},{... | collective-permute-start | bytes 393224 | tf_op jit(solution)/shard_map/ppermute | solution.py:756
  16.6 2.2 %collective-permute-start.4 = (bf16[128,512]{1,0:T(8,128)(2,1)S(1)}, bf16[128,512]{1,0:T(8,128)(2,1)S(1)}, u32[]{:S(2)}, u32[]{:S(2)}) collective-permute-start(bf16[128,512]{1,0:T(8,128)(2,1)S(1)} %add_convert_fusion.3), channel_id=1, source_target_pairs={{0,32},{8,40},{16,48},{24,56},{32,64},{40,72},{48,80},{56,88},{64,... | collective-permute-start | bytes 393224 | tf_op jit(solution)/shard_map/ppermute | solution.py:756
  18.8 3.0 %collective-permute-done.3.halo = bf16[2,128,512]{2,1,0:T(8,128)(2,1)S(1)} collective-permute-done((bf16[2,128,512]{2,1,0:T(8,128)(2,1)S(1)}, bf16[2,128,512]{2,1,0:T(8,128)(2,1)S(1)}, u32[]{:S(2)}, u32[]{:S(2)}) %collective-permute-start.3) | collective-permute-done | bytes 262176 | tf_op jit(solution)/shard_map/ppermute | solution.py:743
  21.9 8.2 %all-to-all-start = ((s32[128,1,128]{2,1,0:T(1,128)}), s32[128,1,128]{2,1,0:T(1,128)S(1)}, u32[]{:S(2)}, u32[]{:S(2)}) async-start(s32[128,1,128]{2,1,0:T(1,128)} %bitcast.39), calls=%async_computation | async-start | bytes 131072 | tf_op jit(solution)/shard_map/all_to_all | solution.py:747
  30.1 0.0 collective-permute-done.6
  30.1 0.0 collective-permute-done.5
  30.1 0.1 add_convert_fusion.2.glob0
  30.2 2.8 %collective-permute-start.9 = (bf16[128,512]{1,0:T(8,128)(2,1)S(1)}, bf16[128,512]{1,0:T(8,128)(2,1)S(1)}, u32[]{:S(2)}, u32[]{:S(2)}) collective-permute-start(bf16[128,512]{1,0:T(8,128)(2,1)S(1)} %add_convert_fusion.2.glob0), channel_id=1, source_target_pairs={{0,24},{8,0},{16,8},{24,16},{32,56},{40,32},{48,40},{56,48},{64,88... | collective-permute-start | bytes 393224 | tf_op jit(solution)/shard_map/ppermute | solution.py:752
  33.0 0.8 collective-permute-start.8
  33.8 0.9 collective-permute-start.7
  34.7 4.4 %all-to-all-done = s32[128,1,128]{2,1,0:T(1,128)S(1)} async-done(((s32[128,1,128]{2,1,0:T(1,128)}), s32[128,1,128]{2,1,0:T(1,128)S(1)}, u32[]{:S(2)}, u32[]{:S(2)}) %all-to-all-start) | async-done | bytes 65568 | tf_op jit(solution)/shard_map/all_to_all | solution.py:747
  39.1 6.5 %gather_rows.1 = (bf16[4096,128]{1,0:T(8,128)(2,1)}, s32[128,128]{1,0:T(8,128)}) custom-call(s32[128,128]{1,0:T(8,128)S(1)} %bitcast.33, bf16[4096,128]{1,0:T(8,128)(2,1)} %table_far.1), custom_call_target="tpu_custom_call" | custom-call | flops 4294967296 | bytes 2000000 | tf_op jit(solution)/shard_map/gather_rows/pallas_call | solution.py:229
  45.6 0.0 copy-start
  45.6 0.0 copy-start.4
  45.6 0.0 copy-start.5
  45.6 0.0 collective-permute-done.8.glob2
  45.6 0.0 collective-permute-done.7.glob1
  45.6 5.0 %all-to-all-start.1 = ((bf16[128,32,128]{2,1,0:T(8,128)(2,1)}), bf16[128,32,128]{2,1,0:T(8,128)(2,1)S(1)}, u32[]{:S(2)}, u32[]{:S(2)}) async-start(bf16[128,32,128]{2,1,0:T(8,128)(2,1)} %bitcast.35), calls=%async_computation.1 | async-start | bytes 2097152 | tf_op jit(solution)/shard_map/all_to_all | solution.py:747
  50.7 4.6 %near_forward.1 = (bf16[8,512,256]{2,1,0:T(8,128)(2,1)}, bf16[8,512,256]{2,1,0:T(8,128)(2,1)}, f32[512,512]{1,0:T(8,128)S(1)}) custom-call(s32[8]{0:T(128)} %lengths.5, bf16[512,512]{1,0:T(8,128)(2,1)S(1)} %bitcast.21, bf16[512,512]{1,0:T(8,128)(2,1)S(1)} %bitcast.25, bf16[512,512]{1,0:T(8,128)(2,1)S(1)} %bitcast.28, ...), custom_call_target="tpu_custom_call" | custom-call | flops 500000000 | bytes 7000000 | tf_op jit(solution)/shard_map/near_forward/pallas_call | solution.py:421
  55.3 6.5 %far_forward.1 = (bf16[8,512,256]{2,1,0:T(8,128)(2,1)}, bf16[8,512,256]{2,1,0:T(8,128)(2,1)}, f32[512,512]{1,0:T(8,128)}, f32[512,1]{1,0:T(8,128)}, bf16[512,128]{1,0:T(8,128)(2,1)}) custom-call(s32[8]{0:T(128)} %lengths.5, s32[1,2]{1,0:T(1,128)} %gids.5, bf16[512,512]{1,0:T(8,128)(2,1)S(1)} %bitcast.22, bf16[128,512]{1,0:T(8,128)(2,1)S(1)} %add_convert_fusion.2.glob0, ...), custom_call_target="tpu_custom_call" | custom-call | flops 600000000 | bytes 9000000 | tf_op jit(solution)/shard_map/far_forward/pallas_call | solution.py:436
  61.8 7.7 %all-to-all-done.1 = bf16[128,32,128]{2,1,0:T(8,128)(2,1)S(1)} async-done(((bf16[128,32,128]{2,1,0:T(8,128)(2,1)}), bf16[128,32,128]{2,1,0:T(8,128)(2,1)S(1)}, u32[]{:S(2)}, u32[]{:S(2)}) %all-to-all-start.1) | async-done | bytes 1048608 | tf_op jit(solution)/shard_map/all_to_all | solution.py:747
  69.5 6.1 %ranking.1 = (bf16[4096,128]{1,0:T(8,128)(2,1)}, bf16[512,512]{1,0:T(8,128)(2,1)}, bf16[512,512]{1,0:T(8,128)(2,1)}) custom-call(s32[8]{0:T(128)} %lengths.5, bf16[4096,128]{1,0:T(8,128)(2,1)S(1)} %bitcast.32, bf16[128,512]{1,0:T(8,128)(2,1)} %get-tuple-element.88.code, bf16[512,128]{1,0:T(8,128)(2,1)} %get-tuple-element.94.user, ...), custom_call_target="tpu_custom_call" | custom-call | flops 2000000000 | bytes 6000000 | tf_op jit(solution)/shard_map/ranking/pallas_call | solution.py:680
  75.6 4.9 %all-to-all-start.2 = ((bf16[128,32,128]{2,1,0:T(8,128)(2,1)}), bf16[128,32,128]{2,1,0:T(8,128)(2,1)S(1)}, u32[]{:S(2)}, u32[]{:S(2)}) async-start(bf16[128,32,128]{2,1,0:T(8,128)(2,1)} %bitcast.34), calls=%async_computation.2 | async-start | bytes 2097152 | tf_op jit(solution)/shard_map/all_to_all | solution.py:747
  80.5 0.0 copy-start.1
  80.5 0.0 copy-start.2
  80.6 0.0 copy-start.6
  80.6 5.5 %far_backward.1 = (f32[512,512]{1,0:T(8,128)S(1)}, bf16[128,512]{1,0:T(8,128)(2,1)S(1)}, bf16[128,512]{1,0:T(8,128)(2,1)S(1)}, bf16[128,512]{1,0:T(8,128)(2,1)S(1)}, bf16[128,512]{1,0:T(8,128)(2,1)S(1)}) custom-call(bf16[512,512]{1,0:T(8,128)(2,1)} %bitcast.20, bf16[128,512]{1,0:T(8,128)(2,1)S(1)} %add_convert_fusion.2.glob0, ...), custom_call_target="tpu_custom_call" | custom-call | flops 1000000000 | bytes 7000000 | tf_op jit(solution)/shard_map/far_backward/pallas_call | solution.py:496
  86.1 1.5 %collective-permute-start.10 = (bf16[128,512]{1,0:T(8,128)(2,1)S(1)}, bf16[128,512]{1,0:T(8,128)(2,1)S(1)}, u32[]{:S(2)}, u32[]{:S(2)}) collective-permute-start(bf16[128,512]{1,0:T(8,128)(2,1)S(1)} %get-tuple-element.106), channel_id=1, source_target_pairs={{0,8},{8,16},{16,24},{24,0},{32,40},{40,48},{48,56},{56,32},{64,72... | collective-permute-start | bytes 393224 | tf_op jit(solution)/shard_map/ppermute | solution.py:752
  87.6 2.7 %collective-permute-start.11 = (bf16[128,512]{1,0:T(8,128)(2,1)S(1)}, bf16[128,512]{1,0:T(8,128)(2,1)S(1)}, u32[]{:S(2)}, u32[]{:S(2)}) collective-permute-start(bf16[128,512]{1,0:T(8,128)(2,1)S(1)} %get-tuple-element.107), channel_id=1, source_target_pairs={{0,16},{8,24},{16,0},{24,8},{32,48},{40,56},{48,32},{56,40},{64,80... | collective-permute-start | bytes 393224 | tf_op jit(solution)/shard_map/ppermute | solution.py:752
  90.4 1.4 %collective-permute-start.12 = (bf16[128,512]{1,0:T(8,128)(2,1)S(1)}, bf16[128,512]{1,0:T(8,128)(2,1)S(1)}, u32[]{:S(2)}, u32[]{:S(2)}) collective-permute-start(bf16[128,512]{1,0:T(8,128)(2,1)S(1)} %get-tuple-element.108), channel_id=1, source_target_pairs={{0,24},{8,0},{16,8},{24,16},{32,56},{40,32},{48,40},{56,48},{64,88... | collective-permute-start | bytes 393224 | tf_op jit(solution)/shard_map/ppermute | solution.py:752
  91.8 4.2 %near_backward.1 = (bf16[512,512]{1,0:T(8,128)(2,1)}, bf16[512,512]{1,0:T(8,128)(2,1)}, bf16[512,512]{1,0:T(8,128)(2,1)}, bf16[2,128,512]{2,1,0:T(8,128)(2,1)S(1)}) custom-call(bf16[512,512]{1,0:T(8,128)(2,1)S(1)} %bitcast.23, bf16[512,512]{1,0:T(8,128)(2,1)S(1)} %bitcast.26, bf16[512,512]{1,0:T(8,128)(2,1)S(1)} %bitcast.29, ...), custom_call_target="tpu_custom_call" | custom-call | flops 1000000000 | bytes 9000000 | tf_op jit(solution)/shard_map/near_backward/pallas_call | solution.py:561
  96.1 1.9 %collective-permute-start.13 = (bf16[2,128,512]{2,1,0:T(8,128)(2,1)S(1)}, bf16[2,128,512]{2,1,0:T(8,128)(2,1)S(1)}, u32[]{:S(2)}, u32[]{:S(2)}) collective-permute-start(bf16[2,128,512]{2,1,0:T(8,128)(2,1)S(1)} %get-tuple-element.111), channel_id=1, source_target_pairs={{8,0},{16,8},{24,16},{32,24},{40,32},{48,40},{56,48},{64,56},{72,6... | collective-permute-start | bytes 786440 | tf_op jit(solution)/shard_map/ppermute | solution.py:743
  98.0 0.0 collective-permute-done.10
  98.0 2.7 %collective-permute-done.11 = bf16[128,512]{1,0:T(8,128)(2,1)S(1)} collective-permute-done((bf16[128,512]{1,0:T(8,128)(2,1)S(1)}, bf16[128,512]{1,0:T(8,128)(2,1)S(1)}, u32[]{:S(2)}, u32[]{:S(2)}) %collective-permute-start.11) | collective-permute-done | bytes 131104 | tf_op jit(solution)/shard_map/ppermute | solution.py:752
  100.7 0.0 collective-permute-done.12
  100.7 0.1 add_convert_fusion.1
  100.8 0.4 collective-permute-start.16
  101.2 2.9 %collective-permute-start.15 = (bf16[128,512]{1,0:T(8,128)(2,1)S(1)}, bf16[128,512]{1,0:T(8,128)(2,1)S(1)}, u32[]{:S(2)}, u32[]{:S(2)}) collective-permute-start(bf16[128,512]{1,0:T(8,128)(2,1)S(1)} %add_convert_fusion.1), channel_id=1, source_target_pairs={{0,64},{8,72},{16,80},{24,88},{32,96},{40,104},{48,112},{56,120},{... | collective-permute-start | bytes 393224 | tf_op jit(solution)/shard_map/ppermute | solution.py:756
  104.1 2.0 %collective-permute-start.14 = (bf16[128,512]{1,0:T(8,128)(2,1)S(1)}, bf16[128,512]{1,0:T(8,128)(2,1)S(1)}, u32[]{:S(2)}, u32[]{:S(2)}) collective-permute-start(bf16[128,512]{1,0:T(8,128)(2,1)S(1)} %add_convert_fusion.1), channel_id=1, source_target_pairs={{0,32},{8,40},{16,48},{24,56},{32,64},{40,72},{48,80},{56,88},{64,... | collective-permute-start | bytes 393224 | tf_op jit(solution)/shard_map/ppermute | solution.py:756
  106.1 4.0 %scatter_rows.2.refs_0_ = f32[4,1024,128]{2,1,0:T(8,128)} custom-call(s32[128,128]{1,0:T(8,128)S(1)} %copy-done.9, bf16[4096,128]{1,0:T(8,128)(2,1)S(1)} %bitcast.30), custom_call_target="tpu_custom_call" | custom-call | flops 2147483648 | bytes 2000000 | tf_op jit(solution)/shard_map/scatter_rows/pallas_call | solution.py:276
  110.1 0.0 collective-permute-done.16
  110.1 0.5 collective-permute-done.14
  110.6 0.1 add_convert_fusion.glob0
  110.7 0.0 copy-start.7
  110.7 0.0 copy-start.8
  110.7 4.3 %collective-permute-start.19 = (bf16[128,512]{1,0:T(8,128)(2,1)S(1)}, bf16[128,512]{1,0:T(8,128)(2,1)S(1)}, u32[]{:S(2)}, u32[]{:S(2)}) collective-permute-start(bf16[128,512]{1,0:T(8,128)(2,1)S(1)} %add_convert_fusion.glob0), channel_id=1, source_target_pairs={{0,24},{8,0},{16,8},{24,16},{32,56},{40,32},{48,40},{56,48},{64,88... | collective-permute-start | bytes 393224 | tf_op jit(solution)/shard_map/ppermute | solution.py:752
  115.0 0.9 collective-permute-start.17
  115.9 4.0 %scatter_rows.3 = f32[4,1024,128]{2,1,0:T(8,128)} custom-call(s32[128,128]{1,0:T(8,128)S(1)} %copy-done.9, bf16[4096,128]{1,0:T(8,128)(2,1)S(1)} %bitcast.31, f32[4,1024,128]{2,1,0:T(8,128)} %scatter_rows.2.refs_0_), custom_call_target="tpu_custom_call", output_to_operand_aliasing={{}: (2, {})} | custom-call | flops 2147483648 | bytes 2000000 | tf_op jit(solution)/shard_map/scatter_rows/pallas_call | solution.py:276
  119.9 0.8 collective-permute-done.19.glob3
  120.7 2.2 %collective-permute-done.18.glob2 = bf16[128,512]{1,0:T(8,128)(2,1)S(1)} collective-permute-done((bf16[128,512]{1,0:T(8,128)(2,1)S(1)}, bf16[128,512]{1,0:T(8,128)(2,1)S(1)}, u32[]{:S(2)}, u32[]{:S(2)}) %collective-permute-start.18) | collective-permute-done | bytes 131104 | tf_op jit(solution)/shard_map/ppermute | solution.py:752
  122.9 1.3 collective-permute-done.17.glob1
  124.1 0.0 collective-permute-done.13.edge
  124.1 1.8 %add_received.1 = (bf16[512,512]{1,0:T(8,128)(2,1)}, bf16[512,512]{1,0:T(8,128)(2,1)}) custom-call(s32[1,2]{1,0:T(1,128)} %gids.5, bf16[512,512]{1,0:T(8,128)(2,1)S(1)} %copy-done.7, bf16[512,512]{1,0:T(8,128)(2,1)S(1)} %copy-done.8, bf16[2,128,512]{2,1,0:T(8,128)(2,1)S(1)} %collective-permute-done.13.edge, bf16[128,512]{1,0:T(8,128)(2,1)S(1)} %add_convert_fusion.glob0, ...), custom_call_target="tpu_custom_call" | custom-call | flops 1000000 | bytes 3000000 | tf_op jit(solution)/shard_map/add_received/pallas_call | solution.py:729
  (17 shorter events, 0.0 us)
Async XLA Ops:
  2.3 10.7 %collective-permute-start = (bf16[128,512]{1,0:T(8,128)(2,1)S(1)}, bf16[128,512]{1,0:T(8,128)(2,1)S(1)}, u32[]{:S(2)}, u32[]{:S(2)}) collective-permute-start(bf16[128,512]{1,0:T(8,128)(2,1)S(1)} %get-tuple-element.73), channel_id=1, source_target_pairs={{0,8},{8,16},{16,24},{24,0},{32,40},{40,48},{48,56},{56,32},{64,72... | collective-permute-start | bytes 393224 | tf_op jit(solution)/shard_map/ppermute | solution.py:752
  3.9 9.2 %collective-permute-start.1 = (bf16[128,512]{1,0:T(8,128)(2,1)S(1)}, bf16[128,512]{1,0:T(8,128)(2,1)S(1)}, u32[]{:S(2)}, u32[]{:S(2)}) collective-permute-start(bf16[128,512]{1,0:T(8,128)(2,1)S(1)} %get-tuple-element.74), channel_id=1, source_target_pairs={{0,16},{8,24},{16,0},{24,8},{32,48},{40,56},{48,32},{56,40},{64,80... | collective-permute-start | bytes 393224 | tf_op jit(solution)/shard_map/ppermute | solution.py:752
  6.6 6.5 %collective-permute-start.2 = (bf16[128,512]{1,0:T(8,128)(2,1)S(1)}, bf16[128,512]{1,0:T(8,128)(2,1)S(1)}, u32[]{:S(2)}, u32[]{:S(2)}) collective-permute-start(bf16[128,512]{1,0:T(8,128)(2,1)S(1)} %get-tuple-element.75), channel_id=1, source_target_pairs={{0,24},{8,0},{16,8},{24,16},{32,56},{40,32},{48,40},{56,48},{64,88... | collective-permute-start | bytes 393224 | tf_op jit(solution)/shard_map/ppermute | solution.py:752
  10.6 11.3 %collective-permute-start.3 = (bf16[2,128,512]{2,1,0:T(8,128)(2,1)S(1)}, bf16[2,128,512]{2,1,0:T(8,128)(2,1)S(1)}, u32[]{:S(2)}, u32[]{:S(2)}) collective-permute-start(bf16[2,128,512]{2,1,0:T(8,128)(2,1)S(1)} %get-tuple-element.78), channel_id=1, source_target_pairs={{0,8},{8,16},{16,24},{24,32},{32,40},{40,48},{48,56},{56,64},{64,7... | collective-permute-start | bytes 786440 | tf_op jit(solution)/shard_map/ppermute | solution.py:743
  13.2 16.9 %collective-permute-start.6 = (bf16[128,512]{1,0:T(8,128)(2,1)S(1)}, bf16[128,512]{1,0:T(8,128)(2,1)S(1)}, u32[]{:S(2)}, u32[]{:S(2)}) collective-permute-start(bf16[128,512]{1,0:T(8,128)(2,1)S(1)} %add_convert_fusion.3), channel_id=1, source_target_pairs={{0,96},{8,104},{16,112},{24,120},{32,0},{40,8},{48,16},{56,24},{64... | collective-permute-start | bytes 393224 | tf_op jit(solution)/shard_map/ppermute | solution.py:756
  13.4 16.7 %collective-permute-start.5 = (bf16[128,512]{1,0:T(8,128)(2,1)S(1)}, bf16[128,512]{1,0:T(8,128)(2,1)S(1)}, u32[]{:S(2)}, u32[]{:S(2)}) collective-permute-start(bf16[128,512]{1,0:T(8,128)(2,1)S(1)} %add_convert_fusion.3), channel_id=1, source_target_pairs={{0,64},{8,72},{16,80},{24,88},{32,96},{40,104},{48,112},{56,120},{... | collective-permute-start | bytes 393224 | tf_op jit(solution)/shard_map/ppermute | solution.py:756
  16.6 13.5 %collective-permute-start.4 = (bf16[128,512]{1,0:T(8,128)(2,1)S(1)}, bf16[128,512]{1,0:T(8,128)(2,1)S(1)}, u32[]{:S(2)}, u32[]{:S(2)}) collective-permute-start(bf16[128,512]{1,0:T(8,128)(2,1)S(1)} %add_convert_fusion.3), channel_id=1, source_target_pairs={{0,32},{8,40},{16,48},{24,56},{32,64},{40,72},{48,80},{56,88},{64,... | collective-permute-start | bytes 393224 | tf_op jit(solution)/shard_map/ppermute | solution.py:756
  21.9 17.2 %all-to-all-start = ((s32[128,1,128]{2,1,0:T(1,128)}), s32[128,1,128]{2,1,0:T(1,128)S(1)}, u32[]{:S(2)}, u32[]{:S(2)}) async-start(s32[128,1,128]{2,1,0:T(1,128)} %bitcast.39), calls=%async_computation | async-start | bytes 131072 | tf_op jit(solution)/shard_map/all_to_all | solution.py:747
  30.2 15.4 %collective-permute-start.9 = (bf16[128,512]{1,0:T(8,128)(2,1)S(1)}, bf16[128,512]{1,0:T(8,128)(2,1)S(1)}, u32[]{:S(2)}, u32[]{:S(2)}) collective-permute-start(bf16[128,512]{1,0:T(8,128)(2,1)S(1)} %add_convert_fusion.2.glob0), channel_id=1, source_target_pairs={{0,24},{8,0},{16,8},{24,16},{32,56},{40,32},{48,40},{56,48},{64,88... | collective-permute-start | bytes 393224 | tf_op jit(solution)/shard_map/ppermute | solution.py:752
  33.0 12.6 %collective-permute-start.8 = (bf16[128,512]{1,0:T(8,128)(2,1)S(1)}, bf16[128,512]{1,0:T(8,128)(2,1)S(1)}, u32[]{:S(2)}, u32[]{:S(2)}) collective-permute-start(bf16[128,512]{1,0:T(8,128)(2,1)S(1)} %add_convert_fusion.2.glob0), channel_id=1, source_target_pairs={{0,16},{8,24},{16,0},{24,8},{32,48},{40,56},{48,32},{56,40},{64,80... | collective-permute-start | bytes 393224 | tf_op jit(solution)/shard_map/ppermute | solution.py:752
  33.8 11.8 %collective-permute-start.7 = (bf16[128,512]{1,0:T(8,128)(2,1)S(1)}, bf16[128,512]{1,0:T(8,128)(2,1)S(1)}, u32[]{:S(2)}, u32[]{:S(2)}) collective-permute-start(bf16[128,512]{1,0:T(8,128)(2,1)S(1)} %add_convert_fusion.2.glob0), channel_id=1, source_target_pairs={{0,8},{8,16},{16,24},{24,0},{32,40},{40,48},{48,56},{56,32},{64,72... | collective-permute-start | bytes 393224 | tf_op jit(solution)/shard_map/ppermute | solution.py:752
  45.6 5.1 %copy-start = (bf16[1,512,512]{2,1,0:T(8,128)(2,1)S(1)}, bf16[1,512,512]{2,1,0:T(8,128)(2,1)}, u32[]{:S(2)}) copy-start(bf16[1,512,512]{2,1,0:T(8,128)(2,1)} %param.11) | copy-start | bytes 1572868
  45.6 5.1 %copy-start.4 = (bf16[1,512,512]{2,1,0:T(8,128)(2,1)S(1)}, bf16[1,512,512]{2,1,0:T(8,128)(2,1)}, u32[]{:S(2)}) copy-start(bf16[1,512,512]{2,1,0:T(8,128)(2,1)} %param.12) | copy-start | bytes 1572868
  45.6 5.1 %copy-start.5 = (bf16[1,512,512]{2,1,0:T(8,128)(2,1)S(1)}, bf16[1,512,512]{2,1,0:T(8,128)(2,1)}, u32[]{:S(2)}) copy-start(bf16[1,512,512]{2,1,0:T(8,128)(2,1)} %param.13) | copy-start | bytes 1572868
  45.6 23.9 %all-to-all-start.1 = ((bf16[128,32,128]{2,1,0:T(8,128)(2,1)}), bf16[128,32,128]{2,1,0:T(8,128)(2,1)S(1)}, u32[]{:S(2)}, u32[]{:S(2)}) async-start(bf16[128,32,128]{2,1,0:T(8,128)(2,1)} %bitcast.35), calls=%async_computation.1 | async-start | bytes 2097152 | tf_op jit(solution)/shard_map/all_to_all | solution.py:747
  75.6 25.2 %all-to-all-start.2 = ((bf16[128,32,128]{2,1,0:T(8,128)(2,1)}), bf16[128,32,128]{2,1,0:T(8,128)(2,1)S(1)}, u32[]{:S(2)}, u32[]{:S(2)}) async-start(bf16[128,32,128]{2,1,0:T(8,128)(2,1)} %bitcast.34), calls=%async_computation.2 | async-start | bytes 2097152 | tf_op jit(solution)/shard_map/all_to_all | solution.py:747
  80.5 11.3 %copy-start.1 = (bf16[1,512,512]{2,1,0:T(8,128)(2,1)S(1)}, bf16[1,512,512]{2,1,0:T(8,128)(2,1)}, u32[]{:S(2)}) copy-start(bf16[1,512,512]{2,1,0:T(8,128)(2,1)} %param.11) | copy-start | bytes 1572868
  80.5 11.3 %copy-start.2 = (bf16[8,512,256]{2,1,0:T(8,128)(2,1)S(1)}, bf16[8,512,256]{2,1,0:T(8,128)(2,1)}, u32[]{:S(2)}) copy-start(bf16[8,512,256]{2,1,0:T(8,128)(2,1)} %get-tuple-element.98.probs) | copy-start | bytes 6291460
  80.6 11.3 %copy-start.3 = (bf16[8,512,256]{2,1,0:T(8,128)(2,1)S(1)}, bf16[8,512,256]{2,1,0:T(8,128)(2,1)}, u32[]{:S(2)}) copy-start(bf16[8,512,256]{2,1,0:T(8,128)(2,1)} %get-tuple-element.99.slope) | copy-start | bytes 6291460
  80.6 11.3 %copy-start.6 = (bf16[512,512]{1,0:T(8,128)(2,1)S(1)}, bf16[512,512]{1,0:T(8,128)(2,1)}, u32[]{:S(2)}) copy-start(bf16[512,512]{1,0:T(8,128)(2,1)} %get-tuple-element.97.grad) | copy-start | bytes 1572868
  86.1 11.9 %collective-permute-start.10 = (bf16[128,512]{1,0:T(8,128)(2,1)S(1)}, bf16[128,512]{1,0:T(8,128)(2,1)S(1)}, u32[]{:S(2)}, u32[]{:S(2)}) collective-permute-start(bf16[128,512]{1,0:T(8,128)(2,1)S(1)} %get-tuple-element.106), channel_id=1, source_target_pairs={{0,8},{8,16},{16,24},{24,0},{32,40},{40,48},{48,56},{56,32},{64,72... | collective-permute-start | bytes 393224 | tf_op jit(solution)/shard_map/ppermute | solution.py:752
  87.6 13.1 %collective-permute-start.11 = (bf16[128,512]{1,0:T(8,128)(2,1)S(1)}, bf16[128,512]{1,0:T(8,128)(2,1)S(1)}, u32[]{:S(2)}, u32[]{:S(2)}) collective-permute-start(bf16[128,512]{1,0:T(8,128)(2,1)S(1)} %get-tuple-element.107), channel_id=1, source_target_pairs={{0,16},{8,24},{16,0},{24,8},{32,48},{40,56},{48,32},{56,40},{64,80... | collective-permute-start | bytes 393224 | tf_op jit(solution)/shard_map/ppermute | solution.py:752
  90.4 10.4 %collective-permute-start.12 = (bf16[128,512]{1,0:T(8,128)(2,1)S(1)}, bf16[128,512]{1,0:T(8,128)(2,1)S(1)}, u32[]{:S(2)}, u32[]{:S(2)}) collective-permute-start(bf16[128,512]{1,0:T(8,128)(2,1)S(1)} %get-tuple-element.108), channel_id=1, source_target_pairs={{0,24},{8,0},{16,8},{24,16},{32,56},{40,32},{48,40},{56,48},{64,88... | collective-permute-start | bytes 393224 | tf_op jit(solution)/shard_map/ppermute | solution.py:752
  91.8 14.3 %copy-start.9 = (s32[128,128]{1,0:T(8,128)S(1)}, s32[128,128]{1,0:T(8,128)}, u32[]{:S(2)}) copy-start(s32[128,128]{1,0:T(8,128)} %get-tuple-element.112.asked) | copy-start | bytes 196612
  96.1 28.1 %collective-permute-start.13 = (bf16[2,128,512]{2,1,0:T(8,128)(2,1)S(1)}, bf16[2,128,512]{2,1,0:T(8,128)(2,1)S(1)}, u32[]{:S(2)}, u32[]{:S(2)}) collective-permute-start(bf16[2,128,512]{2,1,0:T(8,128)(2,1)S(1)} %get-tuple-element.111), channel_id=1, source_target_pairs={{8,0},{16,8},{24,16},{32,24},{40,32},{48,40},{56,48},{64,56},{72,6... | collective-permute-start | bytes 786440 | tf_op jit(solution)/shard_map/ppermute | solution.py:743
  100.8 9.3 %collective-permute-start.16 = (bf16[128,512]{1,0:T(8,128)(2,1)S(1)}, bf16[128,512]{1,0:T(8,128)(2,1)S(1)}, u32[]{:S(2)}, u32[]{:S(2)}) collective-permute-start(bf16[128,512]{1,0:T(8,128)(2,1)S(1)} %add_convert_fusion.1), channel_id=1, source_target_pairs={{0,96},{8,104},{16,112},{24,120},{32,0},{40,8},{48,16},{56,24},{64... | collective-permute-start | bytes 393224 | tf_op jit(solution)/shard_map/ppermute | solution.py:756
  101.2 8.9 %collective-permute-start.15 = (bf16[128,512]{1,0:T(8,128)(2,1)S(1)}, bf16[128,512]{1,0:T(8,128)(2,1)S(1)}, u32[]{:S(2)}, u32[]{:S(2)}) collective-permute-start(bf16[128,512]{1,0:T(8,128)(2,1)S(1)} %add_convert_fusion.1), channel_id=1, source_target_pairs={{0,64},{8,72},{16,80},{24,88},{32,96},{40,104},{48,112},{56,120},{... | collective-permute-start | bytes 393224 | tf_op jit(solution)/shard_map/ppermute | solution.py:756
  104.1 6.5 %collective-permute-start.14 = (bf16[128,512]{1,0:T(8,128)(2,1)S(1)}, bf16[128,512]{1,0:T(8,128)(2,1)S(1)}, u32[]{:S(2)}, u32[]{:S(2)}) collective-permute-start(bf16[128,512]{1,0:T(8,128)(2,1)S(1)} %add_convert_fusion.1), channel_id=1, source_target_pairs={{0,32},{8,40},{16,48},{24,56},{32,64},{40,72},{48,80},{56,88},{64,... | collective-permute-start | bytes 393224 | tf_op jit(solution)/shard_map/ppermute | solution.py:756
  110.7 13.5 %copy-start.7 = (bf16[512,512]{1,0:T(8,128)(2,1)S(1)}, bf16[512,512]{1,0:T(8,128)(2,1)}, u32[]{:S(2)}) copy-start(bf16[512,512]{1,0:T(8,128)(2,1)} %get-tuple-element.109.d_k) | copy-start | bytes 1572868
  110.7 13.5 %copy-start.8 = (bf16[512,512]{1,0:T(8,128)(2,1)S(1)}, bf16[512,512]{1,0:T(8,128)(2,1)}, u32[]{:S(2)}) copy-start(bf16[512,512]{1,0:T(8,128)(2,1)} %get-tuple-element.110.d_v) | copy-start | bytes 1572868
  110.7 10.0 %collective-permute-start.19 = (bf16[128,512]{1,0:T(8,128)(2,1)S(1)}, bf16[128,512]{1,0:T(8,128)(2,1)S(1)}, u32[]{:S(2)}, u32[]{:S(2)}) collective-permute-start(bf16[128,512]{1,0:T(8,128)(2,1)S(1)} %add_convert_fusion.glob0), channel_id=1, source_target_pairs={{0,24},{8,0},{16,8},{24,16},{32,56},{40,32},{48,40},{56,48},{64,88... | collective-permute-start | bytes 393224 | tf_op jit(solution)/shard_map/ppermute | solution.py:752
  115.0 7.9 %collective-permute-start.18 = (bf16[128,512]{1,0:T(8,128)(2,1)S(1)}, bf16[128,512]{1,0:T(8,128)(2,1)S(1)}, u32[]{:S(2)}, u32[]{:S(2)}) collective-permute-start(bf16[128,512]{1,0:T(8,128)(2,1)S(1)} %add_convert_fusion.glob0), channel_id=1, source_target_pairs={{0,16},{8,24},{16,0},{24,8},{32,48},{40,56},{48,32},{56,40},{64,80... | collective-permute-start | bytes 393224 | tf_op jit(solution)/shard_map/ppermute | solution.py:752
  115.0 9.2 %collective-permute-start.17 = (bf16[128,512]{1,0:T(8,128)(2,1)S(1)}, bf16[128,512]{1,0:T(8,128)(2,1)S(1)}, u32[]{:S(2)}, u32[]{:S(2)}) collective-permute-start(bf16[128,512]{1,0:T(8,128)(2,1)S(1)} %add_convert_fusion.glob0), channel_id=1, source_target_pairs={{0,8},{8,16},{16,24},{24,0},{32,40},{40,48},{48,56},{56,32},{64,72... | collective-permute-start | bytes 393224 | tf_op jit(solution)/shard_map/ppermute | solution.py:752

commit v3 on v2

--- a/solution.py
+++ b/solution.py
@@ -738,9 +738,8 @@
 
 
 def from_behind(block, axis, distance):
-    devices = range(lax.axis_size(axis))
-    route_pairs = [(i - distance, i) for i in devices if i - distance in devices]
-    return lax.ppermute(block, axis, route_pairs)
+    size = lax.axis_size(axis)
+    return lax.ppermute(block, axis, [(i, (i + distance) % size) for i in range(size)])
 
 
 def exchange(x, axis):

time: 126 us -> 124 us (0.984)
  starting transfers between devices: 54.6 us -> 50.8 us
  waiting for transfers between devices: 22.6 us -> 24.6 us
    ppermute x12, waiting for transfers between devices: 7.01 us -> 11.1 us  [around_x(): return lax.ppermute(x, 'seq', pairs)]
    ppermute x2, starting transfers between devices: 4.4 us -> 0.6 us  [from_behind(): lax.ppermute(block, axis, [(i, (i + distance) % size) for i in range(size)])]
    ppermute x2, waiting for transfers between devices: 3.01 us -> 0.89 us  [from_behind(): lax.ppermute(block, axis, [(i, (i + distance) % size) for i in range(size)])]
  transfers between devices with their start and end apart: 23 -> 23, of which waited for: 8 -> 10; matrix products, arithmetic and copies ran while one was open for 0% -> 0% of each run, Pallas kernels for 30% -> 30%
where the time goes in v3:
time: 124 us
  starting transfers between devices  50.8 us (41%)
  Pallas kernels  47.4 us (38%)
  waiting for transfers between devices  24.6 us (20%)
    ppermute x12, starting transfers between devices, around_x(): return lax.ppermute(x, 'seq', pairs)  21.1 us
    all_to_all x3, starting transfers between devices, exchange(): return lax.all_to_all(x, axis, split_axis=0, concat_axis=0, tiled=True)  18 us
    all_to_all x3, waiting for transfers between devices, exchange(): return lax.all_to_all(x, axis, split_axis=0, concat_axis=0, tiled=True)  12.1 us
    ppermute x12, waiting for transfers between devices, around_x(): return lax.ppermute(x, 'seq', pairs)  11.1 us
    ppermute x6, starting transfers between devices, around_z(): lax.ppermute(x, 'seq', [(i, (i + distance * XSIZE) % NSEQ) for i in range...  11 us
    pallas_call x2, Pallas kernels, scatter(): pl.pallas_call(functools.partial(scatter_kernel, half), grid=(1,), out_sh...  7.96 us
    pallas_call x1, Pallas kernels, gather(): pl.pallas_call(gather_kernel, out_shape=(slow((NDEV * SLOTS, E), BF), slo...  6.5 us
    pallas_call x1, Pallas kernels, far_forward(): pl.pallas_call(far_forward_kernel, grid=(PAIRS,), out_shape=(SQUARE, SQUA...  6.47 us
  transfers between devices with their start and end apart: 23, of which 10 were waited for; matrix products, arithmetic and copies ran while one was open for 0% of the time, Pallas kernels for 30%

profile of v3, /device:TPU:32, one launch (start us, length us, event | category | flops | bytes accessed | tf_op | source)
XLA Modules:
  0.0 124.0 jit_solution(1376956972730910058)
XLA Ops:
  0.6 1.7 %pieces.1 = (bf16[2,128,512]{2,1,0:T(8,128)(2,1)S(1)}, bf16[128,512]{1,0:T(8,128)(2,1)S(1)}, bf16[128,512]{1,0:T(8,128)(2,1)S(1)}, bf16[128,512]{1,0:T(8,128)(2,1)S(1)}, bf16[128,512]{1,0:T(8,128)(2,1)S(1)}) custom-call(s32[1,2]{1,0:T(1,128)} %gids.5, bf16[512,512]{1,0:T(8,128)(2,1)} %bitcast.24, bf16[512,512]{1,0:T(8,128)(2,1)} %bitcast.27), custom_call_target="tpu_custom_call" | custom-call | flops 1000000 | bytes 2000000 | tf_op jit(solution)/shard_map/pieces/pallas_call | solution.py:121
  2.3 1.6 %collective-permute-start = (bf16[128,512]{1,0:T(8,128)(2,1)S(1)}, bf16[128,512]{1,0:T(8,128)(2,1)S(1)}, u32[]{:S(2)}, u32[]{:S(2)}) collective-permute-start(bf16[128,512]{1,0:T(8,128)(2,1)S(1)} %get-tuple-element.73), channel_id=1, source_target_pairs={{0,8},{8,16},{16,24},{24,0},{32,40},{40,48},{48,56},{56,32},{64,72... | collective-permute-start | bytes 393224 | tf_op jit(solution)/shard_map/ppermute | solution.py:751
  3.9 2.7 %collective-permute-start.1 = (bf16[128,512]{1,0:T(8,128)(2,1)S(1)}, bf16[128,512]{1,0:T(8,128)(2,1)S(1)}, u32[]{:S(2)}, u32[]{:S(2)}) collective-permute-start(bf16[128,512]{1,0:T(8,128)(2,1)S(1)} %get-tuple-element.74), channel_id=1, source_target_pairs={{0,16},{8,24},{16,0},{24,8},{32,48},{40,56},{48,32},{56,40},{64,80... | collective-permute-start | bytes 393224 | tf_op jit(solution)/shard_map/ppermute | solution.py:751
  6.6 1.4 %collective-permute-start.2 = (bf16[128,512]{1,0:T(8,128)(2,1)S(1)}, bf16[128,512]{1,0:T(8,128)(2,1)S(1)}, u32[]{:S(2)}, u32[]{:S(2)}) collective-permute-start(bf16[128,512]{1,0:T(8,128)(2,1)S(1)} %get-tuple-element.75), channel_id=1, source_target_pairs={{0,24},{8,0},{16,8},{24,16},{32,56},{40,32},{48,40},{56,48},{64,88... | collective-permute-start | bytes 393224 | tf_op jit(solution)/shard_map/ppermute | solution.py:751
  8.1 2.5 %route.1 = (s32[128,128]{1,0:T(8,128)}, bf16[128,512]{1,0:T(8,128)(2,1)}) custom-call(s32[5,1,512]{2,1,0:T(1,128)} %bitcast.43, s32[5,1,512]{2,1,0:T(1,128)} %bitcast.44), custom_call_target="tpu_custom_call" | custom-call | flops 100000000 | bytes 1000000 | tf_op jit(solution)/shard_map/route/pallas_call | solution.py:154
  10.6 0.6 collective-permute-start.3
  11.2 0.0 collective-permute-done
  11.2 2.2 %collective-permute-done.1 = bf16[128,512]{1,0:T(8,128)(2,1)S(1)} collective-permute-done((bf16[128,512]{1,0:T(8,128)(2,1)S(1)}, bf16[128,512]{1,0:T(8,128)(2,1)S(1)}, u32[]{:S(2)}, u32[]{:S(2)}) %collective-permute-start.1) | collective-permute-done | bytes 131104 | tf_op jit(solution)/shard_map/ppermute | solution.py:751
  13.3 0.0 collective-permute-done.2
  13.3 0.1 add_convert_fusion.3
  13.4 0.2 collective-permute-start.6
  13.6 3.3 %collective-permute-start.5 = (bf16[128,512]{1,0:T(8,128)(2,1)S(1)}, bf16[128,512]{1,0:T(8,128)(2,1)S(1)}, u32[]{:S(2)}, u32[]{:S(2)}) collective-permute-start(bf16[128,512]{1,0:T(8,128)(2,1)S(1)} %add_convert_fusion.3), channel_id=1, source_target_pairs={{0,64},{8,72},{16,80},{24,88},{32,96},{40,104},{48,112},{56,120},{... | collective-permute-start | bytes 393224 | tf_op jit(solution)/shard_map/ppermute | solution.py:755
  16.9 2.2 %collective-permute-start.4 = (bf16[128,512]{1,0:T(8,128)(2,1)S(1)}, bf16[128,512]{1,0:T(8,128)(2,1)S(1)}, u32[]{:S(2)}, u32[]{:S(2)}) collective-permute-start(bf16[128,512]{1,0:T(8,128)(2,1)S(1)} %add_convert_fusion.3), channel_id=1, source_target_pairs={{0,32},{8,40},{16,48},{24,56},{32,64},{40,72},{48,80},{56,88},{64,... | collective-permute-start | bytes 393224 | tf_op jit(solution)/shard_map/ppermute | solution.py:755
  19.1 0.9 collective-permute-done.3.halo
  20.0 8.1 %all-to-all-start = ((s32[128,1,128]{2,1,0:T(1,128)}), s32[128,1,128]{2,1,0:T(1,128)S(1)}, u32[]{:S(2)}, u32[]{:S(2)}) async-start(s32[128,1,128]{2,1,0:T(1,128)} %bitcast.39), calls=%async_computation | async-start | bytes 131072 | tf_op jit(solution)/shard_map/all_to_all | solution.py:746
  28.1 0.0 collective-permute-done.6
  28.1 0.0 collective-permute-done.5
  28.1 0.0 collective-permute-done.4
  28.1 0.1 add_convert_fusion.2.glob0
  28.2 2.8 %collective-permute-start.9 = (bf16[128,512]{1,0:T(8,128)(2,1)S(1)}, bf16[128,512]{1,0:T(8,128)(2,1)S(1)}, u32[]{:S(2)}, u32[]{:S(2)}) collective-permute-start(bf16[128,512]{1,0:T(8,128)(2,1)S(1)} %add_convert_fusion.2.glob0), channel_id=1, source_target_pairs={{0,24},{8,0},{16,8},{24,16},{32,56},{40,32},{48,40},{56,48},{64,88... | collective-permute-start | bytes 393224 | tf_op jit(solution)/shard_map/ppermute | solution.py:751
  31.0 0.8 collective-permute-start.8
  31.8 0.9 collective-permute-start.7
  32.7 4.4 %all-to-all-done = s32[128,1,128]{2,1,0:T(1,128)S(1)} async-done(((s32[128,1,128]{2,1,0:T(1,128)}), s32[128,1,128]{2,1,0:T(1,128)S(1)}, u32[]{:S(2)}, u32[]{:S(2)}) %all-to-all-start) | async-done | bytes 65568 | tf_op jit(solution)/shard_map/all_to_all | solution.py:746
  37.1 6.5 %gather_rows.1 = (bf16[4096,128]{1,0:T(8,128)(2,1)}, s32[128,128]{1,0:T(8,128)}) custom-call(s32[128,128]{1,0:T(8,128)S(1)} %bitcast.33, bf16[4096,128]{1,0:T(8,128)(2,1)} %table_far.1), custom_call_target="tpu_custom_call" | custom-call | flops 4294967296 | bytes 2000000 | tf_op jit(solution)/shard_map/gather_rows/pallas_call | solution.py:229
  43.6 0.0 copy-start
  43.6 0.0 copy-start.4
  43.6 0.0 copy-start.5
  43.6 0.0 collective-permute-done.9.glob3
  43.7 0.0 collective-permute-done.7.glob1
  43.7 5.0 %all-to-all-start.1 = ((bf16[128,32,128]{2,1,0:T(8,128)(2,1)}), bf16[128,32,128]{2,1,0:T(8,128)(2,1)S(1)}, u32[]{:S(2)}, u32[]{:S(2)}) async-start(bf16[128,32,128]{2,1,0:T(8,128)(2,1)} %bitcast.35), calls=%async_computation.1 | async-start | bytes 2097152 | tf_op jit(solution)/shard_map/all_to_all | solution.py:746
  48.7 4.6 %near_forward.1 = (bf16[8,512,256]{2,1,0:T(8,128)(2,1)}, bf16[8,512,256]{2,1,0:T(8,128)(2,1)}, f32[512,512]{1,0:T(8,128)S(1)}) custom-call(s32[8]{0:T(128)} %lengths.5, bf16[512,512]{1,0:T(8,128)(2,1)S(1)} %bitcast.21, bf16[512,512]{1,0:T(8,128)(2,1)S(1)} %bitcast.25, bf16[512,512]{1,0:T(8,128)(2,1)S(1)} %bitcast.28, ...), custom_call_target="tpu_custom_call" | custom-call | flops 500000000 | bytes 7000000 | tf_op jit(solution)/shard_map/near_forward/pallas_call | solution.py:421
  53.3 6.5 %far_forward.1 = (bf16[8,512,256]{2,1,0:T(8,128)(2,1)}, bf16[8,512,256]{2,1,0:T(8,128)(2,1)}, f32[512,512]{1,0:T(8,128)}, f32[512,1]{1,0:T(8,128)}, bf16[512,128]{1,0:T(8,128)(2,1)}) custom-call(s32[8]{0:T(128)} %lengths.5, s32[1,2]{1,0:T(1,128)} %gids.5, bf16[512,512]{1,0:T(8,128)(2,1)S(1)} %bitcast.22, bf16[128,512]{1,0:T(8,128)(2,1)S(1)} %add_convert_fusion.2.glob0, ...), custom_call_target="tpu_custom_call" | custom-call | flops 600000000 | bytes 9000000 | tf_op jit(solution)/shard_map/far_forward/pallas_call | solution.py:436
  59.8 7.7 %all-to-all-done.1 = bf16[128,32,128]{2,1,0:T(8,128)(2,1)S(1)} async-done(((bf16[128,32,128]{2,1,0:T(8,128)(2,1)}), bf16[128,32,128]{2,1,0:T(8,128)(2,1)S(1)}, u32[]{:S(2)}, u32[]{:S(2)}) %all-to-all-start.1) | async-done | bytes 1048608 | tf_op jit(solution)/shard_map/all_to_all | solution.py:746
  67.5 6.1 %ranking.1 = (bf16[4096,128]{1,0:T(8,128)(2,1)}, bf16[512,512]{1,0:T(8,128)(2,1)}, bf16[512,512]{1,0:T(8,128)(2,1)}) custom-call(s32[8]{0:T(128)} %lengths.5, bf16[4096,128]{1,0:T(8,128)(2,1)S(1)} %bitcast.32, bf16[128,512]{1,0:T(8,128)(2,1)} %get-tuple-element.88.code, bf16[512,128]{1,0:T(8,128)(2,1)} %get-tuple-element.94.user, ...), custom_call_target="tpu_custom_call" | custom-call | flops 2000000000 | bytes 6000000 | tf_op jit(solution)/shard_map/ranking/pallas_call | solution.py:680
  73.7 4.9 %all-to-all-start.2 = ((bf16[128,32,128]{2,1,0:T(8,128)(2,1)}), bf16[128,32,128]{2,1,0:T(8,128)(2,1)S(1)}, u32[]{:S(2)}, u32[]{:S(2)}) async-start(bf16[128,32,128]{2,1,0:T(8,128)(2,1)} %bitcast.34), calls=%async_computation.2 | async-start | bytes 2097152 | tf_op jit(solution)/shard_map/all_to_all | solution.py:746
  78.6 0.0 copy-start.1
  78.6 0.0 copy-start.2
  78.6 0.0 copy-start.6
  78.6 5.5 %far_backward.1 = (f32[512,512]{1,0:T(8,128)S(1)}, bf16[128,512]{1,0:T(8,128)(2,1)S(1)}, bf16[128,512]{1,0:T(8,128)(2,1)S(1)}, bf16[128,512]{1,0:T(8,128)(2,1)S(1)}, bf16[128,512]{1,0:T(8,128)(2,1)S(1)}) custom-call(bf16[512,512]{1,0:T(8,128)(2,1)} %bitcast.20, bf16[128,512]{1,0:T(8,128)(2,1)S(1)} %add_convert_fusion.2.glob0, ...), custom_call_target="tpu_custom_call" | custom-call | flops 1000000000 | bytes 7000000 | tf_op jit(solution)/shard_map/far_backward/pallas_call | solution.py:496
  84.1 1.5 %collective-permute-start.10 = (bf16[128,512]{1,0:T(8,128)(2,1)S(1)}, bf16[128,512]{1,0:T(8,128)(2,1)S(1)}, u32[]{:S(2)}, u32[]{:S(2)}) collective-permute-start(bf16[128,512]{1,0:T(8,128)(2,1)S(1)} %get-tuple-element.106), channel_id=1, source_target_pairs={{0,8},{8,16},{16,24},{24,0},{32,40},{40,48},{48,56},{56,32},{64,72... | collective-permute-start | bytes 393224 | tf_op jit(solution)/shard_map/ppermute | solution.py:751
  85.7 2.7 %collective-permute-start.11 = (bf16[128,512]{1,0:T(8,128)(2,1)S(1)}, bf16[128,512]{1,0:T(8,128)(2,1)S(1)}, u32[]{:S(2)}, u32[]{:S(2)}) collective-permute-start(bf16[128,512]{1,0:T(8,128)(2,1)S(1)} %get-tuple-element.107), channel_id=1, source_target_pairs={{0,16},{8,24},{16,0},{24,8},{32,48},{40,56},{48,32},{56,40},{64,80... | collective-permute-start | bytes 393224 | tf_op jit(solution)/shard_map/ppermute | solution.py:751
  88.4 1.4 %collective-permute-start.12 = (bf16[128,512]{1,0:T(8,128)(2,1)S(1)}, bf16[128,512]{1,0:T(8,128)(2,1)S(1)}, u32[]{:S(2)}, u32[]{:S(2)}) collective-permute-start(bf16[128,512]{1,0:T(8,128)(2,1)S(1)} %get-tuple-element.108), channel_id=1, source_target_pairs={{0,24},{8,0},{16,8},{24,16},{32,56},{40,32},{48,40},{56,48},{64,88... | collective-permute-start | bytes 393224 | tf_op jit(solution)/shard_map/ppermute | solution.py:751
  89.9 4.2 %near_backward.1 = (bf16[512,512]{1,0:T(8,128)(2,1)}, bf16[512,512]{1,0:T(8,128)(2,1)}, bf16[512,512]{1,0:T(8,128)(2,1)}, bf16[2,128,512]{2,1,0:T(8,128)(2,1)S(1)}) custom-call(bf16[512,512]{1,0:T(8,128)(2,1)S(1)} %bitcast.23, bf16[512,512]{1,0:T(8,128)(2,1)S(1)} %bitcast.26, bf16[512,512]{1,0:T(8,128)(2,1)S(1)} %bitcast.29, ...), custom_call_target="tpu_custom_call" | custom-call | flops 1000000000 | bytes 9000000 | tf_op jit(solution)/shard_map/near_backward/pallas_call | solution.py:561
  94.1 0.0 collective-permute-start.13
  94.1 1.8 %collective-permute-done.10 = bf16[128,512]{1,0:T(8,128)(2,1)S(1)} collective-permute-done((bf16[128,512]{1,0:T(8,128)(2,1)S(1)}, bf16[128,512]{1,0:T(8,128)(2,1)S(1)}, u32[]{:S(2)}, u32[]{:S(2)}) %collective-permute-start.10) | collective-permute-done | bytes 131104 | tf_op jit(solution)/shard_map/ppermute | solution.py:751
  95.9 2.9 %collective-permute-done.11 = bf16[128,512]{1,0:T(8,128)(2,1)S(1)} collective-permute-done((bf16[128,512]{1,0:T(8,128)(2,1)S(1)}, bf16[128,512]{1,0:T(8,128)(2,1)S(1)}, u32[]{:S(2)}, u32[]{:S(2)}) %collective-permute-start.11) | collective-permute-done | bytes 131104 | tf_op jit(solution)/shard_map/ppermute | solution.py:751
  98.8 0.0 collective-permute-done.12
  98.8 0.1 add_convert_fusion.1
  98.8 0.0 all-to-all-done.2
  98.9 0.4 collective-permute-start.16
  99.2 2.9 %collective-permute-start.15 = (bf16[128,512]{1,0:T(8,128)(2,1)S(1)}, bf16[128,512]{1,0:T(8,128)(2,1)S(1)}, u32[]{:S(2)}, u32[]{:S(2)}) collective-permute-start(bf16[128,512]{1,0:T(8,128)(2,1)S(1)} %add_convert_fusion.1), channel_id=1, source_target_pairs={{0,64},{8,72},{16,80},{24,88},{32,96},{40,104},{48,112},{56,120},{... | collective-permute-start | bytes 393224 | tf_op jit(solution)/shard_map/ppermute | solution.py:755
  102.1 2.0 %collective-permute-start.14 = (bf16[128,512]{1,0:T(8,128)(2,1)S(1)}, bf16[128,512]{1,0:T(8,128)(2,1)S(1)}, u32[]{:S(2)}, u32[]{:S(2)}) collective-permute-start(bf16[128,512]{1,0:T(8,128)(2,1)S(1)} %add_convert_fusion.1), channel_id=1, source_target_pairs={{0,32},{8,40},{16,48},{24,56},{32,64},{40,72},{48,80},{56,88},{64,... | collective-permute-start | bytes 393224 | tf_op jit(solution)/shard_map/ppermute | solution.py:755
  104.2 4.0 %scatter_rows.2.refs_0_ = f32[4,1024,128]{2,1,0:T(8,128)} custom-call(s32[128,128]{1,0:T(8,128)S(1)} %copy-done.9, bf16[4096,128]{1,0:T(8,128)(2,1)S(1)} %bitcast.30), custom_call_target="tpu_custom_call" | custom-call | flops 2147483648 | bytes 2000000 | tf_op jit(solution)/shard_map/scatter_rows/pallas_call | solution.py:276
  108.2 0.5 collective-permute-done.14
  108.6 0.1 add_convert_fusion.glob0
  108.7 0.0 copy-start.7
  108.7 0.0 copy-start.8
  108.7 4.3 %collective-permute-start.19 = (bf16[128,512]{1,0:T(8,128)(2,1)S(1)}, bf16[128,512]{1,0:T(8,128)(2,1)S(1)}, u32[]{:S(2)}, u32[]{:S(2)}) collective-permute-start(bf16[128,512]{1,0:T(8,128)(2,1)S(1)} %add_convert_fusion.glob0), channel_id=1, source_target_pairs={{0,24},{8,0},{16,8},{24,16},{32,56},{40,32},{48,40},{56,48},{64,88... | collective-permute-start | bytes 393224 | tf_op jit(solution)/shard_map/ppermute | solution.py:751
  113.0 0.9 collective-permute-start.17
  114.0 4.0 %scatter_rows.3 = f32[4,1024,128]{2,1,0:T(8,128)} custom-call(s32[128,128]{1,0:T(8,128)S(1)} %copy-done.9, bf16[4096,128]{1,0:T(8,128)(2,1)S(1)} %bitcast.31, f32[4,1024,128]{2,1,0:T(8,128)} %scatter_rows.2.refs_0_), custom_call_target="tpu_custom_call", output_to_operand_aliasing={{}: (2, {})} | custom-call | flops 2147483648 | bytes 2000000 | tf_op jit(solution)/shard_map/scatter_rows/pallas_call | solution.py:276
  117.9 0.8 collective-permute-done.19.glob3
  118.8 2.2 %collective-permute-done.18.glob2 = bf16[128,512]{1,0:T(8,128)(2,1)S(1)} collective-permute-done((bf16[128,512]{1,0:T(8,128)(2,1)S(1)}, bf16[128,512]{1,0:T(8,128)(2,1)S(1)}, u32[]{:S(2)}, u32[]{:S(2)}) %collective-permute-start.18) | collective-permute-done | bytes 131104 | tf_op jit(solution)/shard_map/ppermute | solution.py:751
  120.9 1.3 %collective-permute-done.17.glob1 = bf16[128,512]{1,0:T(8,128)(2,1)S(1)} collective-permute-done((bf16[128,512]{1,0:T(8,128)(2,1)S(1)}, bf16[128,512]{1,0:T(8,128)(2,1)S(1)}, u32[]{:S(2)}, u32[]{:S(2)}) %collective-permute-start.17) | collective-permute-done | bytes 131104 | tf_op jit(solution)/shard_map/ppermute | solution.py:751
  122.2 1.8 %add_received.1 = (bf16[512,512]{1,0:T(8,128)(2,1)}, bf16[512,512]{1,0:T(8,128)(2,1)}) custom-call(s32[1,2]{1,0:T(1,128)} %gids.5, bf16[512,512]{1,0:T(8,128)(2,1)S(1)} %copy-done.7, bf16[512,512]{1,0:T(8,128)(2,1)S(1)} %copy-done.8, bf16[2,128,512]{2,1,0:T(8,128)(2,1)S(1)} %collective-permute-done.13.edge, bf16[128,512]{1,0:T(8,128)(2,1)S(1)} %add_convert_fusion.glob0, ...), custom_call_target="tpu_custom_call" | custom-call | flops 1000000 | bytes 3000000 | tf_op jit(solution)/shard_map/add_received/pallas_call | solution.py:729
  (17 shorter events, 0.0 us)
Async XLA Ops:
  2.3 8.8 %collective-permute-start = (bf16[128,512]{1,0:T(8,128)(2,1)S(1)}, bf16[128,512]{1,0:T(8,128)(2,1)S(1)}, u32[]{:S(2)}, u32[]{:S(2)}) collective-permute-start(bf16[128,512]{1,0:T(8,128)(2,1)S(1)} %get-tuple-element.73), channel_id=1, source_target_pairs={{0,8},{8,16},{16,24},{24,0},{32,40},{40,48},{48,56},{56,32},{64,72... | collective-permute-start | bytes 393224 | tf_op jit(solution)/shard_map/ppermute | solution.py:751
  3.9 9.4 %collective-permute-start.1 = (bf16[128,512]{1,0:T(8,128)(2,1)S(1)}, bf16[128,512]{1,0:T(8,128)(2,1)S(1)}, u32[]{:S(2)}, u32[]{:S(2)}) collective-permute-start(bf16[128,512]{1,0:T(8,128)(2,1)S(1)} %get-tuple-element.74), channel_id=1, source_target_pairs={{0,16},{8,24},{16,0},{24,8},{32,48},{40,56},{48,32},{56,40},{64,80... | collective-permute-start | bytes 393224 | tf_op jit(solution)/shard_map/ppermute | solution.py:751
  6.6 6.7 %collective-permute-start.2 = (bf16[128,512]{1,0:T(8,128)(2,1)S(1)}, bf16[128,512]{1,0:T(8,128)(2,1)S(1)}, u32[]{:S(2)}, u32[]{:S(2)}) collective-permute-start(bf16[128,512]{1,0:T(8,128)(2,1)S(1)} %get-tuple-element.75), channel_id=1, source_target_pairs={{0,24},{8,0},{16,8},{24,16},{32,56},{40,32},{48,40},{56,48},{64,88... | collective-permute-start | bytes 393224 | tf_op jit(solution)/shard_map/ppermute | solution.py:751
  10.6 9.4 %collective-permute-start.3 = (bf16[2,128,512]{2,1,0:T(8,128)(2,1)S(1)}, bf16[2,128,512]{2,1,0:T(8,128)(2,1)S(1)}, u32[]{:S(2)}, u32[]{:S(2)}) collective-permute-start(bf16[2,128,512]{2,1,0:T(8,128)(2,1)S(1)} %get-tuple-element.78), channel_id=1, source_target_pairs={{0,8},{8,16},{16,24},{24,32},{32,40},{40,48},{48,56},{56,64},{64,7... | collective-permute-start | bytes 786440 | tf_op jit(solution)/shard_map/ppermute | solution.py:742
  13.4 14.7 %collective-permute-start.6 = (bf16[128,512]{1,0:T(8,128)(2,1)S(1)}, bf16[128,512]{1,0:T(8,128)(2,1)S(1)}, u32[]{:S(2)}, u32[]{:S(2)}) collective-permute-start(bf16[128,512]{1,0:T(8,128)(2,1)S(1)} %add_convert_fusion.3), channel_id=1, source_target_pairs={{0,96},{8,104},{16,112},{24,120},{32,0},{40,8},{48,16},{56,24},{64... | collective-permute-start | bytes 393224 | tf_op jit(solution)/shard_map/ppermute | solution.py:755
  13.6 14.5 %collective-permute-start.5 = (bf16[128,512]{1,0:T(8,128)(2,1)S(1)}, bf16[128,512]{1,0:T(8,128)(2,1)S(1)}, u32[]{:S(2)}, u32[]{:S(2)}) collective-permute-start(bf16[128,512]{1,0:T(8,128)(2,1)S(1)} %add_convert_fusion.3), channel_id=1, source_target_pairs={{0,64},{8,72},{16,80},{24,88},{32,96},{40,104},{48,112},{56,120},{... | collective-permute-start | bytes 393224 | tf_op jit(solution)/shard_map/ppermute | solution.py:755
  16.9 11.3 %collective-permute-start.4 = (bf16[128,512]{1,0:T(8,128)(2,1)S(1)}, bf16[128,512]{1,0:T(8,128)(2,1)S(1)}, u32[]{:S(2)}, u32[]{:S(2)}) collective-permute-start(bf16[128,512]{1,0:T(8,128)(2,1)S(1)} %add_convert_fusion.3), channel_id=1, source_target_pairs={{0,32},{8,40},{16,48},{24,56},{32,64},{40,72},{48,80},{56,88},{64,... | collective-permute-start | bytes 393224 | tf_op jit(solution)/shard_map/ppermute | solution.py:755
  20.0 17.1 %all-to-all-start = ((s32[128,1,128]{2,1,0:T(1,128)}), s32[128,1,128]{2,1,0:T(1,128)S(1)}, u32[]{:S(2)}, u32[]{:S(2)}) async-start(s32[128,1,128]{2,1,0:T(1,128)} %bitcast.39), calls=%async_computation | async-start | bytes 131072 | tf_op jit(solution)/shard_map/all_to_all | solution.py:746
  28.2 15.4 %collective-permute-start.9 = (bf16[128,512]{1,0:T(8,128)(2,1)S(1)}, bf16[128,512]{1,0:T(8,128)(2,1)S(1)}, u32[]{:S(2)}, u32[]{:S(2)}) collective-permute-start(bf16[128,512]{1,0:T(8,128)(2,1)S(1)} %add_convert_fusion.2.glob0), channel_id=1, source_target_pairs={{0,24},{8,0},{16,8},{24,16},{32,56},{40,32},{48,40},{56,48},{64,88... | collective-permute-start | bytes 393224 | tf_op jit(solution)/shard_map/ppermute | solution.py:751
  31.0 12.6 %collective-permute-start.8 = (bf16[128,512]{1,0:T(8,128)(2,1)S(1)}, bf16[128,512]{1,0:T(8,128)(2,1)S(1)}, u32[]{:S(2)}, u32[]{:S(2)}) collective-permute-start(bf16[128,512]{1,0:T(8,128)(2,1)S(1)} %add_convert_fusion.2.glob0), channel_id=1, source_target_pairs={{0,16},{8,24},{16,0},{24,8},{32,48},{40,56},{48,32},{56,40},{64,80... | collective-permute-start | bytes 393224 | tf_op jit(solution)/shard_map/ppermute | solution.py:751
  31.8 11.8 %collective-permute-start.7 = (bf16[128,512]{1,0:T(8,128)(2,1)S(1)}, bf16[128,512]{1,0:T(8,128)(2,1)S(1)}, u32[]{:S(2)}, u32[]{:S(2)}) collective-permute-start(bf16[128,512]{1,0:T(8,128)(2,1)S(1)} %add_convert_fusion.2.glob0), channel_id=1, source_target_pairs={{0,8},{8,16},{16,24},{24,0},{32,40},{40,48},{48,56},{56,32},{64,72... | collective-permute-start | bytes 393224 | tf_op jit(solution)/shard_map/ppermute | solution.py:751
  43.6 5.1 %copy-start = (bf16[1,512,512]{2,1,0:T(8,128)(2,1)S(1)}, bf16[1,512,512]{2,1,0:T(8,128)(2,1)}, u32[]{:S(2)}) copy-start(bf16[1,512,512]{2,1,0:T(8,128)(2,1)} %param.11) | copy-start | bytes 1572868
  43.6 5.1 %copy-start.4 = (bf16[1,512,512]{2,1,0:T(8,128)(2,1)S(1)}, bf16[1,512,512]{2,1,0:T(8,128)(2,1)}, u32[]{:S(2)}) copy-start(bf16[1,512,512]{2,1,0:T(8,128)(2,1)} %param.12) | copy-start | bytes 1572868
  43.6 5.1 %copy-start.5 = (bf16[1,512,512]{2,1,0:T(8,128)(2,1)S(1)}, bf16[1,512,512]{2,1,0:T(8,128)(2,1)}, u32[]{:S(2)}) copy-start(bf16[1,512,512]{2,1,0:T(8,128)(2,1)} %param.13) | copy-start | bytes 1572868
  43.7 23.9 %all-to-all-start.1 = ((bf16[128,32,128]{2,1,0:T(8,128)(2,1)}), bf16[128,32,128]{2,1,0:T(8,128)(2,1)S(1)}, u32[]{:S(2)}, u32[]{:S(2)}) async-start(bf16[128,32,128]{2,1,0:T(8,128)(2,1)} %bitcast.35), calls=%async_computation.1 | async-start | bytes 2097152 | tf_op jit(solution)/shard_map/all_to_all | solution.py:746
  73.7 25.2 %all-to-all-start.2 = ((bf16[128,32,128]{2,1,0:T(8,128)(2,1)}), bf16[128,32,128]{2,1,0:T(8,128)(2,1)S(1)}, u32[]{:S(2)}, u32[]{:S(2)}) async-start(bf16[128,32,128]{2,1,0:T(8,128)(2,1)} %bitcast.34), calls=%async_computation.2 | async-start | bytes 2097152 | tf_op jit(solution)/shard_map/all_to_all | solution.py:746
  78.6 11.3 %copy-start.1 = (bf16[1,512,512]{2,1,0:T(8,128)(2,1)S(1)}, bf16[1,512,512]{2,1,0:T(8,128)(2,1)}, u32[]{:S(2)}) copy-start(bf16[1,512,512]{2,1,0:T(8,128)(2,1)} %param.11) | copy-start | bytes 1572868
  78.6 11.3 %copy-start.2 = (bf16[8,512,256]{2,1,0:T(8,128)(2,1)S(1)}, bf16[8,512,256]{2,1,0:T(8,128)(2,1)}, u32[]{:S(2)}) copy-start(bf16[8,512,256]{2,1,0:T(8,128)(2,1)} %get-tuple-element.98.probs) | copy-start | bytes 6291460
  78.6 11.3 %copy-start.3 = (bf16[8,512,256]{2,1,0:T(8,128)(2,1)S(1)}, bf16[8,512,256]{2,1,0:T(8,128)(2,1)}, u32[]{:S(2)}) copy-start(bf16[8,512,256]{2,1,0:T(8,128)(2,1)} %get-tuple-element.99.slope) | copy-start | bytes 6291460
  78.6 11.3 %copy-start.6 = (bf16[512,512]{1,0:T(8,128)(2,1)S(1)}, bf16[512,512]{1,0:T(8,128)(2,1)}, u32[]{:S(2)}) copy-start(bf16[512,512]{1,0:T(8,128)(2,1)} %get-tuple-element.97.grad) | copy-start | bytes 1572868
  84.1 11.7 %collective-permute-start.10 = (bf16[128,512]{1,0:T(8,128)(2,1)S(1)}, bf16[128,512]{1,0:T(8,128)(2,1)S(1)}, u32[]{:S(2)}, u32[]{:S(2)}) collective-permute-start(bf16[128,512]{1,0:T(8,128)(2,1)S(1)} %get-tuple-element.106), channel_id=1, source_target_pairs={{0,8},{8,16},{16,24},{24,0},{32,40},{40,48},{48,56},{56,32},{64,72... | collective-permute-start | bytes 393224 | tf_op jit(solution)/shard_map/ppermute | solution.py:751
  85.7 13.1 %collective-permute-start.11 = (bf16[128,512]{1,0:T(8,128)(2,1)S(1)}, bf16[128,512]{1,0:T(8,128)(2,1)S(1)}, u32[]{:S(2)}, u32[]{:S(2)}) collective-permute-start(bf16[128,512]{1,0:T(8,128)(2,1)S(1)} %get-tuple-element.107), channel_id=1, source_target_pairs={{0,16},{8,24},{16,0},{24,8},{32,48},{40,56},{48,32},{56,40},{64,80... | collective-permute-start | bytes 393224 | tf_op jit(solution)/shard_map/ppermute | solution.py:751
  88.4 10.4 %collective-permute-start.12 = (bf16[128,512]{1,0:T(8,128)(2,1)S(1)}, bf16[128,512]{1,0:T(8,128)(2,1)S(1)}, u32[]{:S(2)}, u32[]{:S(2)}) collective-permute-start(bf16[128,512]{1,0:T(8,128)(2,1)S(1)} %get-tuple-element.108), channel_id=1, source_target_pairs={{0,24},{8,0},{16,8},{24,16},{32,56},{40,32},{48,40},{56,48},{64,88... | collective-permute-start | bytes 393224 | tf_op jit(solution)/shard_map/ppermute | solution.py:751
  89.9 14.3 %copy-start.9 = (s32[128,128]{1,0:T(8,128)S(1)}, s32[128,128]{1,0:T(8,128)}, u32[]{:S(2)}) copy-start(s32[128,128]{1,0:T(8,128)} %get-tuple-element.112.asked) | copy-start | bytes 196612
  94.1 28.1 %collective-permute-start.13 = (bf16[2,128,512]{2,1,0:T(8,128)(2,1)S(1)}, bf16[2,128,512]{2,1,0:T(8,128)(2,1)S(1)}, u32[]{:S(2)}, u32[]{:S(2)}) collective-permute-start(bf16[2,128,512]{2,1,0:T(8,128)(2,1)S(1)} %get-tuple-element.111), channel_id=1, source_target_pairs={{0,120},{8,0},{16,8},{24,16},{32,24},{40,32},{48,40},{56,48},{64,5... | collective-permute-start | bytes 786440 | tf_op jit(solution)/shard_map/ppermute | solution.py:742
  98.9 9.3 %collective-permute-start.16 = (bf16[128,512]{1,0:T(8,128)(2,1)S(1)}, bf16[128,512]{1,0:T(8,128)(2,1)S(1)}, u32[]{:S(2)}, u32[]{:S(2)}) collective-permute-start(bf16[128,512]{1,0:T(8,128)(2,1)S(1)} %add_convert_fusion.1), channel_id=1, source_target_pairs={{0,96},{8,104},{16,112},{24,120},{32,0},{40,8},{48,16},{56,24},{64... | collective-permute-start | bytes 393224 | tf_op jit(solution)/shard_map/ppermute | solution.py:755
  99.2 8.9 %collective-permute-start.15 = (bf16[128,512]{1,0:T(8,128)(2,1)S(1)}, bf16[128,512]{1,0:T(8,128)(2,1)S(1)}, u32[]{:S(2)}, u32[]{:S(2)}) collective-permute-start(bf16[128,512]{1,0:T(8,128)(2,1)S(1)} %add_convert_fusion.1), channel_id=1, source_target_pairs={{0,64},{8,72},{16,80},{24,88},{32,96},{40,104},{48,112},{56,120},{... | collective-permute-start | bytes 393224 | tf_op jit(solution)/shard_map/ppermute | solution.py:755
  102.1 6.5 %collective-permute-start.14 = (bf16[128,512]{1,0:T(8,128)(2,1)S(1)}, bf16[128,512]{1,0:T(8,128)(2,1)S(1)}, u32[]{:S(2)}, u32[]{:S(2)}) collective-permute-start(bf16[128,512]{1,0:T(8,128)(2,1)S(1)} %add_convert_fusion.1), channel_id=1, source_target_pairs={{0,32},{8,40},{16,48},{24,56},{32,64},{40,72},{48,80},{56,88},{64,... | collective-permute-start | bytes 393224 | tf_op jit(solution)/shard_map/ppermute | solution.py:755
  108.7 13.5 %copy-start.7 = (bf16[512,512]{1,0:T(8,128)(2,1)S(1)}, bf16[512,512]{1,0:T(8,128)(2,1)}, u32[]{:S(2)}) copy-start(bf16[512,512]{1,0:T(8,128)(2,1)} %get-tuple-element.109.d_k) | copy-start | bytes 1572868
  108.7 13.5 %copy-start.8 = (bf16[512,512]{1,0:T(8,128)(2,1)S(1)}, bf16[512,512]{1,0:T(8,128)(2,1)}, u32[]{:S(2)}) copy-start(bf16[512,512]{1,0:T(8,128)(2,1)} %get-tuple-element.110.d_v) | copy-start | bytes 1572868
  108.7 10.0 %collective-permute-start.19 = (bf16[128,512]{1,0:T(8,128)(2,1)S(1)}, bf16[128,512]{1,0:T(8,128)(2,1)S(1)}, u32[]{:S(2)}, u32[]{:S(2)}) collective-permute-start(bf16[128,512]{1,0:T(8,128)(2,1)S(1)} %add_convert_fusion.glob0), channel_id=1, source_target_pairs={{0,24},{8,0},{16,8},{24,16},{32,56},{40,32},{48,40},{56,48},{64,88... | collective-permute-start | bytes 393224 | tf_op jit(solution)/shard_map/ppermute | solution.py:751
  113.0 7.9 %collective-permute-start.18 = (bf16[128,512]{1,0:T(8,128)(2,1)S(1)}, bf16[128,512]{1,0:T(8,128)(2,1)S(1)}, u32[]{:S(2)}, u32[]{:S(2)}) collective-permute-start(bf16[128,512]{1,0:T(8,128)(2,1)S(1)} %add_convert_fusion.glob0), channel_id=1, source_target_pairs={{0,16},{8,24},{16,0},{24,8},{32,48},{40,56},{48,32},{56,40},{64,80... | collective-permute-start | bytes 393224 | tf_op jit(solution)/shard_map/ppermute | solution.py:751
  113.0 9.2 %collective-permute-start.17 = (bf16[128,512]{1,0:T(8,128)(2,1)S(1)}, bf16[128,512]{1,0:T(8,128)(2,1)S(1)}, u32[]{:S(2)}, u32[]{:S(2)}) collective-permute-start(bf16[128,512]{1,0:T(8,128)(2,1)S(1)} %add_convert_fusion.glob0), channel_id=1, source_target_pairs={{0,8},{8,16},{16,24},{24,0},{32,40},{40,48},{48,56},{56,32},{64,72... | collective-permute-start | bytes 393224 | tf_op jit(solution)/shard_map/ppermute | solution.py:751

commit v4 on v3

--- a/solution.py
+++ b/solution.py
@@ -192,12 +192,12 @@
     ]
     for load in loads:
         load.start()
-    keep = pltpu.make_async_copy(asked, kept, sems.at[HI + 4])
+    keep = pltpu.make_async_copy(asked, kept, sems.at[HI + 8])
     keep.start()
     columns = slot_columns(slot_rows(asked, NDEV // 4))
     lo = columns & (LO - 1)
     hi = columns >> (LO.bit_length() - 1)
-    group = 8
+    group = 4
     size = group * E
     lane = iota((size, E), 1)
     sends = []
@@ -234,7 +234,7 @@
         scratch_shapes=[
             pltpu.VMEM((ROWS, E), BF),
             pltpu.VMEM((NDEV * SLOTS, E), BF),
-            pltpu.SemaphoreType.DMA((HI + 5,)),
+            pltpu.SemaphoreType.DMA((HI + 9,)),
         ],
         compiler_params=params(),
         cost_estimate=pl.CostEstimate(
@@ -244,24 +244,28 @@
     )(*in_vmem(asked), *in_hbm(table))
 
 
-HALVES = 2
-
-
-def scatter_kernel(half, asked, incoming, *refs):
+PORTION = LO // 2
+
+
+def scatter_kernel(start, asked, incoming, *refs):
     grad, spread = refs[-2:]
+    step = pl.program_id(0)
     rows = slot_rows(asked, NDEV // 4)
-    hi = slot_columns(rows) >> (LO.bit_length() - 1)
-    group = 2
-    size = group * E
-    for first in range(0, NDEV // 4, group):
-        high = spread_columns(hi, first, group)
-        part = incoming[first * E : first * E + size, :].astype(F32)
-        for h in range(HI):
-            spread[first * E : first * E + size, h * E : (h + 1) * E] = jnp.where(
-                high == h, part, 0.0
-            ).astype(BF)
-    size = LO // HALVES
-    sub = iota((size, E), 0) + half * size
+    @pl.when(step == 0)
+    def _():
+        hi = slot_columns(rows) >> (LO.bit_length() - 1)
+        group = 2
+        size = group * E
+        for first in range(0, NDEV // 4, group):
+            high = spread_columns(hi, first, group)
+            part = incoming[first * E : first * E + size, :].astype(F32)
+            for h in range(HI):
+                spread[first * E : first * E + size, h * E : (h + 1) * E] = jnp.where(
+                    high == h, part, 0.0
+                ).astype(BF)
+
+    size = PORTION
+    sub = iota((size, E), 0) + (start + step) * size
     lo = rows & (LO - 1)
     onehot = jnp.concatenate(
         [jnp.where(sub == lo[i : i + 1, :], 1.0, 0.0).astype(BF) for i in range(NDEV // 4)], axis=1
@@ -271,14 +275,14 @@
         grad[h] = total[:, h * E : (h + 1) * E]
 
 
-def scatter(half, asked, incoming, before=()):
+def scatter(start, steps, asked, incoming, before=()):
     count = NDEV * SLOTS
     return pl.pallas_call(
-        functools.partial(scatter_kernel, half),
-        grid=(1,),
+        functools.partial(scatter_kernel, start),
+        grid=(steps,),
         out_shape=slow((HI, LO, E), F32),
         in_specs=[whole((NDEV, E)), whole((count, E))] + [ANY_SPEC] * len(before),
-        out_specs=pl.BlockSpec((HI, LO // HALVES, E), lambda i: (0, half, 0)),
+        out_specs=pl.BlockSpec((HI, PORTION, E), lambda i: (0, start + i, 0)),
         scratch_shapes=[pltpu.VMEM((count, HI * E), BF)],
         input_output_aliases={2 + i: i for i in range(len(before))},
         compiler_params=params(),
@@ -396,7 +400,7 @@
             var = jnp.mean(centered * centered, axis=1, keepdims=True)
             inv = lax.rsqrt(var + 1e-05)
             normed = centered * inv
-            normed_out[rows, :] = normed
+            normed_out[rows, :] = normed.astype(BF)
             inv_out[rows, :] = inv
             gated = (normed * gate[rows, :].astype(F32)).astype(BF)
             user[rows, :] = (dot(gated, w_out[...]) + history[rows, :].astype(F32)).astype(BF)
@@ -439,7 +443,7 @@
         out_shape=(
             SQUARE,
             SQUARE,
-            slow((EVENTS, D), F32),
+            slow((EVENTS, D), BF),
             slow((EVENTS, 1), F32),
             slow((EVENTS, E), BF),
         ),
@@ -468,13 +472,66 @@
 
 
 def far_backward_kernel(
-    q, glob0, glob1, glob2, glob3, grad, probs, slope, d_q, out0, out1, out2, out3, scratch
+    d_user,
+    w_out,
+    inv,
+    normed,
+    gate,
+    q,
+    glob0,
+    glob1,
+    glob2,
+    glob3,
+    probs,
+    slope,
+    d_q,
+    out0,
+    out1,
+    out2,
+    out3,
+    attn_far,
+    gate_far,
+    scratch,
+    d_attn,
+    d_gate,
+    sems,
 ):
+    pair = pl.program_id(0)
+    width = 2 * HEAD_DIM
+    copies = [
+        pltpu.make_async_copy(
+            d_attn.at[p], attn_far.at[:, p * width : (p + 1) * width], sems.at[p]
+        )
+        for p in range(PAIRS)
+    ] + [pltpu.make_async_copy(d_gate, gate_far, sems.at[PAIRS])]
+
+    @pl.when(pair == 0)
+    def _():
+        step = 128
+        for r in range(0, EVENTS, step):
+            rows = slice(r, r + step)
+            d_gated = dot_nt(d_user[rows, :], w_out[...])
+            n = normed[rows, :].astype(F32)
+            d_gate[rows, :] = (d_gated * n).astype(BF)
+            dn = d_gated * gate[rows, :].astype(F32)
+            result = (
+                (
+                    dn
+                    - jnp.mean(dn, axis=1, keepdims=True)
+                    - n * jnp.mean(dn * n, axis=1, keepdims=True)
+                )
+                * inv[rows, :]
+            ).astype(BF)
+            for p in range(PAIRS):
+                d_attn[p, rows, :] = result[:, p * width : (p + 1) * width]
+        for copy in copies:
+            copy.start()
+
     masks = head_masks()
     sixteenth = jnp.asarray(1.0 / 16.0, BF)
     q16 = q[...] * sixteenth
     kg, vg = unrotate((glob0, glob1, glob2, glob3), scratch)
-    do = grad[...]
+    do = d_attn[pair]
     q_t = jnp.concatenate([(q16 * m).T for m in masks], axis=1)
     do_t = jnp.concatenate([(do * m).T for m in masks], axis=1)
     kg_both = jnp.concatenate([kg * (m * sixteenth) for m in masks], axis=0)
@@ -491,25 +548,40 @@
     for d, out in enumerate((out0, out1, out2, out3)):
         out[...] = scratch[chunk_of(d)]
 
-
-def far_backward(q, glob, grad, probs, slope):
+    @pl.when(pair == PAIRS - 1)
+    def _():
+        for copy in copies:
+            copy.wait()
+
+
+def far_backward(d_user, w_out, inv, normed, gate, q, glob, probs, slope):
     return pl.pallas_call(
         far_backward_kernel,
         grid=(PAIRS,),
         out_shape=(fast((EVENTS, D), F32),)
-        + (jax.ShapeDtypeStruct((BLK, D), BF),) * CHUNKS,
-        in_specs=[pair_block(EVENTS)]
+        + (jax.ShapeDtypeStruct((BLK, D), BF),) * CHUNKS
+        + (slow((EVENTS, D), BF),) * 2,
+        in_specs=[
+            whole((EVENTS, E)),
+            whole((D, E)),
+            whole((EVENTS, 1)),
+            whole((EVENTS, D)),
+            whole((EVENTS, D)),
+            pair_block(EVENTS),
+        ]
         + [pair_block(BLK)] * CHUNKS
-        + [pair_block(EVENTS)]
         + [head_block()] * 2,
-        out_specs=[pair_block(EVENTS)] + [pair_block(BLK)] * CHUNKS,
-        scratch_shapes=[pltpu.VMEM((CHUNKS, BLK, 2 * HEAD_DIM), BF)],
-        compiler_params=params(),
-        cost_estimate=pl.CostEstimate(
-            flops=10**9, bytes_accessed=7 * 10**6, transcendentals=0
-        ),
+        out_specs=[pair_block(EVENTS)] + [pair_block(BLK)] * CHUNKS + [ANY_SPEC] * 2,
+        scratch_shapes=[
+            pltpu.VMEM((CHUNKS, BLK, 2 * HEAD_DIM), BF),
+            pltpu.VMEM((PAIRS, EVENTS, 2 * HEAD_DIM), BF),
+            pltpu.VMEM((EVENTS, D), BF),
+            pltpu.SemaphoreType.DMA((PAIRS + 1,)),
+        ],
+        compiler_params=params(),
+        cost_estimate=pl.CostEstimate(flops=10**9, bytes_accessed=7 * 10**6, transcendentals=0),
         name="far_backward",
-    )(*in_hbm(q), *glob, *in_hbm(grad, probs, slope))
+    )(*in_hbm(d_user, w_out, inv, normed, gate, q), *glob, *in_hbm(probs, slope))
 
 
 def near_backward_kernel(q, k, v, halo, grad, probs, slope, far, d_q, d_k, d_v, edge):
@@ -577,53 +649,20 @@
             flops=10**9, bytes_accessed=9 * 10**6, transcendentals=0
         ),
         name="near_backward",
-    )(q, k, v, halo, grad, probs, slope, *in_vmem(far))
+    )(q, k, v, halo, *in_hbm(grad), probs, slope, *in_vmem(far))
 
 
 def middle_kernel(
-    lengths,
-    items,
-    code,
-    user,
-    normed_far,
-    gate_far,
-    inv_far,
-    w_far,
-    out_far,
-    attn_far,
-    gated_far,
-    score,
-    normed,
-    gate,
-    inv,
-    w_out,
-    outgoing,
-    d_attn,
-    d_gate,
-    sems,
+    lengths, items, code, user, out_far, d_user, score, share, outgoing, sems
 ):
-    loads = [
-        pltpu.make_async_copy(normed_far, normed, sems.at[0]),
-        pltpu.make_async_copy(gate_far, gate, sems.at[1]),
-        pltpu.make_async_copy(inv_far, inv, sems.at[2]),
-        pltpu.make_async_copy(w_far, w_out, sems.at[3]),
-    ]
-    for load in loads:
-        load.start()
     sends = []
-
-    def send(near, far, rows):
-        copy = pltpu.make_async_copy(near.at[rows, :], far.at[rows, :], sems.at[4 + len(sends)])
-        copy.start()
-        sends.append(copy)
-
     portion = NDEV * SLOTS // 4
     user_b = user[...]
     user_t = user_b.T
     mark = code[...].astype(F32)
     first = mark >= FIRST
     rank = jnp.where(first, mark - FIRST, mark)
-    group = 8
+    group = 16
     size = group * SLOTS
     slot = iota((SLOTS, EVENTS), 0).astype(F32)
     for d in range(0, NDEV, group):
@@ -638,8 +677,8 @@
     other = (rank >= 0.0) & jnp.logical_not(first)
     side = jnp.where(other, jax.nn.sigmoid(score[...] - score0), 0.0) * valid
     coef = jnp.where(first, -jnp.sum(side, axis=0, keepdims=True), side)
-    d_user_t = jnp.zeros((E, EVENTS), F32)
     for d in range(0, NDEV, group):
+        rows = slice(d * SLOTS, d * SLOTS + size)
         c = jnp.concatenate(
             [
                 jnp.where(rank[r : r + 1, :] == slot, coef[r : r + 1, :], 0.0).astype(BF)
@@ -647,62 +686,39 @@
             ],
             axis=0,
         )
-        rows = slice(d * SLOTS, d * SLOTS + size)
+        share[rows, :] = c
         outgoing[rows, :] = dot(c, user_b).astype(BF)
-        d_user_t = d_user_t + dot_tn(items[rows, :], c)
         if rows.stop % portion == 0:
-            send(outgoing, out_far, slice(rows.stop - portion, rows.stop))
-    d_user = d_user_t.T.astype(BF)
-    for load in loads:
-        load.wait()
-    step = 128
-    for r in range(0, EVENTS, step):
-        rows = slice(r, r + step)
-        d_gated = dot_nt(d_user[rows], w_out[...])
-        n = normed[rows, :]
-        d_gate[rows, :] = (d_gated * n).astype(BF)
-        dn = d_gated * gate[rows, :].astype(F32)
-        d_attn[rows, :] = (
-            (
-                dn
-                - jnp.mean(dn, axis=1, keepdims=True)
-                - n * jnp.mean(dn * n, axis=1, keepdims=True)
+            part = slice(rows.stop - portion, rows.stop)
+            sends.append(
+                pltpu.make_async_copy(
+                    outgoing.at[part, :], out_far.at[part, :], sems.at[len(sends)]
+                )
             )
-            * inv[rows, :]
-        ).astype(BF)
-        send(d_attn, attn_far, rows)
-        send(d_gate, gated_far, rows)
+            sends[-1].start()
+    d_user[...] = dot_tn(items[...], share[...]).T.astype(BF)
     for copy in sends:
         copy.wait()
 
 
-def middle(lengths, items, code, user, normed, inv, gate, w_out):
+def middle(lengths, items, code, user):
     return pl.pallas_call(
         middle_kernel,
-        out_shape=(
-            slow((NDEV * SLOTS, E), BF),
-            slow((EVENTS, D), BF),
-            slow((EVENTS, D), BF),
-        ),
-        in_specs=[SMEM_SPEC] + [VMEM_SPEC] * 3 + [ANY_SPEC] * 4,
-        out_specs=[ANY_SPEC] * 3,
+        out_shape=(slow((NDEV * SLOTS, E), BF), slow((EVENTS, E), BF)),
+        in_specs=[SMEM_SPEC] + [VMEM_SPEC] * 3,
+        out_specs=[ANY_SPEC, VMEM_SPEC],
         scratch_shapes=[
             pltpu.VMEM((NDEV, EVENTS), F32),
-            pltpu.VMEM((EVENTS, D), F32),
-            pltpu.VMEM((EVENTS, D), BF),
-            pltpu.VMEM((EVENTS, 1), F32),
-            pltpu.VMEM((D, E), BF),
+            pltpu.VMEM((NDEV * SLOTS, EVENTS), BF),
             pltpu.VMEM((NDEV * SLOTS, E), BF),
-            pltpu.VMEM((EVENTS, D), BF),
-            pltpu.VMEM((EVENTS, D), BF),
-            pltpu.SemaphoreType.DMA((4 + 4 + 2 * EVENTS // 128,)),
+            pltpu.SemaphoreType.DMA((4,)),
         ],
         compiler_params=params(),
         cost_estimate=pl.CostEstimate(
             flops=2 * 10**9, bytes_accessed=6 * 10**6, transcendentals=10**5
         ),
         name="ranking",
-    )(*in_hbm(lengths), *in_vmem(items), *in_hbm(code, user, normed, gate, inv, w_out))
+    )(*in_hbm(lengths), *in_vmem(items), *in_hbm(code, user))
 
 
 def finish_kernel(gids, d_k, d_v, edge, glob0, glob1, glob2, glob3, key_out, value_out):
@@ -802,20 +818,22 @@
     far_p, far_f, normed, inv, user = far_forward(
         lengths, gids, q, glob, near, gate[0], history[0], w_out
     )
-    outgoing, d_attn, d_gate = middle(lengths, items, code, user, normed, inv, gate[0], w_out)
+    outgoing, d_user = middle(lengths, items, code, user)
     incoming = exchange(outgoing.reshape(NDEV, SLOTS, E), ("seq", "user"))
-    far_q, *d_glob = far_backward(q, glob, d_attn, far_p, far_f)
+    far_q, *d_glob, d_attn, d_gate = far_backward(
+        d_user, w_out, inv, normed, gate[0], q, glob, far_p, far_f
+    )
     parts = from_x(d_glob)
     d_q, d_k, d_v, edge = near_backward(q, k, v, halo, d_attn, near_p, near_f, far_q)
     d_k, *parts = together(d_k, *parts)
     mine = add_all(parts)
     back = from_behind(edge, "seq", -1)
     incoming, mine = together(incoming.reshape(NDEV * SLOTS, E), mine)
-    grad = scatter(0, asked, incoming)
+    grad = scatter(0, 1, asked, incoming)
     grad, *parts = together(grad, *from_z(mine))
     mine = add_all(parts)
     grad, mine = together(grad, mine)
-    grad = scatter(1, asked, incoming, (grad,))
+    grad = scatter(1, 1, asked, incoming, (grad,))
     grad, *total = together(grad, *share_x(mine))
     d_key, d_value = finish(gids, d_k, d_v, back, total)
     return (d_q[None], d_key[None], d_value[None], d_gate[None], grad.reshape(ROWS, E))

time: 124 us -> 124 us (level)
  waiting for transfers between devices: 24.6 us -> 23 us
    ppermute x12, waiting for transfers between devices: 11.1 us -> 9.09 us  [around_x(): return lax.ppermute(x, 'seq', pairs)]
  transfers between devices with their start and end apart: 23 -> 23, of which waited for: 10 -> 9; matrix products, arithmetic and copies ran while one was open for 0% -> 0% of each run, Pallas kernels for 30% -> 32%
where the time goes in v4:
time: 124 us
  starting transfers between devices  51.1 us (41%)
  Pallas kernels  48.3 us (39%)
  waiting for transfers between devices  23 us (19%)
    ppermute x12, starting transfers between devices, around_x(): return lax.ppermute(x, 'seq', pairs)  21.5 us
    all_to_all x3, starting transfers between devices, exchange(): return lax.all_to_all(x, axis, split_axis=0, concat_axis=0, tiled=True)  17.9 us
    all_to_all x3, waiting for transfers between devices, exchange(): return lax.all_to_all(x, axis, split_axis=0, concat_axis=0, tiled=True)  12.4 us
    ppermute x6, starting transfers between devices, around_z(): lax.ppermute(x, 'seq', [(i, (i + distance * XSIZE) % NSEQ) for i in range...  11.1 us
    ppermute x12, waiting for transfers between devices, around_x(): return lax.ppermute(x, 'seq', pairs)  9.09 us
    pallas_call x2, Pallas kernels, scatter(): pl.pallas_call(functools.partial(scatter_kernel, start), grid=(steps,), o...  7.96 us
    pallas_call x1, Pallas kernels, far_backward(): pl.pallas_call(far_backward_kernel, grid=(PAIRS,), out_shape=(fast((EVENT...  6.61 us
    pallas_call x1, Pallas kernels, gather(): pl.pallas_call(gather_kernel, out_shape=(slow((NDEV * SLOTS, E), BF), slo...  6.48 us
  transfers between devices with their start and end apart: 23, of which 9 were waited for; matrix products, arithmetic and copies ran while one was open for 0% of the time, Pallas kernels for 32%

profile of v4, /device:TPU:32, one launch (start us, length us, event | category | flops | bytes accessed | tf_op | source)
XLA Modules:
  0.0 123.6 jit_solution(14697150595829636878)
XLA Ops:
  0.6 1.7 %pieces.1 = (bf16[2,128,512]{2,1,0:T(8,128)(2,1)S(1)}, bf16[128,512]{1,0:T(8,128)(2,1)S(1)}, bf16[128,512]{1,0:T(8,128)(2,1)S(1)}, bf16[128,512]{1,0:T(8,128)(2,1)S(1)}, bf16[128,512]{1,0:T(8,128)(2,1)S(1)}) custom-call(s32[1,2]{1,0:T(1,128)} %gids.5, bf16[512,512]{1,0:T(8,128)(2,1)} %bitcast.24, bf16[512,512]{1,0:T(8,128)(2,1)} %bitcast.27), custom_call_target="tpu_custom_call" | custom-call | flops 1000000 | bytes 2000000 | tf_op jit(solution)/shard_map/pieces/pallas_call | solution.py:121
  2.3 1.6 %collective-permute-start = (bf16[128,512]{1,0:T(8,128)(2,1)S(1)}, bf16[128,512]{1,0:T(8,128)(2,1)S(1)}, u32[]{:S(2)}, u32[]{:S(2)}) collective-permute-start(bf16[128,512]{1,0:T(8,128)(2,1)S(1)} %get-tuple-element.74), channel_id=1, source_target_pairs={{0,8},{8,16},{16,24},{24,0},{32,40},{40,48},{48,56},{56,32},{64,72... | collective-permute-start | bytes 393224 | tf_op jit(solution)/shard_map/ppermute | solution.py:767
  3.9 2.7 %collective-permute-start.1 = (bf16[128,512]{1,0:T(8,128)(2,1)S(1)}, bf16[128,512]{1,0:T(8,128)(2,1)S(1)}, u32[]{:S(2)}, u32[]{:S(2)}) collective-permute-start(bf16[128,512]{1,0:T(8,128)(2,1)S(1)} %get-tuple-element.75), channel_id=1, source_target_pairs={{0,16},{8,24},{16,0},{24,8},{32,48},{40,56},{48,32},{56,40},{64,80... | collective-permute-start | bytes 393224 | tf_op jit(solution)/shard_map/ppermute | solution.py:767
  6.6 1.4 %collective-permute-start.2 = (bf16[128,512]{1,0:T(8,128)(2,1)S(1)}, bf16[128,512]{1,0:T(8,128)(2,1)S(1)}, u32[]{:S(2)}, u32[]{:S(2)}) collective-permute-start(bf16[128,512]{1,0:T(8,128)(2,1)S(1)} %get-tuple-element.76), channel_id=1, source_target_pairs={{0,24},{8,0},{16,8},{24,16},{32,56},{40,32},{48,40},{56,48},{64,88... | collective-permute-start | bytes 393224 | tf_op jit(solution)/shard_map/ppermute | solution.py:767
  8.1 2.5 %route.1 = (s32[128,128]{1,0:T(8,128)}, bf16[128,512]{1,0:T(8,128)(2,1)}) custom-call(s32[5,1,512]{2,1,0:T(1,128)} %bitcast.44, s32[5,1,512]{2,1,0:T(1,128)} %bitcast.45), custom_call_target="tpu_custom_call" | custom-call | flops 100000000 | bytes 1000000 | tf_op jit(solution)/shard_map/route/pallas_call | solution.py:154
  10.6 0.6 collective-permute-start.3
  11.2 0.0 collective-permute-done
  11.2 2.0 %collective-permute-done.1 = bf16[128,512]{1,0:T(8,128)(2,1)S(1)} collective-permute-done((bf16[128,512]{1,0:T(8,128)(2,1)S(1)}, bf16[128,512]{1,0:T(8,128)(2,1)S(1)}, u32[]{:S(2)}, u32[]{:S(2)}) %collective-permute-start.1) | collective-permute-done | bytes 131104 | tf_op jit(solution)/shard_map/ppermute | solution.py:767
  13.2 0.0 collective-permute-done.2
  13.2 0.1 add_convert_fusion.3
  13.2 0.3 collective-permute-start.6
  13.6 3.3 %collective-permute-start.5 = (bf16[128,512]{1,0:T(8,128)(2,1)S(1)}, bf16[128,512]{1,0:T(8,128)(2,1)S(1)}, u32[]{:S(2)}, u32[]{:S(2)}) collective-permute-start(bf16[128,512]{1,0:T(8,128)(2,1)S(1)} %add_convert_fusion.3), channel_id=1, source_target_pairs={{0,64},{8,72},{16,80},{24,88},{32,96},{40,104},{48,112},{56,120},{... | collective-permute-start | bytes 393224 | tf_op jit(solution)/shard_map/ppermute | solution.py:771
  16.9 2.2 %collective-permute-start.4 = (bf16[128,512]{1,0:T(8,128)(2,1)S(1)}, bf16[128,512]{1,0:T(8,128)(2,1)S(1)}, u32[]{:S(2)}, u32[]{:S(2)}) collective-permute-start(bf16[128,512]{1,0:T(8,128)(2,1)S(1)} %add_convert_fusion.3), channel_id=1, source_target_pairs={{0,32},{8,40},{16,48},{24,56},{32,64},{40,72},{48,80},{56,88},{64,... | collective-permute-start | bytes 393224 | tf_op jit(solution)/shard_map/ppermute | solution.py:771
  19.1 1.0 collective-permute-done.3.halo
  20.1 7.9 %all-to-all-start = ((s32[128,1,128]{2,1,0:T(1,128)}), s32[128,1,128]{2,1,0:T(1,128)S(1)}, u32[]{:S(2)}, u32[]{:S(2)}) async-start(s32[128,1,128]{2,1,0:T(1,128)} %bitcast.39), calls=%async_computation | async-start | bytes 131072 | tf_op jit(solution)/shard_map/all_to_all | solution.py:762
  28.1 0.0 collective-permute-done.6
  28.1 0.0 collective-permute-done.5
  28.1 0.0 collective-permute-done.4
  28.1 0.1 add_convert_fusion.2.glob0
  28.2 2.8 %collective-permute-start.9 = (bf16[128,512]{1,0:T(8,128)(2,1)S(1)}, bf16[128,512]{1,0:T(8,128)(2,1)S(1)}, u32[]{:S(2)}, u32[]{:S(2)}) collective-permute-start(bf16[128,512]{1,0:T(8,128)(2,1)S(1)} %add_convert_fusion.2.glob0), channel_id=1, source_target_pairs={{0,24},{8,0},{16,8},{24,16},{32,56},{40,32},{48,40},{56,48},{64,88... | collective-permute-start | bytes 393224 | tf_op jit(solution)/shard_map/ppermute | solution.py:767
  31.0 0.8 collective-permute-start.8
  31.8 0.9 collective-permute-start.7
  32.7 4.4 %all-to-all-done = s32[128,1,128]{2,1,0:T(1,128)S(1)} async-done(((s32[128,1,128]{2,1,0:T(1,128)}), s32[128,1,128]{2,1,0:T(1,128)S(1)}, u32[]{:S(2)}, u32[]{:S(2)}) %all-to-all-start) | async-done | bytes 65568 | tf_op jit(solution)/shard_map/all_to_all | solution.py:762
  37.1 6.5 %gather_rows.1 = (bf16[4096,128]{1,0:T(8,128)(2,1)}, s32[128,128]{1,0:T(8,128)}) custom-call(s32[128,128]{1,0:T(8,128)S(1)} %bitcast.33, bf16[4096,128]{1,0:T(8,128)(2,1)} %table_far.1), custom_call_target="tpu_custom_call" | custom-call | flops 4294967296 | bytes 2000000 | tf_op jit(solution)/shard_map/gather_rows/pallas_call | solution.py:229
  43.6 0.0 copy-start
  43.6 0.0 copy-start.4
  43.6 0.0 copy-start.5
  43.6 0.0 collective-permute-done.9.glob3
  43.6 0.0 collective-permute-done.8.glob2
  43.6 0.0 collective-permute-done.7.glob1
  43.6 5.0 %all-to-all-start.1 = ((bf16[128,32,128]{2,1,0:T(8,128)(2,1)}), bf16[128,32,128]{2,1,0:T(8,128)(2,1)S(1)}, u32[]{:S(2)}, u32[]{:S(2)}) async-start(bf16[128,32,128]{2,1,0:T(8,128)(2,1)} %bitcast.37), calls=%async_computation.1 | async-start | bytes 2097152 | tf_op jit(solution)/shard_map/all_to_all | solution.py:762
  48.7 4.6 %near_forward.1 = (bf16[8,512,256]{2,1,0:T(8,128)(2,1)}, bf16[8,512,256]{2,1,0:T(8,128)(2,1)}, f32[512,512]{1,0:T(8,128)S(1)}) custom-call(s32[8]{0:T(128)} %lengths.5, bf16[512,512]{1,0:T(8,128)(2,1)S(1)} %bitcast.21, bf16[512,512]{1,0:T(8,128)(2,1)S(1)} %bitcast.25, bf16[512,512]{1,0:T(8,128)(2,1)S(1)} %bitcast.28, ...), custom_call_target="tpu_custom_call" | custom-call | flops 500000000 | bytes 7000000 | tf_op jit(solution)/shard_map/near_forward/pallas_call | solution.py:425
  53.3 6.2 %far_forward.1 = (bf16[8,512,256]{2,1,0:T(8,128)(2,1)}, bf16[8,512,256]{2,1,0:T(8,128)(2,1)}, bf16[512,512]{1,0:T(8,128)(2,1)}, f32[512,1]{1,0:T(8,128)}, bf16[512,128]{1,0:T(8,128)(2,1)}) custom-call(s32[8]{0:T(128)} %lengths.5, s32[1,2]{1,0:T(1,128)} %gids.5, bf16[512,512]{1,0:T(8,128)(2,1)S(1)} %bitcast.22, bf16[128,512]{1,0:T(8,128)(2,1)S(1)} %add_convert_fusion.2.glob0, ...), custom_call_target="tpu_custom_call" | custom-call | flops 600000000 | bytes 9000000 | tf_op jit(solution)/shard_map/far_forward/pallas_call | solution.py:440
  59.5 8.0 %all-to-all-done.1 = bf16[128,32,128]{2,1,0:T(8,128)(2,1)S(1)} async-done(((bf16[128,32,128]{2,1,0:T(8,128)(2,1)}), bf16[128,32,128]{2,1,0:T(8,128)(2,1)S(1)}, u32[]{:S(2)}, u32[]{:S(2)}) %all-to-all-start.1) | async-done | bytes 1048608 | tf_op jit(solution)/shard_map/all_to_all | solution.py:762
  67.5 5.4 %ranking.1 = (bf16[4096,128]{1,0:T(8,128)(2,1)}, bf16[512,128]{1,0:T(8,128)(2,1)}) custom-call(s32[8]{0:T(128)} %lengths.5, bf16[4096,128]{1,0:T(8,128)(2,1)S(1)} %bitcast.32, bf16[128,512]{1,0:T(8,128)(2,1)} %get-tuple-element.89.code, bf16[512,128]{1,0:T(8,128)(2,1)} %get-tuple-element.95.user), custom_call_target="tpu_custom_call" | custom-call | flops 2000000000 | bytes 6000000 | tf_op jit(solution)/shard_map/ranking/pallas_call | solution.py:705
  72.9 4.9 %all-to-all-start.2 = ((bf16[128,32,128]{2,1,0:T(8,128)(2,1)}), bf16[128,32,128]{2,1,0:T(8,128)(2,1)S(1)}, u32[]{:S(2)}, u32[]{:S(2)}) async-start(bf16[128,32,128]{2,1,0:T(8,128)(2,1)} %bitcast.36), calls=%async_computation.2 | async-start | bytes 2097152 | tf_op jit(solution)/shard_map/all_to_all | solution.py:762
  77.8 0.0 copy-start.1
  77.8 0.0 copy-start.2
  77.9 6.6 %far_backward.1 = (f32[512,512]{1,0:T(8,128)S(1)}, bf16[128,512]{1,0:T(8,128)(2,1)S(1)}, bf16[128,512]{1,0:T(8,128)(2,1)S(1)}, bf16[128,512]{1,0:T(8,128)(2,1)S(...) custom-call(bf16[512,128]{1,0:T(8,128)(2,1)} %get-tuple-element.96.d_user, ...), custom_call_target="tpu_custom_call" | custom-call | flops 1000000000 | bytes 7000000 | tf_op jit(solution)/shard_map/far_backward/pallas_call | solution.py:558
  84.5 1.6 %collective-permute-start.10 = (bf16[128,512]{1,0:T(8,128)(2,1)S(1)}, bf16[128,512]{1,0:T(8,128)(2,1)S(1)}, u32[]{:S(2)}, u32[]{:S(2)}) collective-permute-start(bf16[128,512]{1,0:T(8,128)(2,1)S(1)} %get-tuple-element.108), channel_id=1, source_target_pairs={{0,8},{8,16},{16,24},{24,0},{32,40},{40,48},{48,56},{56,32},{64,72... | collective-permute-start | bytes 393224 | tf_op jit(solution)/shard_map/ppermute | solution.py:767
  86.0 2.7 %collective-permute-start.11 = (bf16[128,512]{1,0:T(8,128)(2,1)S(1)}, bf16[128,512]{1,0:T(8,128)(2,1)S(1)}, u32[]{:S(2)}, u32[]{:S(2)}) collective-permute-start(bf16[128,512]{1,0:T(8,128)(2,1)S(1)} %get-tuple-element.109), channel_id=1, source_target_pairs={{0,16},{8,24},{16,0},{24,8},{32,48},{40,56},{48,32},{56,40},{64,80... | collective-permute-start | bytes 393224 | tf_op jit(solution)/shard_map/ppermute | solution.py:767
  88.7 1.4 %collective-permute-start.12 = (bf16[128,512]{1,0:T(8,128)(2,1)S(1)}, bf16[128,512]{1,0:T(8,128)(2,1)S(1)}, u32[]{:S(2)}, u32[]{:S(2)}) collective-permute-start(bf16[128,512]{1,0:T(8,128)(2,1)S(1)} %get-tuple-element.110), channel_id=1, source_target_pairs={{0,24},{8,0},{16,8},{24,16},{32,56},{40,32},{48,40},{56,48},{64,88... | collective-permute-start | bytes 393224 | tf_op jit(solution)/shard_map/ppermute | solution.py:767
  90.2 5.0 %near_backward.1 = (bf16[512,512]{1,0:T(8,128)(2,1)}, bf16[512,512]{1,0:T(8,128)(2,1)}, bf16[512,512]{1,0:T(8,128)(2,1)}, bf16[2,128,512]{2,1,0:T(8,128)(2,1)S(1)}) custom-call(bf16[512,512]{1,0:T(8,128)(2,1)S(1)} %bitcast.23, bf16[512,512]{1,0:T(8,128)(2,1)S(1)} %bitcast.26, bf16[512,512]{1,0:T(8,128)(2,1)S(1)} %bitcast.29, ...), custom_call_target="tpu_custom_call" | custom-call | flops 1000000000 | bytes 9000000 | tf_op jit(solution)/shard_map/near_backward/pallas_call | solution.py:633
  95.2 2.8 %collective-permute-done.11 = bf16[128,512]{1,0:T(8,128)(2,1)S(1)} collective-permute-done((bf16[128,512]{1,0:T(8,128)(2,1)S(1)}, bf16[128,512]{1,0:T(8,128)(2,1)S(1)}, u32[]{:S(2)}, u32[]{:S(2)}) %collective-permute-start.11) | collective-permute-done | bytes 131104 | tf_op jit(solution)/shard_map/ppermute | solution.py:767
  98.0 0.0 collective-permute-done.12
  98.0 0.1 add_convert_fusion.1
  98.1 0.0 all-to-all-done.2
  98.1 0.5 collective-permute-start.16
  98.6 2.8 %collective-permute-start.15 = (bf16[128,512]{1,0:T(8,128)(2,1)S(1)}, bf16[128,512]{1,0:T(8,128)(2,1)S(1)}, u32[]{:S(2)}, u32[]{:S(2)}) collective-permute-start(bf16[128,512]{1,0:T(8,128)(2,1)S(1)} %add_convert_fusion.1), channel_id=1, source_target_pairs={{0,64},{8,72},{16,80},{24,88},{32,96},{40,104},{48,112},{56,120},{... | collective-permute-start | bytes 393224 | tf_op jit(solution)/shard_map/ppermute | solution.py:771
  101.4 2.0 %collective-permute-start.14 = (bf16[128,512]{1,0:T(8,128)(2,1)S(1)}, bf16[128,512]{1,0:T(8,128)(2,1)S(1)}, u32[]{:S(2)}, u32[]{:S(2)}) collective-permute-start(bf16[128,512]{1,0:T(8,128)(2,1)S(1)} %add_convert_fusion.1), channel_id=1, source_target_pairs={{0,32},{8,40},{16,48},{24,56},{32,64},{40,72},{48,80},{56,88},{64,... | collective-permute-start | bytes 393224 | tf_op jit(solution)/shard_map/ppermute | solution.py:771
  103.4 4.0 %scatter_rows.2.refs_0_ = f32[4,1024,128]{2,1,0:T(8,128)} custom-call(s32[128,128]{1,0:T(8,128)S(1)} %copy-done.8, bf16[4096,128]{1,0:T(8,128)(2,1)S(1)} %bitcast.30), custom_call_target="tpu_custom_call" | custom-call | flops 2147483648 | bytes 2000000 | tf_op jit(solution)/shard_map/scatter_rows/pallas_call | solution.py:280
  107.4 0.0 collective-permute-done.16
  107.4 0.0 collective-permute-done.15
  107.4 0.5 collective-permute-done.14
  107.9 0.1 add_convert_fusion.glob0
  108.0 0.0 copy-start.6
  108.0 4.6 %collective-permute-start.19 = (bf16[128,512]{1,0:T(8,128)(2,1)S(1)}, bf16[128,512]{1,0:T(8,128)(2,1)S(1)}, u32[]{:S(2)}, u32[]{:S(2)}) collective-permute-start(bf16[128,512]{1,0:T(8,128)(2,1)S(1)} %add_convert_fusion.glob0), channel_id=1, source_target_pairs={{0,24},{8,0},{16,8},{24,16},{32,56},{40,32},{48,40},{56,48},{64,88... | collective-permute-start | bytes 393224 | tf_op jit(solution)/shard_map/ppermute | solution.py:767
  112.6 0.9 collective-permute-start.17
  113.5 4.0 %scatter_rows.3 = f32[4,1024,128]{2,1,0:T(8,128)} custom-call(s32[128,128]{1,0:T(8,128)S(1)} %copy-done.8, bf16[4096,128]{1,0:T(8,128)(2,1)S(1)} %bitcast.31, f32[4,1024,128]{2,1,0:T(8,128)} %scatter_rows.2.refs_0_), custom_call_target="tpu_custom_call", output_to_operand_aliasing={{}: (2, {})} | custom-call | flops 2147483648 | bytes 2000000 | tf_op jit(solution)/shard_map/scatter_rows/pallas_call | solution.py:280
  117.5 0.8 collective-permute-done.19.glob3
  118.3 2.2 %collective-permute-done.18.glob2 = bf16[128,512]{1,0:T(8,128)(2,1)S(1)} collective-permute-done((bf16[128,512]{1,0:T(8,128)(2,1)S(1)}, bf16[128,512]{1,0:T(8,128)(2,1)S(1)}, u32[]{:S(2)}, u32[]{:S(2)}) %collective-permute-start.18) | collective-permute-done | bytes 131104 | tf_op jit(solution)/shard_map/ppermute | solution.py:767
  120.5 1.3 %collective-permute-done.17.glob1 = bf16[128,512]{1,0:T(8,128)(2,1)S(1)} collective-permute-done((bf16[128,512]{1,0:T(8,128)(2,1)S(1)}, bf16[128,512]{1,0:T(8,128)(2,1)S(1)}, u32[]{:S(2)}, u32[]{:S(2)}) %collective-permute-start.17) | collective-permute-done | bytes 131104 | tf_op jit(solution)/shard_map/ppermute | solution.py:767
  121.7 0.0 collective-permute-done.13.edge
  121.7 1.8 %add_received.1 = (bf16[512,512]{1,0:T(8,128)(2,1)}, bf16[512,512]{1,0:T(8,128)(2,1)}) custom-call(s32[1,2]{1,0:T(1,128)} %gids.5, bf16[512,512]{1,0:T(8,128)(2,1)S(1)} %copy-done.6, bf16[512,512]{1,0:T(8,128)(2,1)S(1)} %copy-done.7, bf16[2,128,512]{2,1,0:T(8,128)(2,1)S(1)} %collective-permute-done.13.edge, bf16[128,512]{1,0:T(8,128)(2,1)S(1)} %add_convert_fusion.glob0, ...), custom_call_target="tpu_custom_call" | custom-call | flops 1000000 | bytes 3000000 | tf_op jit(solution)/shard_map/add_received/pallas_call | solution.py:745
  (15 shorter events, 0.0 us)
Async XLA Ops:
  2.3 8.8 %collective-permute-start = (bf16[128,512]{1,0:T(8,128)(2,1)S(1)}, bf16[128,512]{1,0:T(8,128)(2,1)S(1)}, u32[]{:S(2)}, u32[]{:S(2)}) collective-permute-start(bf16[128,512]{1,0:T(8,128)(2,1)S(1)} %get-tuple-element.74), channel_id=1, source_target_pairs={{0,8},{8,16},{16,24},{24,0},{32,40},{40,48},{48,56},{56,32},{64,72... | collective-permute-start | bytes 393224 | tf_op jit(solution)/shard_map/ppermute | solution.py:767
  3.9 9.3 %collective-permute-start.1 = (bf16[128,512]{1,0:T(8,128)(2,1)S(1)}, bf16[128,512]{1,0:T(8,128)(2,1)S(1)}, u32[]{:S(2)}, u32[]{:S(2)}) collective-permute-start(bf16[128,512]{1,0:T(8,128)(2,1)S(1)} %get-tuple-element.75), channel_id=1, source_target_pairs={{0,16},{8,24},{16,0},{24,8},{32,48},{40,56},{48,32},{56,40},{64,80... | collective-permute-start | bytes 393224 | tf_op jit(solution)/shard_map/ppermute | solution.py:767
  6.6 6.6 %collective-permute-start.2 = (bf16[128,512]{1,0:T(8,128)(2,1)S(1)}, bf16[128,512]{1,0:T(8,128)(2,1)S(1)}, u32[]{:S(2)}, u32[]{:S(2)}) collective-permute-start(bf16[128,512]{1,0:T(8,128)(2,1)S(1)} %get-tuple-element.76), channel_id=1, source_target_pairs={{0,24},{8,0},{16,8},{24,16},{32,56},{40,32},{48,40},{56,48},{64,88... | collective-permute-start | bytes 393224 | tf_op jit(solution)/shard_map/ppermute | solution.py:767
  10.6 9.6 %collective-permute-start.3 = (bf16[2,128,512]{2,1,0:T(8,128)(2,1)S(1)}, bf16[2,128,512]{2,1,0:T(8,128)(2,1)S(1)}, u32[]{:S(2)}, u32[]{:S(2)}) collective-permute-start(bf16[2,128,512]{2,1,0:T(8,128)(2,1)S(1)} %get-tuple-element.79), channel_id=1, source_target_pairs={{0,8},{8,16},{16,24},{24,32},{32,40},{40,48},{48,56},{56,64},{64,7... | collective-permute-start | bytes 786440 | tf_op jit(solution)/shard_map/ppermute | solution.py:758
  13.2 14.8 %collective-permute-start.6 = (bf16[128,512]{1,0:T(8,128)(2,1)S(1)}, bf16[128,512]{1,0:T(8,128)(2,1)S(1)}, u32[]{:S(2)}, u32[]{:S(2)}) collective-permute-start(bf16[128,512]{1,0:T(8,128)(2,1)S(1)} %add_convert_fusion.3), channel_id=1, source_target_pairs={{0,96},{8,104},{16,112},{24,120},{32,0},{40,8},{48,16},{56,24},{64... | collective-permute-start | bytes 393224 | tf_op jit(solution)/shard_map/ppermute | solution.py:771
  13.6 14.5 %collective-permute-start.5 = (bf16[128,512]{1,0:T(8,128)(2,1)S(1)}, bf16[128,512]{1,0:T(8,128)(2,1)S(1)}, u32[]{:S(2)}, u32[]{:S(2)}) collective-permute-start(bf16[128,512]{1,0:T(8,128)(2,1)S(1)} %add_convert_fusion.3), channel_id=1, source_target_pairs={{0,64},{8,72},{16,80},{24,88},{32,96},{40,104},{48,112},{56,120},{... | collective-permute-start | bytes 393224 | tf_op jit(solution)/shard_map/ppermute | solution.py:771
  16.9 11.3 %collective-permute-start.4 = (bf16[128,512]{1,0:T(8,128)(2,1)S(1)}, bf16[128,512]{1,0:T(8,128)(2,1)S(1)}, u32[]{:S(2)}, u32[]{:S(2)}) collective-permute-start(bf16[128,512]{1,0:T(8,128)(2,1)S(1)} %add_convert_fusion.3), channel_id=1, source_target_pairs={{0,32},{8,40},{16,48},{24,56},{32,64},{40,72},{48,80},{56,88},{64,... | collective-permute-start | bytes 393224 | tf_op jit(solution)/shard_map/ppermute | solution.py:771
  20.1 16.9 %all-to-all-start = ((s32[128,1,128]{2,1,0:T(1,128)}), s32[128,1,128]{2,1,0:T(1,128)S(1)}, u32[]{:S(2)}, u32[]{:S(2)}) async-start(s32[128,1,128]{2,1,0:T(1,128)} %bitcast.39), calls=%async_computation | async-start | bytes 131072 | tf_op jit(solution)/shard_map/all_to_all | solution.py:762
  28.2 15.4 %collective-permute-start.9 = (bf16[128,512]{1,0:T(8,128)(2,1)S(1)}, bf16[128,512]{1,0:T(8,128)(2,1)S(1)}, u32[]{:S(2)}, u32[]{:S(2)}) collective-permute-start(bf16[128,512]{1,0:T(8,128)(2,1)S(1)} %add_convert_fusion.2.glob0), channel_id=1, source_target_pairs={{0,24},{8,0},{16,8},{24,16},{32,56},{40,32},{48,40},{56,48},{64,88... | collective-permute-start | bytes 393224 | tf_op jit(solution)/shard_map/ppermute | solution.py:767
  31.0 12.6 %collective-permute-start.8 = (bf16[128,512]{1,0:T(8,128)(2,1)S(1)}, bf16[128,512]{1,0:T(8,128)(2,1)S(1)}, u32[]{:S(2)}, u32[]{:S(2)}) collective-permute-start(bf16[128,512]{1,0:T(8,128)(2,1)S(1)} %add_convert_fusion.2.glob0), channel_id=1, source_target_pairs={{0,16},{8,24},{16,0},{24,8},{32,48},{40,56},{48,32},{56,40},{64,80... | collective-permute-start | bytes 393224 | tf_op jit(solution)/shard_map/ppermute | solution.py:767
  31.8 11.8 %collective-permute-start.7 = (bf16[128,512]{1,0:T(8,128)(2,1)S(1)}, bf16[128,512]{1,0:T(8,128)(2,1)S(1)}, u32[]{:S(2)}, u32[]{:S(2)}) collective-permute-start(bf16[128,512]{1,0:T(8,128)(2,1)S(1)} %add_convert_fusion.2.glob0), channel_id=1, source_target_pairs={{0,8},{8,16},{16,24},{24,0},{32,40},{40,48},{48,56},{56,32},{64,72... | collective-permute-start | bytes 393224 | tf_op jit(solution)/shard_map/ppermute | solution.py:767
  43.6 5.1 %copy-start = (bf16[1,512,512]{2,1,0:T(8,128)(2,1)S(1)}, bf16[1,512,512]{2,1,0:T(8,128)(2,1)}, u32[]{:S(2)}) copy-start(bf16[1,512,512]{2,1,0:T(8,128)(2,1)} %param.11) | copy-start | bytes 1572868
  43.6 5.1 %copy-start.4 = (bf16[1,512,512]{2,1,0:T(8,128)(2,1)S(1)}, bf16[1,512,512]{2,1,0:T(8,128)(2,1)}, u32[]{:S(2)}) copy-start(bf16[1,512,512]{2,1,0:T(8,128)(2,1)} %param.12) | copy-start | bytes 1572868
  43.6 5.1 %copy-start.5 = (bf16[1,512,512]{2,1,0:T(8,128)(2,1)S(1)}, bf16[1,512,512]{2,1,0:T(8,128)(2,1)}, u32[]{:S(2)}) copy-start(bf16[1,512,512]{2,1,0:T(8,128)(2,1)} %param.13) | copy-start | bytes 1572868
  43.6 23.9 %all-to-all-start.1 = ((bf16[128,32,128]{2,1,0:T(8,128)(2,1)}), bf16[128,32,128]{2,1,0:T(8,128)(2,1)S(1)}, u32[]{:S(2)}, u32[]{:S(2)}) async-start(bf16[128,32,128]{2,1,0:T(8,128)(2,1)} %bitcast.37), calls=%async_computation.1 | async-start | bytes 2097152 | tf_op jit(solution)/shard_map/all_to_all | solution.py:762
  72.9 25.2 %all-to-all-start.2 = ((bf16[128,32,128]{2,1,0:T(8,128)(2,1)}), bf16[128,32,128]{2,1,0:T(8,128)(2,1)S(1)}, u32[]{:S(2)}, u32[]{:S(2)}) async-start(bf16[128,32,128]{2,1,0:T(8,128)(2,1)} %bitcast.36), calls=%async_computation.2 | async-start | bytes 2097152 | tf_op jit(solution)/shard_map/all_to_all | solution.py:762
  77.8 12.4 %copy-start.1 = (bf16[1,512,512]{2,1,0:T(8,128)(2,1)S(1)}, bf16[1,512,512]{2,1,0:T(8,128)(2,1)}, u32[]{:S(2)}) copy-start(bf16[1,512,512]{2,1,0:T(8,128)(2,1)} %param.11) | copy-start | bytes 1572868
  77.8 12.4 %copy-start.2 = (bf16[8,512,256]{2,1,0:T(8,128)(2,1)S(1)}, bf16[8,512,256]{2,1,0:T(8,128)(2,1)}, u32[]{:S(2)}) copy-start(bf16[8,512,256]{2,1,0:T(8,128)(2,1)} %get-tuple-element.102.probs) | copy-start | bytes 6291460
  77.8 12.3 %copy-start.3 = (bf16[8,512,256]{2,1,0:T(8,128)(2,1)S(1)}, bf16[8,512,256]{2,1,0:T(8,128)(2,1)}, u32[]{:S(2)}) copy-start(bf16[8,512,256]{2,1,0:T(8,128)(2,1)} %get-tuple-element.103.slope) | copy-start | bytes 6291460
  84.5 10.7 %collective-permute-start.10 = (bf16[128,512]{1,0:T(8,128)(2,1)S(1)}, bf16[128,512]{1,0:T(8,128)(2,1)S(1)}, u32[]{:S(2)}, u32[]{:S(2)}) collective-permute-start(bf16[128,512]{1,0:T(8,128)(2,1)S(1)} %get-tuple-element.108), channel_id=1, source_target_pairs={{0,8},{8,16},{16,24},{24,0},{32,40},{40,48},{48,56},{56,32},{64,72... | collective-permute-start | bytes 393224 | tf_op jit(solution)/shard_map/ppermute | solution.py:767
  86.0 12.0 %collective-permute-start.11 = (bf16[128,512]{1,0:T(8,128)(2,1)S(1)}, bf16[128,512]{1,0:T(8,128)(2,1)S(1)}, u32[]{:S(2)}, u32[]{:S(2)}) collective-permute-start(bf16[128,512]{1,0:T(8,128)(2,1)S(1)} %get-tuple-element.109), channel_id=1, source_target_pairs={{0,16},{8,24},{16,0},{24,8},{32,48},{40,56},{48,32},{56,40},{64,80... | collective-permute-start | bytes 393224 | tf_op jit(solution)/shard_map/ppermute | solution.py:767
  88.7 9.3 %collective-permute-start.12 = (bf16[128,512]{1,0:T(8,128)(2,1)S(1)}, bf16[128,512]{1,0:T(8,128)(2,1)S(1)}, u32[]{:S(2)}, u32[]{:S(2)}) collective-permute-start(bf16[128,512]{1,0:T(8,128)(2,1)S(1)} %get-tuple-element.110), channel_id=1, source_target_pairs={{0,24},{8,0},{16,8},{24,16},{32,56},{40,32},{48,40},{56,48},{64,88... | collective-permute-start | bytes 393224 | tf_op jit(solution)/shard_map/ppermute | solution.py:767
  90.2 13.2 %copy-start.8 = (s32[128,128]{1,0:T(8,128)S(1)}, s32[128,128]{1,0:T(8,128)}, u32[]{:S(2)}) copy-start(s32[128,128]{1,0:T(8,128)} %get-tuple-element.114.asked) | copy-start | bytes 196612
  95.2 26.5 %collective-permute-start.13 = (bf16[2,128,512]{2,1,0:T(8,128)(2,1)S(1)}, bf16[2,128,512]{2,1,0:T(8,128)(2,1)S(1)}, u32[]{:S(2)}, u32[]{:S(2)}) collective-permute-start(bf16[2,128,512]{2,1,0:T(8,128)(2,1)S(1)} %get-tuple-element.113), channel_id=1, source_target_pairs={{0,120},{8,0},{16,8},{24,16},{32,24},{40,32},{48,40},{56,48},{64,5... | collective-permute-start | bytes 786440 | tf_op jit(solution)/shard_map/ppermute | solution.py:758
  98.1 9.3 %collective-permute-start.16 = (bf16[128,512]{1,0:T(8,128)(2,1)S(1)}, bf16[128,512]{1,0:T(8,128)(2,1)S(1)}, u32[]{:S(2)}, u32[]{:S(2)}) collective-permute-start(bf16[128,512]{1,0:T(8,128)(2,1)S(1)} %add_convert_fusion.1), channel_id=1, source_target_pairs={{0,96},{8,104},{16,112},{24,120},{32,0},{40,8},{48,16},{56,24},{64... | collective-permute-start | bytes 393224 | tf_op jit(solution)/shard_map/ppermute | solution.py:771
  98.6 8.8 %collective-permute-start.15 = (bf16[128,512]{1,0:T(8,128)(2,1)S(1)}, bf16[128,512]{1,0:T(8,128)(2,1)S(1)}, u32[]{:S(2)}, u32[]{:S(2)}) collective-permute-start(bf16[128,512]{1,0:T(8,128)(2,1)S(1)} %add_convert_fusion.1), channel_id=1, source_target_pairs={{0,64},{8,72},{16,80},{24,88},{32,96},{40,104},{48,112},{56,120},{... | collective-permute-start | bytes 393224 | tf_op jit(solution)/shard_map/ppermute | solution.py:771
  101.4 6.5 %collective-permute-start.14 = (bf16[128,512]{1,0:T(8,128)(2,1)S(1)}, bf16[128,512]{1,0:T(8,128)(2,1)S(1)}, u32[]{:S(2)}, u32[]{:S(2)}) collective-permute-start(bf16[128,512]{1,0:T(8,128)(2,1)S(1)} %add_convert_fusion.1), channel_id=1, source_target_pairs={{0,32},{8,40},{16,48},{24,56},{32,64},{40,72},{48,80},{56,88},{64,... | collective-permute-start | bytes 393224 | tf_op jit(solution)/shard_map/ppermute | solution.py:771
  108.0 13.8 %copy-start.6 = (bf16[512,512]{1,0:T(8,128)(2,1)S(1)}, bf16[512,512]{1,0:T(8,128)(2,1)}, u32[]{:S(2)}) copy-start(bf16[512,512]{1,0:T(8,128)(2,1)} %get-tuple-element.111.d_k) | copy-start | bytes 1572868
  108.0 13.8 %copy-start.7 = (bf16[512,512]{1,0:T(8,128)(2,1)S(1)}, bf16[512,512]{1,0:T(8,128)(2,1)}, u32[]{:S(2)}) copy-start(bf16[512,512]{1,0:T(8,128)(2,1)} %get-tuple-element.112.d_v) | copy-start | bytes 1572868
  108.0 10.3 %collective-permute-start.19 = (bf16[128,512]{1,0:T(8,128)(2,1)S(1)}, bf16[128,512]{1,0:T(8,128)(2,1)S(1)}, u32[]{:S(2)}, u32[]{:S(2)}) collective-permute-start(bf16[128,512]{1,0:T(8,128)(2,1)S(1)} %add_convert_fusion.glob0), channel_id=1, source_target_pairs={{0,24},{8,0},{16,8},{24,16},{32,56},{40,32},{48,40},{56,48},{64,88... | collective-permute-start | bytes 393224 | tf_op jit(solution)/shard_map/ppermute | solution.py:767
  112.6 7.9 %collective-permute-start.18 = (bf16[128,512]{1,0:T(8,128)(2,1)S(1)}, bf16[128,512]{1,0:T(8,128)(2,1)S(1)}, u32[]{:S(2)}, u32[]{:S(2)}) collective-permute-start(bf16[128,512]{1,0:T(8,128)(2,1)S(1)} %add_convert_fusion.glob0), channel_id=1, source_target_pairs={{0,16},{8,24},{16,0},{24,8},{32,48},{40,56},{48,32},{56,40},{64,80... | collective-permute-start | bytes 393224 | tf_op jit(solution)/shard_map/ppermute | solution.py:767
  112.6 9.2 %collective-permute-start.17 = (bf16[128,512]{1,0:T(8,128)(2,1)S(1)}, bf16[128,512]{1,0:T(8,128)(2,1)S(1)}, u32[]{:S(2)}, u32[]{:S(2)}) collective-permute-start(bf16[128,512]{1,0:T(8,128)(2,1)S(1)} %add_convert_fusion.glob0), channel_id=1, source_target_pairs={{0,8},{8,16},{16,24},{24,0},{32,40},{40,48},{48,56},{56,32},{64,72... | collective-permute-start | bytes 393224 | tf_op jit(solution)/shard_map/ppermute | solution.py:767

commit v5 on v4

--- a/solution.py
+++ b/solution.py
@@ -403,7 +403,10 @@
             normed_out[rows, :] = normed.astype(BF)
             inv_out[rows, :] = inv
             gated = (normed * gate[rows, :].astype(F32)).astype(BF)
-            user[rows, :] = (dot(gated, w_out[...]) + history[rows, :].astype(F32)).astype(BF)
+            vector = dot(gated, w_out[...]) + history[rows, :].astype(F32)
+            rounded = vector.astype(BF)
+            user[rows, :E] = rounded
+            user[rows, E:] = (vector - rounded.astype(F32)).astype(BF)
 
 
 def pair_block(rows):
@@ -445,7 +448,7 @@
             SQUARE,
             slow((EVENTS, D), BF),
             slow((EVENTS, 1), F32),
-            slow((EVENTS, E), BF),
+            slow((EVENTS, 2 * E), BF),
         ),
         in_specs=[SMEM_SPEC] * 2
         + [pair_block(EVENTS)]
@@ -457,7 +460,7 @@
             head_block(),
             whole((EVENTS, D)),
             whole((EVENTS, 1)),
-            whole((EVENTS, E)),
+            whole((EVENTS, 2 * E)),
         ],
         scratch_shapes=[
             pltpu.VMEM((PAIRS, EVENTS, 2 * HEAD_DIM), F32),
@@ -657,8 +660,8 @@
 ):
     sends = []
     portion = NDEV * SLOTS // 4
-    user_b = user[...]
-    user_t = user_b.T
+    user_b = user[:, :E]
+    user_t = user[...].T
     mark = code[...].astype(F32)
     first = mark >= FIRST
     rank = jnp.where(first, mark - FIRST, mark)
@@ -666,7 +669,8 @@
     size = group * SLOTS
     slot = iota((SLOTS, EVENTS), 0).astype(F32)
     for d in range(0, NDEV, group):
-        s = dot(items[d * SLOTS : d * SLOTS + size, :], user_t)
+        rows = items[d * SLOTS : d * SLOTS + size, :]
+        s = dot(jnp.concatenate([rows, rows], axis=1), user_t)
         for r in range(group):
             own = rank[d + r : d + r + 1, :] == slot
             part = jnp.where(own, s[r * SLOTS : (r + 1) * SLOTS, :], 0.0)

time: 124 us -> 125 us (level)
  no operation moved by 1% of the time
where the time goes in v5:
time: 125 us; the launch traced here: 124 us
  starting transfers between devices  51.3 us (41%)
  Pallas kernels  48.4 us (39%)
  waiting for transfers between devices  23.1 us (18%)
    ppermute x12, starting transfers between devices, around_x(): return lax.ppermute(x, 'seq', pairs)  21.5 us
    all_to_all x3, starting transfers between devices, exchange(): return lax.all_to_all(x, axis, split_axis=0, concat_axis=0, tiled=True)  18.4 us
    all_to_all x3, waiting for transfers between devices, exchange(): return lax.all_to_all(x, axis, split_axis=0, concat_axis=0, tiled=True)  12.3 us
    ppermute x6, starting transfers between devices, around_z(): lax.ppermute(x, 'seq', [(i, (i + distance * XSIZE) % NSEQ) for i in range...  10.8 us
    ppermute x12, waiting for transfers between devices, around_x(): return lax.ppermute(x, 'seq', pairs)  9.25 us
    pallas_call x2, Pallas kernels, scatter(): pl.pallas_call(functools.partial(scatter_kernel, start), grid=(steps,), o...  7.96 us
    pallas_call x1, Pallas kernels, far_backward(): pl.pallas_call(far_backward_kernel, grid=(PAIRS,), out_shape=(fast((EVENT...  6.61 us
    pallas_call x1, Pallas kernels, gather(): pl.pallas_call(gather_kernel, out_shape=(slow((NDEV * SLOTS, E), BF), slo...  6.48 us
  transfers between devices with their start and end apart: 23, of which 9 were waited for; matrix products, arithmetic and copies ran while one was open for 0% of the time, Pallas kernels for 32%

profile of v5, /device:TPU:32, one launch (start us, length us, event | category | flops | bytes accessed | tf_op | source)
XLA Modules:
  0.0 124.0 jit_solution(3753845681746216501)
XLA Ops:
  0.6 1.7 %pieces.1 = (bf16[2,128,512]{2,1,0:T(8,128)(2,1)S(1)}, bf16[128,512]{1,0:T(8,128)(2,1)S(1)}, bf16[128,512]{1,0:T(8,128)(2,1)S(1)}, bf16[128,512]{1,0:T(8,128)(2,1)S(1)}, bf16[128,512]{1,0:T(8,128)(2,1)S(1)}) custom-call(s32[1,2]{1,0:T(1,128)} %gids.5, bf16[512,512]{1,0:T(8,128)(2,1)} %bitcast.24, bf16[512,512]{1,0:T(8,128)(2,1)} %bitcast.27), custom_call_target="tpu_custom_call" | custom-call | flops 1000000 | bytes 2000000 | tf_op jit(solution)/shard_map/pieces/pallas_call | solution.py:121
  2.3 1.6 %collective-permute-start = (bf16[128,512]{1,0:T(8,128)(2,1)S(1)}, bf16[128,512]{1,0:T(8,128)(2,1)S(1)}, u32[]{:S(2)}, u32[]{:S(2)}) collective-permute-start(bf16[128,512]{1,0:T(8,128)(2,1)S(1)} %get-tuple-element.74), channel_id=1, source_target_pairs={{0,8},{8,16},{16,24},{24,0},{32,40},{40,48},{48,56},{56,32},{64,72... | collective-permute-start | bytes 393224 | tf_op jit(solution)/shard_map/ppermute | solution.py:771
  3.9 2.7 %collective-permute-start.1 = (bf16[128,512]{1,0:T(8,128)(2,1)S(1)}, bf16[128,512]{1,0:T(8,128)(2,1)S(1)}, u32[]{:S(2)}, u32[]{:S(2)}) collective-permute-start(bf16[128,512]{1,0:T(8,128)(2,1)S(1)} %get-tuple-element.75), channel_id=1, source_target_pairs={{0,16},{8,24},{16,0},{24,8},{32,48},{40,56},{48,32},{56,40},{64,80... | collective-permute-start | bytes 393224 | tf_op jit(solution)/shard_map/ppermute | solution.py:771
  6.6 1.4 %collective-permute-start.2 = (bf16[128,512]{1,0:T(8,128)(2,1)S(1)}, bf16[128,512]{1,0:T(8,128)(2,1)S(1)}, u32[]{:S(2)}, u32[]{:S(2)}) collective-permute-start(bf16[128,512]{1,0:T(8,128)(2,1)S(1)} %get-tuple-element.76), channel_id=1, source_target_pairs={{0,24},{8,0},{16,8},{24,16},{32,56},{40,32},{48,40},{56,48},{64,88... | collective-permute-start | bytes 393224 | tf_op jit(solution)/shard_map/ppermute | solution.py:771
  8.1 2.5 %route.1 = (s32[128,128]{1,0:T(8,128)}, bf16[128,512]{1,0:T(8,128)(2,1)}) custom-call(s32[5,1,512]{2,1,0:T(1,128)} %bitcast.44, s32[5,1,512]{2,1,0:T(1,128)} %bitcast.45), custom_call_target="tpu_custom_call" | custom-call | flops 100000000 | bytes 1000000 | tf_op jit(solution)/shard_map/route/pallas_call | solution.py:154
  10.6 0.6 collective-permute-start.3
  11.2 0.0 collective-permute-done
  11.2 2.2 %collective-permute-done.1 = bf16[128,512]{1,0:T(8,128)(2,1)S(1)} collective-permute-done((bf16[128,512]{1,0:T(8,128)(2,1)S(1)}, bf16[128,512]{1,0:T(8,128)(2,1)S(1)}, u32[]{:S(2)}, u32[]{:S(2)}) %collective-permute-start.1) | collective-permute-done | bytes 131104 | tf_op jit(solution)/shard_map/ppermute | solution.py:771
  13.3 0.0 collective-permute-done.2
  13.3 0.1 add_convert_fusion.3
  13.4 0.2 collective-permute-start.6
  13.6 3.3 %collective-permute-start.5 = (bf16[128,512]{1,0:T(8,128)(2,1)S(1)}, bf16[128,512]{1,0:T(8,128)(2,1)S(1)}, u32[]{:S(2)}, u32[]{:S(2)}) collective-permute-start(bf16[128,512]{1,0:T(8,128)(2,1)S(1)} %add_convert_fusion.3), channel_id=1, source_target_pairs={{0,64},{8,72},{16,80},{24,88},{32,96},{40,104},{48,112},{56,120},{... | collective-permute-start | bytes 393224 | tf_op jit(solution)/shard_map/ppermute | solution.py:775
  16.9 2.1 %collective-permute-start.4 = (bf16[128,512]{1,0:T(8,128)(2,1)S(1)}, bf16[128,512]{1,0:T(8,128)(2,1)S(1)}, u32[]{:S(2)}, u32[]{:S(2)}) collective-permute-start(bf16[128,512]{1,0:T(8,128)(2,1)S(1)} %add_convert_fusion.3), channel_id=1, source_target_pairs={{0,32},{8,40},{16,48},{24,56},{32,64},{40,72},{48,80},{56,88},{64,... | collective-permute-start | bytes 393224 | tf_op jit(solution)/shard_map/ppermute | solution.py:775
  18.9 1.1 collective-permute-done.3.halo
  20.0 8.5 %all-to-all-start = ((s32[128,1,128]{2,1,0:T(1,128)}), s32[128,1,128]{2,1,0:T(1,128)S(1)}, u32[]{:S(2)}, u32[]{:S(2)}) async-start(s32[128,1,128]{2,1,0:T(1,128)} %bitcast.39), calls=%async_computation | async-start | bytes 131072 | tf_op jit(solution)/shard_map/all_to_all | solution.py:766
  28.5 0.0 collective-permute-done.6
  28.5 0.0 collective-permute-done.5
  28.5 0.0 collective-permute-done.4
  28.5 0.1 add_convert_fusion.2.glob0
  28.6 2.8 %collective-permute-start.9 = (bf16[128,512]{1,0:T(8,128)(2,1)S(1)}, bf16[128,512]{1,0:T(8,128)(2,1)S(1)}, u32[]{:S(2)}, u32[]{:S(2)}) collective-permute-start(bf16[128,512]{1,0:T(8,128)(2,1)S(1)} %add_convert_fusion.2.glob0), channel_id=1, source_target_pairs={{0,24},{8,0},{16,8},{24,16},{32,56},{40,32},{48,40},{56,48},{64,88... | collective-permute-start | bytes 393224 | tf_op jit(solution)/shard_map/ppermute | solution.py:771
  31.4 0.8 collective-permute-start.8
  32.2 0.9 collective-permute-start.7
  33.1 4.4 %all-to-all-done = s32[128,1,128]{2,1,0:T(1,128)S(1)} async-done(((s32[128,1,128]{2,1,0:T(1,128)}), s32[128,1,128]{2,1,0:T(1,128)S(1)}, u32[]{:S(2)}, u32[]{:S(2)}) %all-to-all-start) | async-done | bytes 65568 | tf_op jit(solution)/shard_map/all_to_all | solution.py:766
  37.5 6.5 %gather_rows.1 = (bf16[4096,128]{1,0:T(8,128)(2,1)}, s32[128,128]{1,0:T(8,128)}) custom-call(s32[128,128]{1,0:T(8,128)S(1)} %bitcast.33, bf16[4096,128]{1,0:T(8,128)(2,1)} %table_far.1), custom_call_target="tpu_custom_call" | custom-call | flops 4294967296 | bytes 2000000 | tf_op jit(solution)/shard_map/gather_rows/pallas_call | solution.py:229
  44.0 0.0 copy-start
  44.0 0.0 copy-start.4
  44.0 0.0 copy-start.5
  44.0 0.0 collective-permute-done.9.glob3
  44.0 0.0 collective-permute-done.8.glob2
  44.0 0.0 collective-permute-done.7.glob1
  44.0 5.0 %all-to-all-start.1 = ((bf16[128,32,128]{2,1,0:T(8,128)(2,1)}), bf16[128,32,128]{2,1,0:T(8,128)(2,1)S(1)}, u32[]{:S(2)}, u32[]{:S(2)}) async-start(bf16[128,32,128]{2,1,0:T(8,128)(2,1)} %bitcast.37), calls=%async_computation.1 | async-start | bytes 2097152 | tf_op jit(solution)/shard_map/all_to_all | solution.py:766
  49.1 4.6 %near_forward.1 = (bf16[8,512,256]{2,1,0:T(8,128)(2,1)}, bf16[8,512,256]{2,1,0:T(8,128)(2,1)}, f32[512,512]{1,0:T(8,128)S(1)}) custom-call(s32[8]{0:T(128)} %lengths.5, bf16[512,512]{1,0:T(8,128)(2,1)S(1)} %bitcast.21, bf16[512,512]{1,0:T(8,128)(2,1)S(1)} %bitcast.25, bf16[512,512]{1,0:T(8,128)(2,1)S(1)} %bitcast.28, ...), custom_call_target="tpu_custom_call" | custom-call | flops 500000000 | bytes 7000000 | tf_op jit(solution)/shard_map/near_forward/pallas_call | solution.py:428
  53.7 6.3 %far_forward.1 = (bf16[8,512,256]{2,1,0:T(8,128)(2,1)}, bf16[8,512,256]{2,1,0:T(8,128)(2,1)}, bf16[512,512]{1,0:T(8,128)(2,1)}, f32[512,1]{1,0:T(8,128)}, bf16[512,256]{1,0:T(8,128)(2,1)}) custom-call(s32[8]{0:T(128)} %lengths.5, s32[1,2]{1,0:T(1,128)} %gids.5, bf16[512,512]{1,0:T(8,128)(2,1)S(1)} %bitcast.22, bf16[128,512]{1,0:T(8,128)(2,1)S(1)} %add_convert_fusion.2.glob0, ...), custom_call_target="tpu_custom_call" | custom-call | flops 600000000 | bytes 9000000 | tf_op jit(solution)/shard_map/far_forward/pallas_call | solution.py:443
  60.0 7.9 %all-to-all-done.1 = bf16[128,32,128]{2,1,0:T(8,128)(2,1)S(1)} async-done(((bf16[128,32,128]{2,1,0:T(8,128)(2,1)}), bf16[128,32,128]{2,1,0:T(8,128)(2,1)S(1)}, u32[]{:S(2)}, u32[]{:S(2)}) %all-to-all-start.1) | async-done | bytes 1048608 | tf_op jit(solution)/shard_map/all_to_all | solution.py:766
  67.9 5.5 %ranking.1 = (bf16[4096,128]{1,0:T(8,128)(2,1)}, bf16[512,128]{1,0:T(8,128)(2,1)}) custom-call(s32[8]{0:T(128)} %lengths.5, bf16[4096,128]{1,0:T(8,128)(2,1)S(1)} %bitcast.32, bf16[128,512]{1,0:T(8,128)(2,1)} %get-tuple-element.89.code, bf16[512,256]{1,0:T(8,128)(2,1)} %get-tuple-element.95.user), custom_call_target="tpu_custom_call" | custom-call | flops 2000000000 | bytes 6000000 | tf_op jit(solution)/shard_map/ranking/pallas_call | solution.py:709
  73.4 4.9 %all-to-all-start.2 = ((bf16[128,32,128]{2,1,0:T(8,128)(2,1)}), bf16[128,32,128]{2,1,0:T(8,128)(2,1)S(1)}, u32[]{:S(2)}, u32[]{:S(2)}) async-start(bf16[128,32,128]{2,1,0:T(8,128)(2,1)} %bitcast.36), calls=%async_computation.2 | async-start | bytes 2097152 | tf_op jit(solution)/shard_map/all_to_all | solution.py:766
  78.3 0.0 copy-start.1
  78.3 0.0 copy-start.2
  78.3 6.6 %far_backward.1 = (f32[512,512]{1,0:T(8,128)S(1)}, bf16[128,512]{1,0:T(8,128)(2,1)S(1)}, bf16[128,512]{1,0:T(8,128)(2,1)S(1)}, bf16[128,512]{1,0:T(8,128)(2,1)S(...) custom-call(bf16[512,128]{1,0:T(8,128)(2,1)} %get-tuple-element.96.d_user, ...), custom_call_target="tpu_custom_call" | custom-call | flops 1000000000 | bytes 7000000 | tf_op jit(solution)/shard_map/far_backward/pallas_call | solution.py:561
  84.9 1.5 %collective-permute-start.10 = (bf16[128,512]{1,0:T(8,128)(2,1)S(1)}, bf16[128,512]{1,0:T(8,128)(2,1)S(1)}, u32[]{:S(2)}, u32[]{:S(2)}) collective-permute-start(bf16[128,512]{1,0:T(8,128)(2,1)S(1)} %get-tuple-element.108), channel_id=1, source_target_pairs={{0,8},{8,16},{16,24},{24,0},{32,40},{40,48},{48,56},{56,32},{64,72... | collective-permute-start | bytes 393224 | tf_op jit(solution)/shard_map/ppermute | solution.py:771
  86.5 2.7 %collective-permute-start.11 = (bf16[128,512]{1,0:T(8,128)(2,1)S(1)}, bf16[128,512]{1,0:T(8,128)(2,1)S(1)}, u32[]{:S(2)}, u32[]{:S(2)}) collective-permute-start(bf16[128,512]{1,0:T(8,128)(2,1)S(1)} %get-tuple-element.109), channel_id=1, source_target_pairs={{0,16},{8,24},{16,0},{24,8},{32,48},{40,56},{48,32},{56,40},{64,80... | collective-permute-start | bytes 393224 | tf_op jit(solution)/shard_map/ppermute | solution.py:771
  89.2 1.4 %collective-permute-start.12 = (bf16[128,512]{1,0:T(8,128)(2,1)S(1)}, bf16[128,512]{1,0:T(8,128)(2,1)S(1)}, u32[]{:S(2)}, u32[]{:S(2)}) collective-permute-start(bf16[128,512]{1,0:T(8,128)(2,1)S(1)} %get-tuple-element.110), channel_id=1, source_target_pairs={{0,24},{8,0},{16,8},{24,16},{32,56},{40,32},{48,40},{56,48},{64,88... | collective-permute-start | bytes 393224 | tf_op jit(solution)/shard_map/ppermute | solution.py:771
  90.7 5.0 %near_backward.1 = (bf16[512,512]{1,0:T(8,128)(2,1)}, bf16[512,512]{1,0:T(8,128)(2,1)}, bf16[512,512]{1,0:T(8,128)(2,1)}, bf16[2,128,512]{2,1,0:T(8,128)(2,1)S(1)}) custom-call(bf16[512,512]{1,0:T(8,128)(2,1)S(1)} %bitcast.23, bf16[512,512]{1,0:T(8,128)(2,1)S(1)} %bitcast.26, bf16[512,512]{1,0:T(8,128)(2,1)S(1)} %bitcast.29, ...), custom_call_target="tpu_custom_call" | custom-call | flops 1000000000 | bytes 9000000 | tf_op jit(solution)/shard_map/near_backward/pallas_call | solution.py:636
  95.7 0.0 collective-permute-start.13
  95.7 0.0 collective-permute-done.10
  95.7 2.8 %collective-permute-done.11 = bf16[128,512]{1,0:T(8,128)(2,1)S(1)} collective-permute-done((bf16[128,512]{1,0:T(8,128)(2,1)S(1)}, bf16[128,512]{1,0:T(8,128)(2,1)S(1)}, u32[]{:S(2)}, u32[]{:S(2)}) %collective-permute-start.11) | collective-permute-done | bytes 131104 | tf_op jit(solution)/shard_map/ppermute | solution.py:771
  98.5 0.0 collective-permute-done.12
  98.5 0.1 add_convert_fusion.1
  98.6 0.0 all-to-all-done.2
  98.6 0.5 collective-permute-start.16
  99.1 2.8 %collective-permute-start.15 = (bf16[128,512]{1,0:T(8,128)(2,1)S(1)}, bf16[128,512]{1,0:T(8,128)(2,1)S(1)}, u32[]{:S(2)}, u32[]{:S(2)}) collective-permute-start(bf16[128,512]{1,0:T(8,128)(2,1)S(1)} %add_convert_fusion.1), channel_id=1, source_target_pairs={{0,64},{8,72},{16,80},{24,88},{32,96},{40,104},{48,112},{56,120},{... | collective-permute-start | bytes 393224 | tf_op jit(solution)/shard_map/ppermute | solution.py:775
  101.8 2.0 %collective-permute-start.14 = (bf16[128,512]{1,0:T(8,128)(2,1)S(1)}, bf16[128,512]{1,0:T(8,128)(2,1)S(1)}, u32[]{:S(2)}, u32[]{:S(2)}) collective-permute-start(bf16[128,512]{1,0:T(8,128)(2,1)S(1)} %add_convert_fusion.1), channel_id=1, source_target_pairs={{0,32},{8,40},{16,48},{24,56},{32,64},{40,72},{48,80},{56,88},{64,... | collective-permute-start | bytes 393224 | tf_op jit(solution)/shard_map/ppermute | solution.py:775
  103.9 4.0 %scatter_rows.2.refs_0_ = f32[4,1024,128]{2,1,0:T(8,128)} custom-call(s32[128,128]{1,0:T(8,128)S(1)} %copy-done.8, bf16[4096,128]{1,0:T(8,128)(2,1)S(1)} %bitcast.30), custom_call_target="tpu_custom_call" | custom-call | flops 2147483648 | bytes 2000000 | tf_op jit(solution)/shard_map/scatter_rows/pallas_call | solution.py:280
  107.9 0.5 collective-permute-done.14
  108.3 0.1 add_convert_fusion.glob0
  108.4 0.0 copy-start.6
  108.4 4.6 %collective-permute-start.19 = (bf16[128,512]{1,0:T(8,128)(2,1)S(1)}, bf16[128,512]{1,0:T(8,128)(2,1)S(1)}, u32[]{:S(2)}, u32[]{:S(2)}) collective-permute-start(bf16[128,512]{1,0:T(8,128)(2,1)S(1)} %add_convert_fusion.glob0), channel_id=1, source_target_pairs={{0,24},{8,0},{16,8},{24,16},{32,56},{40,32},{48,40},{56,48},{64,88... | collective-permute-start | bytes 393224 | tf_op jit(solution)/shard_map/ppermute | solution.py:771
  113.0 0.9 collective-permute-start.17
  114.0 4.0 %scatter_rows.3 = f32[4,1024,128]{2,1,0:T(8,128)} custom-call(s32[128,128]{1,0:T(8,128)S(1)} %copy-done.8, bf16[4096,128]{1,0:T(8,128)(2,1)S(1)} %bitcast.31, f32[4,1024,128]{2,1,0:T(8,128)} %scatter_rows.2.refs_0_), custom_call_target="tpu_custom_call", output_to_operand_aliasing={{}: (2, {})} | custom-call | flops 2147483648 | bytes 2000000 | tf_op jit(solution)/shard_map/scatter_rows/pallas_call | solution.py:280
  117.9 0.8 collective-permute-done.19.glob3
  118.8 2.2 %collective-permute-done.18.glob2 = bf16[128,512]{1,0:T(8,128)(2,1)S(1)} collective-permute-done((bf16[128,512]{1,0:T(8,128)(2,1)S(1)}, bf16[128,512]{1,0:T(8,128)(2,1)S(1)}, u32[]{:S(2)}, u32[]{:S(2)}) %collective-permute-start.18) | collective-permute-done | bytes 131104 | tf_op jit(solution)/shard_map/ppermute | solution.py:771
  120.9 1.3 %collective-permute-done.17.glob1 = bf16[128,512]{1,0:T(8,128)(2,1)S(1)} collective-permute-done((bf16[128,512]{1,0:T(8,128)(2,1)S(1)}, bf16[128,512]{1,0:T(8,128)(2,1)S(1)}, u32[]{:S(2)}, u32[]{:S(2)}) %collective-permute-start.17) | collective-permute-done | bytes 131104 | tf_op jit(solution)/shard_map/ppermute | solution.py:771
  122.2 0.0 collective-permute-done.13.edge
  122.2 1.8 %add_received.1 = (bf16[512,512]{1,0:T(8,128)(2,1)}, bf16[512,512]{1,0:T(8,128)(2,1)}) custom-call(s32[1,2]{1,0:T(1,128)} %gids.5, bf16[512,512]{1,0:T(8,128)(2,1)S(1)} %copy-done.6, bf16[512,512]{1,0:T(8,128)(2,1)S(1)} %copy-done.7, bf16[2,128,512]{2,1,0:T(8,128)(2,1)S(1)} %collective-permute-done.13.edge, bf16[128,512]{1,0:T(8,128)(2,1)S(1)} %add_convert_fusion.glob0, ...), custom_call_target="tpu_custom_call" | custom-call | flops 1000000 | bytes 3000000 | tf_op jit(solution)/shard_map/add_received/pallas_call | solution.py:749
  (15 shorter events, 0.0 us)
Async XLA Ops:
  2.3 8.8 %collective-permute-start = (bf16[128,512]{1,0:T(8,128)(2,1)S(1)}, bf16[128,512]{1,0:T(8,128)(2,1)S(1)}, u32[]{:S(2)}, u32[]{:S(2)}) collective-permute-start(bf16[128,512]{1,0:T(8,128)(2,1)S(1)} %get-tuple-element.74), channel_id=1, source_target_pairs={{0,8},{8,16},{16,24},{24,0},{32,40},{40,48},{48,56},{56,32},{64,72... | collective-permute-start | bytes 393224 | tf_op jit(solution)/shard_map/ppermute | solution.py:771
  3.9 9.4 %collective-permute-start.1 = (bf16[128,512]{1,0:T(8,128)(2,1)S(1)}, bf16[128,512]{1,0:T(8,128)(2,1)S(1)}, u32[]{:S(2)}, u32[]{:S(2)}) collective-permute-start(bf16[128,512]{1,0:T(8,128)(2,1)S(1)} %get-tuple-element.75), channel_id=1, source_target_pairs={{0,16},{8,24},{16,0},{24,8},{32,48},{40,56},{48,32},{56,40},{64,80... | collective-permute-start | bytes 393224 | tf_op jit(solution)/shard_map/ppermute | solution.py:771
  6.6 6.7 %collective-permute-start.2 = (bf16[128,512]{1,0:T(8,128)(2,1)S(1)}, bf16[128,512]{1,0:T(8,128)(2,1)S(1)}, u32[]{:S(2)}, u32[]{:S(2)}) collective-permute-start(bf16[128,512]{1,0:T(8,128)(2,1)S(1)} %get-tuple-element.76), channel_id=1, source_target_pairs={{0,24},{8,0},{16,8},{24,16},{32,56},{40,32},{48,40},{56,48},{64,88... | collective-permute-start | bytes 393224 | tf_op jit(solution)/shard_map/ppermute | solution.py:771
  10.6 9.4 %collective-permute-start.3 = (bf16[2,128,512]{2,1,0:T(8,128)(2,1)S(1)}, bf16[2,128,512]{2,1,0:T(8,128)(2,1)S(1)}, u32[]{:S(2)}, u32[]{:S(2)}) collective-permute-start(bf16[2,128,512]{2,1,0:T(8,128)(2,1)S(1)} %get-tuple-element.79), channel_id=1, source_target_pairs={{0,8},{8,16},{16,24},{24,32},{32,40},{40,48},{48,56},{56,64},{64,7... | collective-permute-start | bytes 786440 | tf_op jit(solution)/shard_map/ppermute | solution.py:762
  13.4 15.1 %collective-permute-start.6 = (bf16[128,512]{1,0:T(8,128)(2,1)S(1)}, bf16[128,512]{1,0:T(8,128)(2,1)S(1)}, u32[]{:S(2)}, u32[]{:S(2)}) collective-permute-start(bf16[128,512]{1,0:T(8,128)(2,1)S(1)} %add_convert_fusion.3), channel_id=1, source_target_pairs={{0,96},{8,104},{16,112},{24,120},{32,0},{40,8},{48,16},{56,24},{64... | collective-permute-start | bytes 393224 | tf_op jit(solution)/shard_map/ppermute | solution.py:775
  13.6 14.9 %collective-permute-start.5 = (bf16[128,512]{1,0:T(8,128)(2,1)S(1)}, bf16[128,512]{1,0:T(8,128)(2,1)S(1)}, u32[]{:S(2)}, u32[]{:S(2)}) collective-permute-start(bf16[128,512]{1,0:T(8,128)(2,1)S(1)} %add_convert_fusion.3), channel_id=1, source_target_pairs={{0,64},{8,72},{16,80},{24,88},{32,96},{40,104},{48,112},{56,120},{... | collective-permute-start | bytes 393224 | tf_op jit(solution)/shard_map/ppermute | solution.py:775
  16.9 11.6 %collective-permute-start.4 = (bf16[128,512]{1,0:T(8,128)(2,1)S(1)}, bf16[128,512]{1,0:T(8,128)(2,1)S(1)}, u32[]{:S(2)}, u32[]{:S(2)}) collective-permute-start(bf16[128,512]{1,0:T(8,128)(2,1)S(1)} %add_convert_fusion.3), channel_id=1, source_target_pairs={{0,32},{8,40},{16,48},{24,56},{32,64},{40,72},{48,80},{56,88},{64,... | collective-permute-start | bytes 393224 | tf_op jit(solution)/shard_map/ppermute | solution.py:775
  20.0 17.5 %all-to-all-start = ((s32[128,1,128]{2,1,0:T(1,128)}), s32[128,1,128]{2,1,0:T(1,128)S(1)}, u32[]{:S(2)}, u32[]{:S(2)}) async-start(s32[128,1,128]{2,1,0:T(1,128)} %bitcast.39), calls=%async_computation | async-start | bytes 131072 | tf_op jit(solution)/shard_map/all_to_all | solution.py:766
  28.6 15.4 %collective-permute-start.9 = (bf16[128,512]{1,0:T(8,128)(2,1)S(1)}, bf16[128,512]{1,0:T(8,128)(2,1)S(1)}, u32[]{:S(2)}, u32[]{:S(2)}) collective-permute-start(bf16[128,512]{1,0:T(8,128)(2,1)S(1)} %add_convert_fusion.2.glob0), channel_id=1, source_target_pairs={{0,24},{8,0},{16,8},{24,16},{32,56},{40,32},{48,40},{56,48},{64,88... | collective-permute-start | bytes 393224 | tf_op jit(solution)/shard_map/ppermute | solution.py:771
  31.4 12.6 %collective-permute-start.8 = (bf16[128,512]{1,0:T(8,128)(2,1)S(1)}, bf16[128,512]{1,0:T(8,128)(2,1)S(1)}, u32[]{:S(2)}, u32[]{:S(2)}) collective-permute-start(bf16[128,512]{1,0:T(8,128)(2,1)S(1)} %add_convert_fusion.2.glob0), channel_id=1, source_target_pairs={{0,16},{8,24},{16,0},{24,8},{32,48},{40,56},{48,32},{56,40},{64,80... | collective-permute-start | bytes 393224 | tf_op jit(solution)/shard_map/ppermute | solution.py:771
  32.2 11.8 %collective-permute-start.7 = (bf16[128,512]{1,0:T(8,128)(2,1)S(1)}, bf16[128,512]{1,0:T(8,128)(2,1)S(1)}, u32[]{:S(2)}, u32[]{:S(2)}) collective-permute-start(bf16[128,512]{1,0:T(8,128)(2,1)S(1)} %add_convert_fusion.2.glob0), channel_id=1, source_target_pairs={{0,8},{8,16},{16,24},{24,0},{32,40},{40,48},{48,56},{56,32},{64,72... | collective-permute-start | bytes 393224 | tf_op jit(solution)/shard_map/ppermute | solution.py:771
  44.0 5.1 %copy-start = (bf16[1,512,512]{2,1,0:T(8,128)(2,1)S(1)}, bf16[1,512,512]{2,1,0:T(8,128)(2,1)}, u32[]{:S(2)}) copy-start(bf16[1,512,512]{2,1,0:T(8,128)(2,1)} %param.11) | copy-start | bytes 1572868
  44.0 5.1 %copy-start.4 = (bf16[1,512,512]{2,1,0:T(8,128)(2,1)S(1)}, bf16[1,512,512]{2,1,0:T(8,128)(2,1)}, u32[]{:S(2)}) copy-start(bf16[1,512,512]{2,1,0:T(8,128)(2,1)} %param.12) | copy-start | bytes 1572868
  44.0 5.1 %copy-start.5 = (bf16[1,512,512]{2,1,0:T(8,128)(2,1)S(1)}, bf16[1,512,512]{2,1,0:T(8,128)(2,1)}, u32[]{:S(2)}) copy-start(bf16[1,512,512]{2,1,0:T(8,128)(2,1)} %param.13) | copy-start | bytes 1572868
  44.0 23.9 %all-to-all-start.1 = ((bf16[128,32,128]{2,1,0:T(8,128)(2,1)}), bf16[128,32,128]{2,1,0:T(8,128)(2,1)S(1)}, u32[]{:S(2)}, u32[]{:S(2)}) async-start(bf16[128,32,128]{2,1,0:T(8,128)(2,1)} %bitcast.37), calls=%async_computation.1 | async-start | bytes 2097152 | tf_op jit(solution)/shard_map/all_to_all | solution.py:766
  73.4 25.2 %all-to-all-start.2 = ((bf16[128,32,128]{2,1,0:T(8,128)(2,1)}), bf16[128,32,128]{2,1,0:T(8,128)(2,1)S(1)}, u32[]{:S(2)}, u32[]{:S(2)}) async-start(bf16[128,32,128]{2,1,0:T(8,128)(2,1)} %bitcast.36), calls=%async_computation.2 | async-start | bytes 2097152 | tf_op jit(solution)/shard_map/all_to_all | solution.py:766
  78.3 12.4 %copy-start.1 = (bf16[1,512,512]{2,1,0:T(8,128)(2,1)S(1)}, bf16[1,512,512]{2,1,0:T(8,128)(2,1)}, u32[]{:S(2)}) copy-start(bf16[1,512,512]{2,1,0:T(8,128)(2,1)} %param.11) | copy-start | bytes 1572868
  78.3 12.4 %copy-start.2 = (bf16[8,512,256]{2,1,0:T(8,128)(2,1)S(1)}, bf16[8,512,256]{2,1,0:T(8,128)(2,1)}, u32[]{:S(2)}) copy-start(bf16[8,512,256]{2,1,0:T(8,128)(2,1)} %get-tuple-element.102.probs) | copy-start | bytes 6291460
  78.3 12.3 %copy-start.3 = (bf16[8,512,256]{2,1,0:T(8,128)(2,1)S(1)}, bf16[8,512,256]{2,1,0:T(8,128)(2,1)}, u32[]{:S(2)}) copy-start(bf16[8,512,256]{2,1,0:T(8,128)(2,1)} %get-tuple-element.103.slope) | copy-start | bytes 6291460
  84.9 10.7 %collective-permute-start.10 = (bf16[128,512]{1,0:T(8,128)(2,1)S(1)}, bf16[128,512]{1,0:T(8,128)(2,1)S(1)}, u32[]{:S(2)}, u32[]{:S(2)}) collective-permute-start(bf16[128,512]{1,0:T(8,128)(2,1)S(1)} %get-tuple-element.108), channel_id=1, source_target_pairs={{0,8},{8,16},{16,24},{24,0},{32,40},{40,48},{48,56},{56,32},{64,72... | collective-permute-start | bytes 393224 | tf_op jit(solution)/shard_map/ppermute | solution.py:771
  86.5 12.0 %collective-permute-start.11 = (bf16[128,512]{1,0:T(8,128)(2,1)S(1)}, bf16[128,512]{1,0:T(8,128)(2,1)S(1)}, u32[]{:S(2)}, u32[]{:S(2)}) collective-permute-start(bf16[128,512]{1,0:T(8,128)(2,1)S(1)} %get-tuple-element.109), channel_id=1, source_target_pairs={{0,16},{8,24},{16,0},{24,8},{32,48},{40,56},{48,32},{56,40},{64,80... | collective-permute-start | bytes 393224 | tf_op jit(solution)/shard_map/ppermute | solution.py:771
  89.2 9.3 %collective-permute-start.12 = (bf16[128,512]{1,0:T(8,128)(2,1)S(1)}, bf16[128,512]{1,0:T(8,128)(2,1)S(1)}, u32[]{:S(2)}, u32[]{:S(2)}) collective-permute-start(bf16[128,512]{1,0:T(8,128)(2,1)S(1)} %get-tuple-element.110), channel_id=1, source_target_pairs={{0,24},{8,0},{16,8},{24,16},{32,56},{40,32},{48,40},{56,48},{64,88... | collective-permute-start | bytes 393224 | tf_op jit(solution)/shard_map/ppermute | solution.py:771
  90.7 13.2 %copy-start.8 = (s32[128,128]{1,0:T(8,128)S(1)}, s32[128,128]{1,0:T(8,128)}, u32[]{:S(2)}) copy-start(s32[128,128]{1,0:T(8,128)} %get-tuple-element.114.asked) | copy-start | bytes 196612
  95.7 26.5 %collective-permute-start.13 = (bf16[2,128,512]{2,1,0:T(8,128)(2,1)S(1)}, bf16[2,128,512]{2,1,0:T(8,128)(2,1)S(1)}, u32[]{:S(2)}, u32[]{:S(2)}) collective-permute-start(bf16[2,128,512]{2,1,0:T(8,128)(2,1)S(1)} %get-tuple-element.113), channel_id=1, source_target_pairs={{0,120},{8,0},{16,8},{24,16},{32,24},{40,32},{48,40},{56,48},{64,5... | collective-permute-start | bytes 786440 | tf_op jit(solution)/shard_map/ppermute | solution.py:762
  98.6 9.3 %collective-permute-start.16 = (bf16[128,512]{1,0:T(8,128)(2,1)S(1)}, bf16[128,512]{1,0:T(8,128)(2,1)S(1)}, u32[]{:S(2)}, u32[]{:S(2)}) collective-permute-start(bf16[128,512]{1,0:T(8,128)(2,1)S(1)} %add_convert_fusion.1), channel_id=1, source_target_pairs={{0,96},{8,104},{16,112},{24,120},{32,0},{40,8},{48,16},{56,24},{64... | collective-permute-start | bytes 393224 | tf_op jit(solution)/shard_map/ppermute | solution.py:775
  99.1 8.8 %collective-permute-start.15 = (bf16[128,512]{1,0:T(8,128)(2,1)S(1)}, bf16[128,512]{1,0:T(8,128)(2,1)S(1)}, u32[]{:S(2)}, u32[]{:S(2)}) collective-permute-start(bf16[128,512]{1,0:T(8,128)(2,1)S(1)} %add_convert_fusion.1), channel_id=1, source_target_pairs={{0,64},{8,72},{16,80},{24,88},{32,96},{40,104},{48,112},{56,120},{... | collective-permute-start | bytes 393224 | tf_op jit(solution)/shard_map/ppermute | solution.py:775
  101.8 6.5 %collective-permute-start.14 = (bf16[128,512]{1,0:T(8,128)(2,1)S(1)}, bf16[128,512]{1,0:T(8,128)(2,1)S(1)}, u32[]{:S(2)}, u32[]{:S(2)}) collective-permute-start(bf16[128,512]{1,0:T(8,128)(2,1)S(1)} %add_convert_fusion.1), channel_id=1, source_target_pairs={{0,32},{8,40},{16,48},{24,56},{32,64},{40,72},{48,80},{56,88},{64,... | collective-permute-start | bytes 393224 | tf_op jit(solution)/shard_map/ppermute | solution.py:775
  108.4 13.8 %copy-start.6 = (bf16[512,512]{1,0:T(8,128)(2,1)S(1)}, bf16[512,512]{1,0:T(8,128)(2,1)}, u32[]{:S(2)}) copy-start(bf16[512,512]{1,0:T(8,128)(2,1)} %get-tuple-element.111.d_k) | copy-start | bytes 1572868
  108.4 13.8 %copy-start.7 = (bf16[512,512]{1,0:T(8,128)(2,1)S(1)}, bf16[512,512]{1,0:T(8,128)(2,1)}, u32[]{:S(2)}) copy-start(bf16[512,512]{1,0:T(8,128)(2,1)} %get-tuple-element.112.d_v) | copy-start | bytes 1572868
  108.4 10.3 %collective-permute-start.19 = (bf16[128,512]{1,0:T(8,128)(2,1)S(1)}, bf16[128,512]{1,0:T(8,128)(2,1)S(1)}, u32[]{:S(2)}, u32[]{:S(2)}) collective-permute-start(bf16[128,512]{1,0:T(8,128)(2,1)S(1)} %add_convert_fusion.glob0), channel_id=1, source_target_pairs={{0,24},{8,0},{16,8},{24,16},{32,56},{40,32},{48,40},{56,48},{64,88... | collective-permute-start | bytes 393224 | tf_op jit(solution)/shard_map/ppermute | solution.py:771
  113.0 7.9 %collective-permute-start.18 = (bf16[128,512]{1,0:T(8,128)(2,1)S(1)}, bf16[128,512]{1,0:T(8,128)(2,1)S(1)}, u32[]{:S(2)}, u32[]{:S(2)}) collective-permute-start(bf16[128,512]{1,0:T(8,128)(2,1)S(1)} %add_convert_fusion.glob0), channel_id=1, source_target_pairs={{0,16},{8,24},{16,0},{24,8},{32,48},{40,56},{48,32},{56,40},{64,80... | collective-permute-start | bytes 393224 | tf_op jit(solution)/shard_map/ppermute | solution.py:771
  113.0 9.2 %collective-permute-start.17 = (bf16[128,512]{1,0:T(8,128)(2,1)S(1)}, bf16[128,512]{1,0:T(8,128)(2,1)S(1)}, u32[]{:S(2)}, u32[]{:S(2)}) collective-permute-start(bf16[128,512]{1,0:T(8,128)(2,1)S(1)} %add_convert_fusion.glob0), channel_id=1, source_target_pairs={{0,8},{8,16},{16,24},{24,0},{32,40},{40,48},{48,56},{56,32},{64,72... | collective-permute-start | bytes 393224 | tf_op jit(solution)/shard_map/ppermute | solution.py:771

commit v6 on v5

--- a/solution.py
+++ b/solution.py
@@ -805,18 +805,18 @@
     parts = from_x(cand)
     owner, _ = together(owner, cand[0])
     req, code = route(owner, row)
-    tail, _ = together(tail, req)
-    halo = from_behind(tail, "seq", 1)
     req, *parts = together(req, *parts)
     mine = add_all(parts)
     parts = from_z(mine)
-    req, halo, _ = together(req, halo, mine)
+    req, _ = together(req, mine)
     asked = exchange(req.reshape(NDEV, 1, E), ("seq", "user")).reshape(NDEV, E)
     mine = add_all(parts)
     glob = share_x(mine)
+    tail, _ = together(tail, mine)
+    halo = from_behind(tail, "seq", 1)
     asked, _ = together(asked, mine)
     found, asked = gather(asked, table)
-    found, *glob = together(found, *glob)
+    found, halo, *glob = together(found, halo, *glob)
     items = exchange(found.reshape(NDEV, SLOTS, E), ("seq", "user")).reshape(NDEV * SLOTS, E)
     near_p, near_f, near = near_forward(lengths, q, k, v, halo)
     far_p, far_f, normed, inv, user = far_forward(

time: 125 us -> 128 us (1.024)
  starting transfers between devices: 51.3 us -> 52.9 us
    ppermute x2, waiting for transfers between devices: 1.05 us -> 2.56 us  [from_behind(): lax.ppermute(block, axis, [(i, (i + distance) % size) for i in range(size)])]
  transfers between devices with their start and end apart: 23 -> 23, of which waited for: 9 -> 9; matrix products, arithmetic and copies ran while one was open for 0% -> 0% of each run, Pallas kernels for 32% -> 31%
where the time goes in v6:
time: 128 us; the launch traced here: 127 us
  starting transfers between devices  52.9 us (41%)
  Pallas kernels  48.4 us (38%)
  waiting for transfers between devices  24.3 us (19%)
    ppermute x12, starting transfers between devices, around_x(): return lax.ppermute(x, 'seq', pairs)  21.6 us
    all_to_all x3, starting transfers between devices, exchange(): return lax.all_to_all(x, axis, split_axis=0, concat_axis=0, tiled=True)  19.7 us
    all_to_all x3, waiting for transfers between devices, exchange(): return lax.all_to_all(x, axis, split_axis=0, concat_axis=0, tiled=True)  12.3 us
    ppermute x6, starting transfers between devices, around_z(): lax.ppermute(x, 'seq', [(i, (i + distance * XSIZE) % NSEQ) for i in range...  11 us
    ppermute x12, waiting for transfers between devices, around_x(): return lax.ppermute(x, 'seq', pairs)  8.98 us
    pallas_call x2, Pallas kernels, scatter(): pl.pallas_call(functools.partial(scatter_kernel, start), grid=(steps,), o...  7.96 us
    pallas_call x1, Pallas kernels, far_backward(): pl.pallas_call(far_backward_kernel, grid=(PAIRS,), out_shape=(fast((EVENT...  6.61 us
    pallas_call x1, Pallas kernels, gather(): pl.pallas_call(gather_kernel, out_shape=(slow((NDEV * SLOTS, E), BF), slo...  6.48 us
  transfers between devices with their start and end apart: 23, of which 9 were waited for; matrix products, arithmetic and copies ran while one was open for 0% of the time, Pallas kernels for 31%

profile of v6, /device:TPU:32, one launch (start us, length us, event | category | flops | bytes accessed | tf_op | source)
XLA Modules:
  0.0 126.9 jit_solution(9478824666033816174)
XLA Ops:
  0.6 1.7 %pieces.1 = (bf16[2,128,512]{2,1,0:T(8,128)(2,1)S(1)}, bf16[128,512]{1,0:T(8,128)(2,1)S(1)}, bf16[128,512]{1,0:T(8,128)(2,1)S(1)}, bf16[128,512]{1,0:T(8,128)(2,1)S(1)}, bf16[128,512]{1,0:T(8,128)(2,1)S(1)}) custom-call(s32[1,2]{1,0:T(1,128)} %gids.5, bf16[512,512]{1,0:T(8,128)(2,1)} %bitcast.24, bf16[512,512]{1,0:T(8,128)(2,1)} %bitcast.27), custom_call_target="tpu_custom_call" | custom-call | flops 1000000 | bytes 2000000 | tf_op jit(solution)/shard_map/pieces/pallas_call | solution.py:121
  2.3 1.6 %collective-permute-start = (bf16[128,512]{1,0:T(8,128)(2,1)S(1)}, bf16[128,512]{1,0:T(8,128)(2,1)S(1)}, u32[]{:S(2)}, u32[]{:S(2)}) collective-permute-start(bf16[128,512]{1,0:T(8,128)(2,1)S(1)} %get-tuple-element.74), channel_id=1, source_target_pairs={{0,8},{8,16},{16,24},{24,0},{32,40},{40,48},{48,56},{56,32},{64,72... | collective-permute-start | bytes 393224 | tf_op jit(solution)/shard_map/ppermute | solution.py:771
  3.9 2.7 %collective-permute-start.1 = (bf16[128,512]{1,0:T(8,128)(2,1)S(1)}, bf16[128,512]{1,0:T(8,128)(2,1)S(1)}, u32[]{:S(2)}, u32[]{:S(2)}) collective-permute-start(bf16[128,512]{1,0:T(8,128)(2,1)S(1)} %get-tuple-element.75), channel_id=1, source_target_pairs={{0,16},{8,24},{16,0},{24,8},{32,48},{40,56},{48,32},{56,40},{64,80... | collective-permute-start | bytes 393224 | tf_op jit(solution)/shard_map/ppermute | solution.py:771
  6.6 1.6 %collective-permute-start.2 = (bf16[128,512]{1,0:T(8,128)(2,1)S(1)}, bf16[128,512]{1,0:T(8,128)(2,1)S(1)}, u32[]{:S(2)}, u32[]{:S(2)}) collective-permute-start(bf16[128,512]{1,0:T(8,128)(2,1)S(1)} %get-tuple-element.76), channel_id=1, source_target_pairs={{0,24},{8,0},{16,8},{24,16},{32,56},{40,32},{48,40},{56,48},{64,88... | collective-permute-start | bytes 393224 | tf_op jit(solution)/shard_map/ppermute | solution.py:771
  8.2 2.5 %route.1 = (s32[128,128]{1,0:T(8,128)}, bf16[128,512]{1,0:T(8,128)(2,1)}) custom-call(s32[5,1,512]{2,1,0:T(1,128)} %bitcast.44, s32[5,1,512]{2,1,0:T(1,128)} %bitcast.45), custom_call_target="tpu_custom_call" | custom-call | flops 100000000 | bytes 1000000 | tf_op jit(solution)/shard_map/route/pallas_call | solution.py:154
  10.7 0.0 collective-permute-done
  10.7 1.9 %collective-permute-done.1 = bf16[128,512]{1,0:T(8,128)(2,1)S(1)} collective-permute-done((bf16[128,512]{1,0:T(8,128)(2,1)S(1)}, bf16[128,512]{1,0:T(8,128)(2,1)S(1)}, u32[]{:S(2)}, u32[]{:S(2)}) %collective-permute-start.1) | collective-permute-done | bytes 131104 | tf_op jit(solution)/shard_map/ppermute | solution.py:771
  12.6 0.0 collective-permute-done.2
  12.6 0.1 add_convert_fusion.3
  12.7 0.2 collective-permute-start.5
  12.9 3.3 %collective-permute-start.4 = (bf16[128,512]{1,0:T(8,128)(2,1)S(1)}, bf16[128,512]{1,0:T(8,128)(2,1)S(1)}, u32[]{:S(2)}, u32[]{:S(2)}) collective-permute-start(bf16[128,512]{1,0:T(8,128)(2,1)S(1)} %add_convert_fusion.3), channel_id=1, source_target_pairs={{0,64},{8,72},{16,80},{24,88},{32,96},{40,104},{48,112},{56,120},{... | collective-permute-start | bytes 393224 | tf_op jit(solution)/shard_map/ppermute | solution.py:775
  16.2 2.2 %collective-permute-start.3 = (bf16[128,512]{1,0:T(8,128)(2,1)S(1)}, bf16[128,512]{1,0:T(8,128)(2,1)S(1)}, u32[]{:S(2)}, u32[]{:S(2)}) collective-permute-start(bf16[128,512]{1,0:T(8,128)(2,1)S(1)} %add_convert_fusion.3), channel_id=1, source_target_pairs={{0,32},{8,40},{16,48},{24,56},{32,64},{40,72},{48,80},{56,88},{64,... | collective-permute-start | bytes 393224 | tf_op jit(solution)/shard_map/ppermute | solution.py:775
  18.4 7.8 %all-to-all-start = ((s32[128,1,128]{2,1,0:T(1,128)}), s32[128,1,128]{2,1,0:T(1,128)S(1)}, u32[]{:S(2)}, u32[]{:S(2)}) async-start(s32[128,1,128]{2,1,0:T(1,128)} %bitcast.39), calls=%async_computation | async-start | bytes 131072 | tf_op jit(solution)/shard_map/all_to_all | solution.py:766
  26.2 0.0 collective-permute-done.5
  26.2 0.0 collective-permute-done.4
  26.2 0.0 collective-permute-done.3
  26.2 0.1 add_convert_fusion.2.glob0
  26.3 2.8 %collective-permute-start.9 = (bf16[128,512]{1,0:T(8,128)(2,1)S(1)}, bf16[128,512]{1,0:T(8,128)(2,1)S(1)}, u32[]{:S(2)}, u32[]{:S(2)}) collective-permute-start(bf16[128,512]{1,0:T(8,128)(2,1)S(1)} %add_convert_fusion.2.glob0), channel_id=1, source_target_pairs={{0,24},{8,0},{16,8},{24,16},{32,56},{40,32},{48,40},{56,48},{64,88... | collective-permute-start | bytes 393224 | tf_op jit(solution)/shard_map/ppermute | solution.py:771
  29.1 0.8 collective-permute-start.8
  29.9 0.9 collective-permute-start.7
  30.8 4.4 %all-to-all-done = s32[128,1,128]{2,1,0:T(1,128)S(1)} async-done(((s32[128,1,128]{2,1,0:T(1,128)}), s32[128,1,128]{2,1,0:T(1,128)S(1)}, u32[]{:S(2)}, u32[]{:S(2)}) %all-to-all-start) | async-done | bytes 65568 | tf_op jit(solution)/shard_map/all_to_all | solution.py:766
  35.2 0.6 collective-permute-start.6
  35.7 6.5 %gather_rows.1 = (bf16[4096,128]{1,0:T(8,128)(2,1)}, s32[128,128]{1,0:T(8,128)}) custom-call(s32[128,128]{1,0:T(8,128)S(1)} %bitcast.33, bf16[4096,128]{1,0:T(8,128)(2,1)} %table_far.1), custom_call_target="tpu_custom_call" | custom-call | flops 4294967296 | bytes 2000000 | tf_op jit(solution)/shard_map/gather_rows/pallas_call | solution.py:229
  42.2 0.0 copy-start
  42.3 0.0 copy-start.4
  42.3 0.0 copy-start.5
  42.3 0.0 collective-permute-done.9.glob3
  42.3 0.0 collective-permute-done.8.glob2
  42.3 0.0 collective-permute-done.7.glob1
  42.3 2.6 %collective-permute-done.6.halo = bf16[2,128,512]{2,1,0:T(8,128)(2,1)S(1)} collective-permute-done((bf16[2,128,512]{2,1,0:T(8,128)(2,1)S(1)}, bf16[2,128,512]{2,1,0:T(8,128)(2,1)S(1)}, u32[]{:S(2)}, u32[]{:S(2)}) %collective-permute-start.6) | collective-permute-done | bytes 262176 | tf_op jit(solution)/shard_map/ppermute | solution.py:762
  44.9 7.0 %all-to-all-start.1 = ((bf16[128,32,128]{2,1,0:T(8,128)(2,1)}), bf16[128,32,128]{2,1,0:T(8,128)(2,1)S(1)}, u32[]{:S(2)}, u32[]{:S(2)}) async-start(bf16[128,32,128]{2,1,0:T(8,128)(2,1)} %bitcast.37), calls=%async_computation.1 | async-start | bytes 2097152 | tf_op jit(solution)/shard_map/all_to_all | solution.py:766
  51.9 4.6 %near_forward.1 = (bf16[8,512,256]{2,1,0:T(8,128)(2,1)}, bf16[8,512,256]{2,1,0:T(8,128)(2,1)}, f32[512,512]{1,0:T(8,128)S(1)}) custom-call(s32[8]{0:T(128)} %lengths.5, bf16[512,512]{1,0:T(8,128)(2,1)S(1)} %bitcast.21, bf16[512,512]{1,0:T(8,128)(2,1)S(1)} %bitcast.25, bf16[512,512]{1,0:T(8,128)(2,1)S(1)} %bitcast.28, ...), custom_call_target="tpu_custom_call" | custom-call | flops 500000000 | bytes 7000000 | tf_op jit(solution)/shard_map/near_forward/pallas_call | solution.py:428
  56.5 6.3 %far_forward.1 = (bf16[8,512,256]{2,1,0:T(8,128)(2,1)}, bf16[8,512,256]{2,1,0:T(8,128)(2,1)}, bf16[512,512]{1,0:T(8,128)(2,1)}, f32[512,1]{1,0:T(8,128)}, bf16[512,256]{1,0:T(8,128)(2,1)}) custom-call(s32[8]{0:T(128)} %lengths.5, s32[1,2]{1,0:T(1,128)} %gids.5, bf16[512,512]{1,0:T(8,128)(2,1)S(1)} %bitcast.22, bf16[128,512]{1,0:T(8,128)(2,1)S(1)} %add_convert_fusion.2.glob0, ...), custom_call_target="tpu_custom_call" | custom-call | flops 600000000 | bytes 9000000 | tf_op jit(solution)/shard_map/far_forward/pallas_call | solution.py:443
  62.8 7.9 %all-to-all-done.1 = bf16[128,32,128]{2,1,0:T(8,128)(2,1)S(1)} async-done(((bf16[128,32,128]{2,1,0:T(8,128)(2,1)}), bf16[128,32,128]{2,1,0:T(8,128)(2,1)S(1)}, u32[]{:S(2)}, u32[]{:S(2)}) %all-to-all-start.1) | async-done | bytes 1048608 | tf_op jit(solution)/shard_map/all_to_all | solution.py:766
  70.7 5.5 %ranking.1 = (bf16[4096,128]{1,0:T(8,128)(2,1)}, bf16[512,128]{1,0:T(8,128)(2,1)}) custom-call(s32[8]{0:T(128)} %lengths.5, bf16[4096,128]{1,0:T(8,128)(2,1)S(1)} %bitcast.32, bf16[128,512]{1,0:T(8,128)(2,1)} %get-tuple-element.89.code, bf16[512,256]{1,0:T(8,128)(2,1)} %get-tuple-element.95.user), custom_call_target="tpu_custom_call" | custom-call | flops 2000000000 | bytes 6000000 | tf_op jit(solution)/shard_map/ranking/pallas_call | solution.py:709
  76.2 4.9 %all-to-all-start.2 = ((bf16[128,32,128]{2,1,0:T(8,128)(2,1)}), bf16[128,32,128]{2,1,0:T(8,128)(2,1)S(1)}, u32[]{:S(2)}, u32[]{:S(2)}) async-start(bf16[128,32,128]{2,1,0:T(8,128)(2,1)} %bitcast.36), calls=%async_computation.2 | async-start | bytes 2097152 | tf_op jit(solution)/shard_map/all_to_all | solution.py:766
  81.1 0.0 copy-start.1
  81.1 0.0 copy-start.2
  81.1 6.6 %far_backward.1 = (f32[512,512]{1,0:T(8,128)S(1)}, bf16[128,512]{1,0:T(8,128)(2,1)S(1)}, bf16[128,512]{1,0:T(8,128)(2,1)S(1)}, bf16[128,512]{1,0:T(8,128)(2,1)S(...) custom-call(bf16[512,128]{1,0:T(8,128)(2,1)} %get-tuple-element.96.d_user, ...), custom_call_target="tpu_custom_call" | custom-call | flops 1000000000 | bytes 7000000 | tf_op jit(solution)/shard_map/far_backward/pallas_call | solution.py:561
  87.8 1.5 %collective-permute-start.10 = (bf16[128,512]{1,0:T(8,128)(2,1)S(1)}, bf16[128,512]{1,0:T(8,128)(2,1)S(1)}, u32[]{:S(2)}, u32[]{:S(2)}) collective-permute-start(bf16[128,512]{1,0:T(8,128)(2,1)S(1)} %get-tuple-element.108), channel_id=1, source_target_pairs={{0,8},{8,16},{16,24},{24,0},{32,40},{40,48},{48,56},{56,32},{64,72... | collective-permute-start | bytes 393224 | tf_op jit(solution)/shard_map/ppermute | solution.py:771
  89.3 2.7 %collective-permute-start.11 = (bf16[128,512]{1,0:T(8,128)(2,1)S(1)}, bf16[128,512]{1,0:T(8,128)(2,1)S(1)}, u32[]{:S(2)}, u32[]{:S(2)}) collective-permute-start(bf16[128,512]{1,0:T(8,128)(2,1)S(1)} %get-tuple-element.109), channel_id=1, source_target_pairs={{0,16},{8,24},{16,0},{24,8},{32,48},{40,56},{48,32},{56,40},{64,80... | collective-permute-start | bytes 393224 | tf_op jit(solution)/shard_map/ppermute | solution.py:771
  92.0 1.4 %collective-permute-start.12 = (bf16[128,512]{1,0:T(8,128)(2,1)S(1)}, bf16[128,512]{1,0:T(8,128)(2,1)S(1)}, u32[]{:S(2)}, u32[]{:S(2)}) collective-permute-start(bf16[128,512]{1,0:T(8,128)(2,1)S(1)} %get-tuple-element.110), channel_id=1, source_target_pairs={{0,24},{8,0},{16,8},{24,16},{32,56},{40,32},{48,40},{56,48},{64,88... | collective-permute-start | bytes 393224 | tf_op jit(solution)/shard_map/ppermute | solution.py:771
  93.5 5.0 %near_backward.1 = (bf16[512,512]{1,0:T(8,128)(2,1)}, bf16[512,512]{1,0:T(8,128)(2,1)}, bf16[512,512]{1,0:T(8,128)(2,1)}, bf16[2,128,512]{2,1,0:T(8,128)(2,1)S(1)}) custom-call(bf16[512,512]{1,0:T(8,128)(2,1)S(1)} %bitcast.23, bf16[512,512]{1,0:T(8,128)(2,1)S(1)} %bitcast.26, bf16[512,512]{1,0:T(8,128)(2,1)S(1)} %bitcast.29, ...), custom_call_target="tpu_custom_call" | custom-call | flops 1000000000 | bytes 9000000 | tf_op jit(solution)/shard_map/near_backward/pallas_call | solution.py:636
  98.5 0.0 collective-permute-start.13
  98.5 0.0 collective-permute-done.10
  98.5 2.8 %collective-permute-done.11 = bf16[128,512]{1,0:T(8,128)(2,1)S(1)} collective-permute-done((bf16[128,512]{1,0:T(8,128)(2,1)S(1)}, bf16[128,512]{1,0:T(8,128)(2,1)S(1)}, u32[]{:S(2)}, u32[]{:S(2)}) %collective-permute-start.11) | collective-permute-done | bytes 131104 | tf_op jit(solution)/shard_map/ppermute | solution.py:771
  101.3 0.0 collective-permute-done.12
  101.3 0.1 add_convert_fusion.1
  101.4 0.5 collective-permute-start.16
  101.9 2.8 %collective-permute-start.15 = (bf16[128,512]{1,0:T(8,128)(2,1)S(1)}, bf16[128,512]{1,0:T(8,128)(2,1)S(1)}, u32[]{:S(2)}, u32[]{:S(2)}) collective-permute-start(bf16[128,512]{1,0:T(8,128)(2,1)S(1)} %add_convert_fusion.1), channel_id=1, source_target_pairs={{0,64},{8,72},{16,80},{24,88},{32,96},{40,104},{48,112},{56,120},{... | collective-permute-start | bytes 393224 | tf_op jit(solution)/shard_map/ppermute | solution.py:775
  104.6 2.0 %collective-permute-start.14 = (bf16[128,512]{1,0:T(8,128)(2,1)S(1)}, bf16[128,512]{1,0:T(8,128)(2,1)S(1)}, u32[]{:S(2)}, u32[]{:S(2)}) collective-permute-start(bf16[128,512]{1,0:T(8,128)(2,1)S(1)} %add_convert_fusion.1), channel_id=1, source_target_pairs={{0,32},{8,40},{16,48},{24,56},{32,64},{40,72},{48,80},{56,88},{64,... | collective-permute-start | bytes 393224 | tf_op jit(solution)/shard_map/ppermute | solution.py:775
  106.7 4.0 %scatter_rows.2.refs_0_ = f32[4,1024,128]{2,1,0:T(8,128)} custom-call(s32[128,128]{1,0:T(8,128)S(1)} %copy-done.8, bf16[4096,128]{1,0:T(8,128)(2,1)S(1)} %bitcast.30), custom_call_target="tpu_custom_call" | custom-call | flops 2147483648 | bytes 2000000 | tf_op jit(solution)/shard_map/scatter_rows/pallas_call | solution.py:280
  110.7 0.0 collective-permute-done.15
  110.7 0.5 collective-permute-done.14
  111.2 0.1 add_convert_fusion.glob0
  111.2 0.0 copy-start.6
  111.3 4.6 %collective-permute-start.19 = (bf16[128,512]{1,0:T(8,128)(2,1)S(1)}, bf16[128,512]{1,0:T(8,128)(2,1)S(1)}, u32[]{:S(2)}, u32[]{:S(2)}) collective-permute-start(bf16[128,512]{1,0:T(8,128)(2,1)S(1)} %add_convert_fusion.glob0), channel_id=1, source_target_pairs={{0,24},{8,0},{16,8},{24,16},{32,56},{40,32},{48,40},{56,48},{64,88... | collective-permute-start | bytes 393224 | tf_op jit(solution)/shard_map/ppermute | solution.py:771
  115.9 0.0 collective-permute-start.18
  115.9 0.9 collective-permute-start.17
  116.8 4.0 %scatter_rows.3 = f32[4,1024,128]{2,1,0:T(8,128)} custom-call(s32[128,128]{1,0:T(8,128)S(1)} %copy-done.8, bf16[4096,128]{1,0:T(8,128)(2,1)S(1)} %bitcast.31, f32[4,1024,128]{2,1,0:T(8,128)} %scatter_rows.2.refs_0_), custom_call_target="tpu_custom_call", output_to_operand_aliasing={{}: (2, {})} | custom-call | flops 2147483648 | bytes 2000000 | tf_op jit(solution)/shard_map/scatter_rows/pallas_call | solution.py:280
  120.8 0.8 collective-permute-done.19.glob3
  121.6 2.2 %collective-permute-done.18.glob2 = bf16[128,512]{1,0:T(8,128)(2,1)S(1)} collective-permute-done((bf16[128,512]{1,0:T(8,128)(2,1)S(1)}, bf16[128,512]{1,0:T(8,128)(2,1)S(1)}, u32[]{:S(2)}, u32[]{:S(2)}) %collective-permute-start.18) | collective-permute-done | bytes 131104 | tf_op jit(solution)/shard_map/ppermute | solution.py:771
  123.8 1.3 collective-permute-done.17.glob1
  125.0 1.8 %add_received.1 = (bf16[512,512]{1,0:T(8,128)(2,1)}, bf16[512,512]{1,0:T(8,128)(2,1)}) custom-call(s32[1,2]{1,0:T(1,128)} %gids.5, bf16[512,512]{1,0:T(8,128)(2,1)S(1)} %copy-done.6, bf16[512,512]{1,0:T(8,128)(2,1)S(1)} %copy-done.7, bf16[2,128,512]{2,1,0:T(8,128)(2,1)S(1)} %collective-permute-done.13.edge, bf16[128,512]{1,0:T(8,128)(2,1)S(1)} %add_convert_fusion.glob0, ...), custom_call_target="tpu_custom_call" | custom-call | flops 1000000 | bytes 3000000 | tf_op jit(solution)/shard_map/add_received/pallas_call | solution.py:749
  (15 shorter events, 0.0 us)
Async XLA Ops:
  2.3 8.4 %collective-permute-start = (bf16[128,512]{1,0:T(8,128)(2,1)S(1)}, bf16[128,512]{1,0:T(8,128)(2,1)S(1)}, u32[]{:S(2)}, u32[]{:S(2)}) collective-permute-start(bf16[128,512]{1,0:T(8,128)(2,1)S(1)} %get-tuple-element.74), channel_id=1, source_target_pairs={{0,8},{8,16},{16,24},{24,0},{32,40},{40,48},{48,56},{56,32},{64,72... | collective-permute-start | bytes 393224 | tf_op jit(solution)/shard_map/ppermute | solution.py:771
  3.9 8.7 %collective-permute-start.1 = (bf16[128,512]{1,0:T(8,128)(2,1)S(1)}, bf16[128,512]{1,0:T(8,128)(2,1)S(1)}, u32[]{:S(2)}, u32[]{:S(2)}) collective-permute-start(bf16[128,512]{1,0:T(8,128)(2,1)S(1)} %get-tuple-element.75), channel_id=1, source_target_pairs={{0,16},{8,24},{16,0},{24,8},{32,48},{40,56},{48,32},{56,40},{64,80... | collective-permute-start | bytes 393224 | tf_op jit(solution)/shard_map/ppermute | solution.py:771
  6.6 6.0 %collective-permute-start.2 = (bf16[128,512]{1,0:T(8,128)(2,1)S(1)}, bf16[128,512]{1,0:T(8,128)(2,1)S(1)}, u32[]{:S(2)}, u32[]{:S(2)}) collective-permute-start(bf16[128,512]{1,0:T(8,128)(2,1)S(1)} %get-tuple-element.76), channel_id=1, source_target_pairs={{0,24},{8,0},{16,8},{24,16},{32,56},{40,32},{48,40},{56,48},{64,88... | collective-permute-start | bytes 393224 | tf_op jit(solution)/shard_map/ppermute | solution.py:771
  12.7 13.5 %collective-permute-start.5 = (bf16[128,512]{1,0:T(8,128)(2,1)S(1)}, bf16[128,512]{1,0:T(8,128)(2,1)S(1)}, u32[]{:S(2)}, u32[]{:S(2)}) collective-permute-start(bf16[128,512]{1,0:T(8,128)(2,1)S(1)} %add_convert_fusion.3), channel_id=1, source_target_pairs={{0,96},{8,104},{16,112},{24,120},{32,0},{40,8},{48,16},{56,24},{64... | collective-permute-start | bytes 393224 | tf_op jit(solution)/shard_map/ppermute | solution.py:775
  12.9 13.3 %collective-permute-start.4 = (bf16[128,512]{1,0:T(8,128)(2,1)S(1)}, bf16[128,512]{1,0:T(8,128)(2,1)S(1)}, u32[]{:S(2)}, u32[]{:S(2)}) collective-permute-start(bf16[128,512]{1,0:T(8,128)(2,1)S(1)} %add_convert_fusion.3), channel_id=1, source_target_pairs={{0,64},{8,72},{16,80},{24,88},{32,96},{40,104},{48,112},{56,120},{... | collective-permute-start | bytes 393224 | tf_op jit(solution)/shard_map/ppermute | solution.py:775
  16.2 10.0 %collective-permute-start.3 = (bf16[128,512]{1,0:T(8,128)(2,1)S(1)}, bf16[128,512]{1,0:T(8,128)(2,1)S(1)}, u32[]{:S(2)}, u32[]{:S(2)}) collective-permute-start(bf16[128,512]{1,0:T(8,128)(2,1)S(1)} %add_convert_fusion.3), channel_id=1, source_target_pairs={{0,32},{8,40},{16,48},{24,56},{32,64},{40,72},{48,80},{56,88},{64,... | collective-permute-start | bytes 393224 | tf_op jit(solution)/shard_map/ppermute | solution.py:775
  18.4 16.8 %all-to-all-start = ((s32[128,1,128]{2,1,0:T(1,128)}), s32[128,1,128]{2,1,0:T(1,128)S(1)}, u32[]{:S(2)}, u32[]{:S(2)}) async-start(s32[128,1,128]{2,1,0:T(1,128)} %bitcast.39), calls=%async_computation | async-start | bytes 131072 | tf_op jit(solution)/shard_map/all_to_all | solution.py:766
  26.3 16.0 %collective-permute-start.9 = (bf16[128,512]{1,0:T(8,128)(2,1)S(1)}, bf16[128,512]{1,0:T(8,128)(2,1)S(1)}, u32[]{:S(2)}, u32[]{:S(2)}) collective-permute-start(bf16[128,512]{1,0:T(8,128)(2,1)S(1)} %add_convert_fusion.2.glob0), channel_id=1, source_target_pairs={{0,24},{8,0},{16,8},{24,16},{32,56},{40,32},{48,40},{56,48},{64,88... | collective-permute-start | bytes 393224 | tf_op jit(solution)/shard_map/ppermute | solution.py:771
  29.1 13.2 %collective-permute-start.8 = (bf16[128,512]{1,0:T(8,128)(2,1)S(1)}, bf16[128,512]{1,0:T(8,128)(2,1)S(1)}, u32[]{:S(2)}, u32[]{:S(2)}) collective-permute-start(bf16[128,512]{1,0:T(8,128)(2,1)S(1)} %add_convert_fusion.2.glob0), channel_id=1, source_target_pairs={{0,16},{8,24},{16,0},{24,8},{32,48},{40,56},{48,32},{56,40},{64,80... | collective-permute-start | bytes 393224 | tf_op jit(solution)/shard_map/ppermute | solution.py:771
  29.9 12.4 %collective-permute-start.7 = (bf16[128,512]{1,0:T(8,128)(2,1)S(1)}, bf16[128,512]{1,0:T(8,128)(2,1)S(1)}, u32[]{:S(2)}, u32[]{:S(2)}) collective-permute-start(bf16[128,512]{1,0:T(8,128)(2,1)S(1)} %add_convert_fusion.2.glob0), channel_id=1, source_target_pairs={{0,8},{8,16},{16,24},{24,0},{32,40},{40,48},{48,56},{56,32},{64,72... | collective-permute-start | bytes 393224 | tf_op jit(solution)/shard_map/ppermute | solution.py:771
  35.2 9.7 %collective-permute-start.6 = (bf16[2,128,512]{2,1,0:T(8,128)(2,1)S(1)}, bf16[2,128,512]{2,1,0:T(8,128)(2,1)S(1)}, u32[]{:S(2)}, u32[]{:S(2)}) collective-permute-start(bf16[2,128,512]{2,1,0:T(8,128)(2,1)S(1)} %get-tuple-element.86), channel_id=1, source_target_pairs={{0,8},{8,16},{16,24},{24,32},{32,40},{40,48},{48,56},{56,64},{64,7... | collective-permute-start | bytes 786440 | tf_op jit(solution)/shard_map/ppermute | solution.py:762
  42.2 9.6 %copy-start = (bf16[1,512,512]{2,1,0:T(8,128)(2,1)S(1)}, bf16[1,512,512]{2,1,0:T(8,128)(2,1)}, u32[]{:S(2)}) copy-start(bf16[1,512,512]{2,1,0:T(8,128)(2,1)} %param.11) | copy-start | bytes 1572868
  42.3 9.6 %copy-start.4 = (bf16[1,512,512]{2,1,0:T(8,128)(2,1)S(1)}, bf16[1,512,512]{2,1,0:T(8,128)(2,1)}, u32[]{:S(2)}) copy-start(bf16[1,512,512]{2,1,0:T(8,128)(2,1)} %param.12) | copy-start | bytes 1572868
  42.3 9.6 %copy-start.5 = (bf16[1,512,512]{2,1,0:T(8,128)(2,1)S(1)}, bf16[1,512,512]{2,1,0:T(8,128)(2,1)}, u32[]{:S(2)}) copy-start(bf16[1,512,512]{2,1,0:T(8,128)(2,1)} %param.13) | copy-start | bytes 1572868
  44.9 25.8 %all-to-all-start.1 = ((bf16[128,32,128]{2,1,0:T(8,128)(2,1)}), bf16[128,32,128]{2,1,0:T(8,128)(2,1)S(1)}, u32[]{:S(2)}, u32[]{:S(2)}) async-start(bf16[128,32,128]{2,1,0:T(8,128)(2,1)} %bitcast.37), calls=%async_computation.1 | async-start | bytes 2097152 | tf_op jit(solution)/shard_map/all_to_all | solution.py:766
  76.2 25.2 %all-to-all-start.2 = ((bf16[128,32,128]{2,1,0:T(8,128)(2,1)}), bf16[128,32,128]{2,1,0:T(8,128)(2,1)S(1)}, u32[]{:S(2)}, u32[]{:S(2)}) async-start(bf16[128,32,128]{2,1,0:T(8,128)(2,1)} %bitcast.36), calls=%async_computation.2 | async-start | bytes 2097152 | tf_op jit(solution)/shard_map/all_to_all | solution.py:766
  81.1 12.4 %copy-start.1 = (bf16[1,512,512]{2,1,0:T(8,128)(2,1)S(1)}, bf16[1,512,512]{2,1,0:T(8,128)(2,1)}, u32[]{:S(2)}) copy-start(bf16[1,512,512]{2,1,0:T(8,128)(2,1)} %param.11) | copy-start | bytes 1572868
  81.1 12.4 %copy-start.2 = (bf16[8,512,256]{2,1,0:T(8,128)(2,1)S(1)}, bf16[8,512,256]{2,1,0:T(8,128)(2,1)}, u32[]{:S(2)}) copy-start(bf16[8,512,256]{2,1,0:T(8,128)(2,1)} %get-tuple-element.102.probs) | copy-start | bytes 6291460
  81.1 12.3 %copy-start.3 = (bf16[8,512,256]{2,1,0:T(8,128)(2,1)S(1)}, bf16[8,512,256]{2,1,0:T(8,128)(2,1)}, u32[]{:S(2)}) copy-start(bf16[8,512,256]{2,1,0:T(8,128)(2,1)} %get-tuple-element.103.slope) | copy-start | bytes 6291460
  87.8 10.7 %collective-permute-start.10 = (bf16[128,512]{1,0:T(8,128)(2,1)S(1)}, bf16[128,512]{1,0:T(8,128)(2,1)S(1)}, u32[]{:S(2)}, u32[]{:S(2)}) collective-permute-start(bf16[128,512]{1,0:T(8,128)(2,1)S(1)} %get-tuple-element.108), channel_id=1, source_target_pairs={{0,8},{8,16},{16,24},{24,0},{32,40},{40,48},{48,56},{56,32},{64,72... | collective-permute-start | bytes 393224 | tf_op jit(solution)/shard_map/ppermute | solution.py:771
  89.3 12.0 %collective-permute-start.11 = (bf16[128,512]{1,0:T(8,128)(2,1)S(1)}, bf16[128,512]{1,0:T(8,128)(2,1)S(1)}, u32[]{:S(2)}, u32[]{:S(2)}) collective-permute-start(bf16[128,512]{1,0:T(8,128)(2,1)S(1)} %get-tuple-element.109), channel_id=1, source_target_pairs={{0,16},{8,24},{16,0},{24,8},{32,48},{40,56},{48,32},{56,40},{64,80... | collective-permute-start | bytes 393224 | tf_op jit(solution)/shard_map/ppermute | solution.py:771
  92.0 9.3 %collective-permute-start.12 = (bf16[128,512]{1,0:T(8,128)(2,1)S(1)}, bf16[128,512]{1,0:T(8,128)(2,1)S(1)}, u32[]{:S(2)}, u32[]{:S(2)}) collective-permute-start(bf16[128,512]{1,0:T(8,128)(2,1)S(1)} %get-tuple-element.110), channel_id=1, source_target_pairs={{0,24},{8,0},{16,8},{24,16},{32,56},{40,32},{48,40},{56,48},{64,88... | collective-permute-start | bytes 393224 | tf_op jit(solution)/shard_map/ppermute | solution.py:771
  93.5 13.2 %copy-start.8 = (s32[128,128]{1,0:T(8,128)S(1)}, s32[128,128]{1,0:T(8,128)}, u32[]{:S(2)}) copy-start(s32[128,128]{1,0:T(8,128)} %get-tuple-element.114.asked) | copy-start | bytes 196612
  98.5 26.5 %collective-permute-start.13 = (bf16[2,128,512]{2,1,0:T(8,128)(2,1)S(1)}, bf16[2,128,512]{2,1,0:T(8,128)(2,1)S(1)}, u32[]{:S(2)}, u32[]{:S(2)}) collective-permute-start(bf16[2,128,512]{2,1,0:T(8,128)(2,1)S(1)} %get-tuple-element.113), channel_id=1, source_target_pairs={{0,120},{8,0},{16,8},{24,16},{32,24},{40,32},{48,40},{56,48},{64,5... | collective-permute-start | bytes 786440 | tf_op jit(solution)/shard_map/ppermute | solution.py:762
  101.4 9.3 %collective-permute-start.16 = (bf16[128,512]{1,0:T(8,128)(2,1)S(1)}, bf16[128,512]{1,0:T(8,128)(2,1)S(1)}, u32[]{:S(2)}, u32[]{:S(2)}) collective-permute-start(bf16[128,512]{1,0:T(8,128)(2,1)S(1)} %add_convert_fusion.1), channel_id=1, source_target_pairs={{0,96},{8,104},{16,112},{24,120},{32,0},{40,8},{48,16},{56,24},{64... | collective-permute-start | bytes 393224 | tf_op jit(solution)/shard_map/ppermute | solution.py:775
  101.9 8.8 %collective-permute-start.15 = (bf16[128,512]{1,0:T(8,128)(2,1)S(1)}, bf16[128,512]{1,0:T(8,128)(2,1)S(1)}, u32[]{:S(2)}, u32[]{:S(2)}) collective-permute-start(bf16[128,512]{1,0:T(8,128)(2,1)S(1)} %add_convert_fusion.1), channel_id=1, source_target_pairs={{0,64},{8,72},{16,80},{24,88},{32,96},{40,104},{48,112},{56,120},{... | collective-permute-start | bytes 393224 | tf_op jit(solution)/shard_map/ppermute | solution.py:775
  104.6 6.5 %collective-permute-start.14 = (bf16[128,512]{1,0:T(8,128)(2,1)S(1)}, bf16[128,512]{1,0:T(8,128)(2,1)S(1)}, u32[]{:S(2)}, u32[]{:S(2)}) collective-permute-start(bf16[128,512]{1,0:T(8,128)(2,1)S(1)} %add_convert_fusion.1), channel_id=1, source_target_pairs={{0,32},{8,40},{16,48},{24,56},{32,64},{40,72},{48,80},{56,88},{64,... | collective-permute-start | bytes 393224 | tf_op jit(solution)/shard_map/ppermute | solution.py:775
  111.2 13.8 %copy-start.6 = (bf16[512,512]{1,0:T(8,128)(2,1)S(1)}, bf16[512,512]{1,0:T(8,128)(2,1)}, u32[]{:S(2)}) copy-start(bf16[512,512]{1,0:T(8,128)(2,1)} %get-tuple-element.111.d_k) | copy-start | bytes 1572868
  111.3 13.8 %copy-start.7 = (bf16[512,512]{1,0:T(8,128)(2,1)S(1)}, bf16[512,512]{1,0:T(8,128)(2,1)}, u32[]{:S(2)}) copy-start(bf16[512,512]{1,0:T(8,128)(2,1)} %get-tuple-element.112.d_v) | copy-start | bytes 1572868
  111.3 10.3 %collective-permute-start.19 = (bf16[128,512]{1,0:T(8,128)(2,1)S(1)}, bf16[128,512]{1,0:T(8,128)(2,1)S(1)}, u32[]{:S(2)}, u32[]{:S(2)}) collective-permute-start(bf16[128,512]{1,0:T(8,128)(2,1)S(1)} %add_convert_fusion.glob0), channel_id=1, source_target_pairs={{0,24},{8,0},{16,8},{24,16},{32,56},{40,32},{48,40},{56,48},{64,88... | collective-permute-start | bytes 393224 | tf_op jit(solution)/shard_map/ppermute | solution.py:771
  115.9 7.9 %collective-permute-start.18 = (bf16[128,512]{1,0:T(8,128)(2,1)S(1)}, bf16[128,512]{1,0:T(8,128)(2,1)S(1)}, u32[]{:S(2)}, u32[]{:S(2)}) collective-permute-start(bf16[128,512]{1,0:T(8,128)(2,1)S(1)} %add_convert_fusion.glob0), channel_id=1, source_target_pairs={{0,16},{8,24},{16,0},{24,8},{32,48},{40,56},{48,32},{56,40},{64,80... | collective-permute-start | bytes 393224 | tf_op jit(solution)/shard_map/ppermute | solution.py:771
  115.9 9.2 %collective-permute-start.17 = (bf16[128,512]{1,0:T(8,128)(2,1)S(1)}, bf16[128,512]{1,0:T(8,128)(2,1)S(1)}, u32[]{:S(2)}, u32[]{:S(2)}) collective-permute-start(bf16[128,512]{1,0:T(8,128)(2,1)S(1)} %add_convert_fusion.glob0), channel_id=1, source_target_pairs={{0,8},{8,16},{16,24},{24,0},{32,40},{40,48},{48,56},{56,32},{64,72... | collective-permute-start | bytes 393224 | tf_op jit(solution)/shard_map/ppermute | solution.py:771
